TPU v7x, 128 devices: a whole 4x4x4 slice. The times are simulated.
128 devices in a mesh: context: 32 (over x_lo, y, z), tensor: 4 (over x_hi, core).
Axes of the slice: x: 4 (x_hi: 2, x_lo: 2; x = x_hi * 2 + x_lo), y: 4, z: 4, core: 2. Of those that a mesh axis runs over, the one named last changes fastest.
Arguments:
- query: bfloat16 [4096, 4096], P('context', 'tensor'), may hold values from -6 to 6
- key_feat: bfloat16 [4096, 4096], P('context', 'tensor'), may hold values from -6 to 6
- value_feat: bfloat16 [4096, 4096], P('context', 'tensor'), may hold values from -6 to 6
- filt: bfloat16 [4096, 4096], P('context', 'tensor'), may hold values from -1 to 1
- skip: float32 [4096], P('tensor'), may hold values from 0.5 to 1.5
- dout: bfloat16 [4096, 4096], P('context', 'tensor'), may hold values from -6 to 6
- w_out: bfloat16 [4096, 4096], P('tensor', 'context'), may hold values from -0.09375 to 0.09375
Outputs:
- grad_query: bfloat16 [4096, 4096], P('context', 'tensor')
- grad_key: bfloat16 [4096, 4096], P('context', 'tensor')
- grad_value: bfloat16 [4096, 4096], P('context', 'tensor')
- grad_filt: bfloat16 [4096, 4096], P('context', 'tensor')
- wo_grad: float32 [4096, 4096], P('tensor', 'context')
All inputs are finite; a program needn't handle non-finite values.
Results may differ from a plain program's by a relative error of at most 0.0058.
Values may be sent and summed in bfloat16 or wider, within the bound.
No kernel may reach another device: no remote copies, remote signals or barrier semaphores. Data moves between devices by JAX's collectives and lax.ppermute only.
A program may use at most 128 MiB of HBM per device.

v0:
```python
import functools

import jax
import jax.numpy as jnp
import numpy as np
from jax import lax
from jax.experimental import pallas as pl
from jax.experimental.pallas import tpu as pltpu
from jax.sharding import Mesh
from jax.sharding import PartitionSpec as P

BF16 = jnp.bfloat16
F32 = jnp.float32
VMEM = pl.BlockSpec(memory_space=pltpu.VMEM)
SMEM = pl.BlockSpec(memory_space=pltpu.SMEM)
PARAMS = pltpu.CompilerParams(vmem_limit_bytes=48 * 1024 * 1024)

M, N = 32, 128
GROUP = 8


def split(values):
    high = values.astype(jnp.bfloat16)
    return high, (values - high.astype(values.dtype)).astype(jnp.bfloat16)


@functools.cache
def tables():
    k1, m, n = np.arange(M) + 0.25, np.arange(M), np.arange(N)
    first = 2 * np.pi * np.outer(k1, m) / M
    second = 2 * np.pi * np.outer(n, n) / N
    turn = 2 * np.pi * np.outer(k1, n) / (M * N)
    eye = np.eye(GROUP)
    one = np.kron(np.concatenate([np.cos(first), -np.sin(first)]), eye)
    cos, sin = np.cos(second), np.sin(second)
    two = np.block([[cos, -sin], [sin, cos]])
    back_two = np.block([[cos, sin], [-sin, cos]])
    back_one = one.T / (M * N)

    def pair(table):
        high = table.astype(jnp.bfloat16)
        low = (table - high.astype(np.float64)).astype(jnp.bfloat16)
        return high, low

    spread = [np.repeat(f(turn), GROUP, axis=0).astype(np.float32) for f in (np.cos, np.sin)]
    return (*pair(one), *pair(two), *pair(back_two), *pair(back_one), *spread)


def dot(lhs, rhs):
    return jnp.dot(lhs, rhs, preferred_element_type=F32)


def rows_of(block, group):
    part = block[:, group * GROUP : (group + 1) * GROUP, :]
    return part.reshape(M * GROUP, N).astype(BF16)


def forward(sides, tabs):
    one_h, one_l, two_h, two_l = (t[...] for t in tabs[:4])
    cos, sin = tabs[8][...], tabs[9][...]
    cat = jnp.concatenate(sides, axis=1)
    part = dot(one_h, cat) + dot(one_l, cat)
    half = part.shape[0] // 2
    out = []
    for index in range(len(sides)):
        lanes = slice(index * N, (index + 1) * N)
        re, im = part[:half, lanes], part[half:, lanes]
        turned = jnp.concatenate([re * cos + im * sin, im * cos - re * sin], axis=1)
        high, low = split(turned)
        out.append(dot(high, two_h) + dot(low, two_h) + dot(high, two_l))
    return out


def inverse(specs, tabs):
    two_h, two_l, one_h, one_l = (t[...] for t in tabs[4:8])
    cos, sin = tabs[8][...], tabs[9][...]
    cols = []
    for spec in specs:
        high, low = split(spec)
        part = dot(high, two_h) + dot(low, two_h) + dot(high, two_l)
        re, im = part[:, :N], part[:, N:]
        cols.append(jnp.concatenate([re * cos - im * sin, im * cos + re * sin], axis=0))
    high, low = split(jnp.concatenate(cols, axis=1))
    full = dot(one_h, high) + dot(one_h, low) + dot(one_l, high)
    return [full[:, i * N : (i + 1) * N] for i in range(len(specs))]


def times(a, b, conj_a):
    are, aim, bre, bim = a[:, :N], a[:, N:], b[:, :N], b[:, N:]
    if conj_a:
        return jnp.concatenate([are * bre + aim * bim, are * bim - aim * bre], axis=1)
    return jnp.concatenate([are * bre - aim * bim, are * bim + aim * bre], axis=1)


def pair_of(first, second):
    shape = (M, GROUP, N)
    return jnp.concatenate([first.reshape(shape), second.reshape(shape)], axis=1)


def prep_kernel(key_ref, value_ref, filt_ref, query_ref, out_ref):
    def put(which, block):
        out_ref[:, which] = block.T.reshape(M, 32, N).astype(BF16)

    signal = key_ref[...].astype(F32) * value_ref[...].astype(F32)
    put(0, signal.astype(BF16).astype(F32))
    put(1, filt_ref[...].astype(F32))
    put(2, query_ref[...].astype(F32))


def conv_kernel(in_ref, skip_ref, *refs):
    tabs, (conv_ref, gated_ref, sig_ref, fil_ref) = refs[:10], refs[10:]
    signal, filt, query = (in_ref[:, i].astype(F32) for i in range(3))
    for pair in range(2):
        groups = (2 * pair, 2 * pair + 1)
        chans = slice(16 * pair, 16 * pair + 16)
        spectra = forward([rows_of(a, g) for a in (signal, filt) for g in groups], tabs)
        for i, g in enumerate(groups):
            sig_ref[g], fil_ref[g] = spectra[i], spectra[2 + i]
        conv = pair_of(*inverse([times(spectra[i], spectra[2 + i], False) for i in range(2)], tabs))
        conv = conv + skip_ref[chans, :][None] * signal[:, chans, :]
        conv = conv.astype(BF16)
        conv_ref[:, chans, :] = conv
        gated = (query[:, chans, :] * conv.astype(F32)).astype(BF16)
        for xl in range(2):
            for y in range(4):
                block = gated[xl * 16 + y * 4 : xl * 16 + y * 4 + 4]
                for copy in range(4):
                    gated_ref[y, copy, xl * 4 : xl * 4 + 4, chans, :] = block


def back_kernel(part_ref, in_ref, conv_ref, skip_ref, sig_ref, fil_ref, *refs):
    tabs, out_ref, gate_s = refs[:10], refs[10], refs[11]
    for y in range(4):
        for b in range(8):
            total = part_ref[4 * y, b].astype(F32)
            for z in range(1, 4):
                total = total + part_ref[4 * y + z, b].astype(F32)
            m = (b // 4) * 16 + y * 4 + b % 4
            out_ref[m, 0] = (total * conv_ref[m].astype(F32)).astype(BF16)
            gate_s[m] = (total * in_ref[m, 2].astype(F32)).astype(BF16).astype(F32)
    gate = gate_s[...]
    for pair in range(2):
        groups = (2 * pair, 2 * pair + 1)
        chans = slice(16 * pair, 16 * pair + 16)
        spectra = forward([rows_of(gate, g) for g in groups], tabs)
        specs = [times(fil_ref[g], s, True) for g, s in zip(groups, spectra)]
        specs += [times(sig_ref[g], s, True) for g, s in zip(groups, spectra)]
        result = inverse(specs, tabs)
        back = pair_of(*result[:2]) + skip_ref[chans, :][None] * gate[:, chans, :]
        out_ref[:, 1, chans, :] = back.astype(BF16)
        out_ref[:, 2, chans, :] = pair_of(*result[2:]).astype(BF16)


def final_kernel(in_ref, key_ref, value_ref, gq_ref, gk_ref, gv_ref, gf_ref):
    def get(which):
        return in_ref[:, which].astype(F32).reshape(M * 32, N).T

    gq_ref[...] = get(0).astype(BF16)
    gf_ref[...] = get(2).astype(BF16)
    back = get(1)
    gk_ref[...] = (back * value_ref[...].astype(F32)).astype(BF16)
    gv_ref[...] = (back * key_ref[...].astype(F32)).astype(BF16)


def grady_kernel(where_ref, *refs):
    d_refs, w_refs, (out_ref, d_ref), w_s = refs[:8], refs[8:12], refs[12:14], refs[14]
    xl, y, q = where_ref[0], where_ref[1], where_ref[2]
    for p in range(8):
        for lo in range(2):
            d_ref[xl ^ (p & 1), 2 * (q ^ (p >> 1)) + lo] = d_refs[p][:, lo]
    for s in range(4):
        for i in range(2):
            w_s[(xl ^ i) * 4 + (y ^ s)] = w_refs[s][i]
    lhs = jnp.concatenate([w_s[j] for j in range(8)], axis=1)
    for side in range(2):
        for z in range(0, 4, 2):
            rhs = jnp.concatenate(
                [d_ref[side, j, z : z + 2].reshape(2 * N, 128) for j in range(8)], axis=1
            )
            part = lax.dot_general(lhs, rhs, (((1,), (1,)), ((), ())), preferred_element_type=F32)
            part = part.astype(BF16)
            for k in range(2):
                out_ref[:, side * 4 + z + k] = part[:, k * N : (k + 1) * N].reshape(16, 32, N)


def wo_kernel(gated_ref, d_ref, out_ref):
    lhs = jnp.concatenate([gated_ref[:, b].reshape(512, N) for b in range(8)], axis=1)
    for j in range(0, 8, 2):
        rhs = jnp.concatenate(
            [
                jnp.concatenate([d_ref[xl, j + k].reshape(512, 128) for xl in range(2)], axis=0)
                for k in range(2)
            ],
            axis=1,
        )
        part = dot(lhs, rhs).astype(BF16)
        for k in range(2):
            out_ref[j + k] = part[:, k * 128 : (k + 1) * 128]


def sum_kernel(in_ref, out_ref):
    for xl in range(2):
        total = in_ref[4 * xl].astype(F32)
        for y in range(1, 4):
            total = total + in_ref[4 * xl + y].astype(F32)
        out_ref[xl * 512 : xl * 512 + 512, :] = total


def call(kernel, ins, outs, scratch=(), first=VMEM):
    return pl.pallas_call(
        kernel,
        out_shape=outs,
        in_specs=[first] + [VMEM] * (len(ins) - 1),
        out_specs=jax.tree.map(lambda _: VMEM, outs),
        scratch_shapes=list(scratch),
        compiler_params=PARAMS,
    )(*ins)


def shape(*dims, dtype=BF16):
    return jax.ShapeDtypeStruct(dims, dtype)


CONTEXT = ("xl", "y", "z")


def flip(value, axes, sizes, by):
    total = int(np.prod(sizes))
    return lax.ppermute(value, axes, [(i, i ^ by) for i in range(total)])


def exchange(value, axes):
    return lax.all_to_all(value, axes, 0, 0)


def body(query, key_feat, value_feat, filt, skip, dout, w_out):
    xl, y, z = (lax.axis_index(a) for a in CONTEXT)
    q = lax.axis_index("xh") * 2 + lax.axis_index("co")
    tabs = tables()
    skip_c = lax.dynamic_slice_in_dim(skip, (xl * 16 + y * 4 + z) * 32, 32, 0)
    skip_c = jnp.broadcast_to(skip_c[:, None], (32, N))

    with jax.named_scope("gather_d"):
        d = dout.reshape(128, 2, 4, 128).transpose(2, 1, 0, 3)
        d = exchange(d, "z")
        d = [d] + [flip(d, ("xl", "xh"), (2, 2), (p & 1) * 2 + (p >> 1)) for p in (1, 2, 3)]
        d_pieces = {}
        for p in range(4):
            a, b = p & 1, p >> 1
            d_pieces[a + 2 * (2 * b)] = d[p]
            d_pieces[a + 2 * (2 * b + 1)] = flip(d[p], "co", (2,), 1)
        d_pieces = [d_pieces[p] for p in range(8)]
    with jax.named_scope("gather_w"):
        halves = w_out.reshape(2, 512, 128)
        keep = lax.dynamic_index_in_dim(halves, xl, 0, keepdims=False)
        give = lax.dynamic_index_in_dim(halves, 1 - xl, 0, keepdims=False)
        w = jnp.stack([keep, flip(give, "xl", (2,), 1)])
        w_pieces = [w] + [flip(w, "y", (4,), s) for s in (1, 2, 3)]

    with jax.named_scope("to_channels"):
        sent = call(prep_kernel, (key_feat, value_feat, filt, query), shape(M, 3, 32, N))
        held = exchange(sent, CONTEXT)
    with jax.named_scope("conv"):
        conv, gated, sig, fil = call(
            conv_kernel,
            (held, skip_c, *tabs),
            (
                shape(M, 32, N),
                shape(4, 4, 8, 32, N),
                shape(4, 256, 256, dtype=F32),
                shape(4, 256, 256, dtype=F32),
            ),
        )
    with jax.named_scope("grady"):
        part, d_all = call(
            grady_kernel,
            (jnp.stack([xl, y, q]).astype(jnp.int32), *d_pieces, *w_pieces),
            (shape(16, 8, 32, N), shape(2, 8, 4, 128, 128)),
            [pltpu.VMEM((8, 512, 128), BF16)],
            SMEM,
        )
        part = exchange(part, ("y", "z"))
    with jax.named_scope("gated"):
        gated = exchange(gated.reshape(16, 8, 32, N), ("y", "z"))
    with jax.named_scope("back"):
        sent = call(
            back_kernel,
            (part, held, conv, skip_c, sig, fil, *tabs),
            shape(M, 3, 32, N),
            [pltpu.VMEM((M, 32, N), F32)],
        )
        got = exchange(sent, CONTEXT)
    with jax.named_scope("wo"):
        wo = call(wo_kernel, (gated, d_all), shape(8, 512, 128))
        wo = exchange(wo, ("xl", "y"))
        wo_grad = call(sum_kernel, (wo,), shape(1024, 128, dtype=F32))
    with jax.named_scope("final"):
        grads = call(final_kernel, (got, key_feat, value_feat), [shape(128, 1024)] * 4)
    return (*grads, wo_grad)


def solution(mesh):
    fine = Mesh(mesh.devices.reshape(2, 4, 4, 2, 2), ("xl", "y", "z", "xh", "co"))
    tokens, channels = P(CONTEXT, ("xh", "co")), P(("xh", "co"))
    rows = P(("xh", "co"), CONTEXT)
    return jax.shard_map(
        body,
        mesh=fine,
        in_specs=(tokens, tokens, tokens, tokens, channels, tokens, rows),
        out_specs=(tokens, tokens, tokens, tokens, rows),
        check_vma=False,
    )
```

profile of v0, /device:TPU:0, one launch (start us, length us, event | category | flops | bytes accessed | tf_op | source)
XLA Modules:
  0.0 131.8 jit_solution(11816949694804286263)
XLA Ops:
  0.7 1.2 copy.22
  1.9 0.9 copy.23
  2.7 5.4 %all-to-all-start = ((bf16[4,2,128,128]{3,2,1,0:T(8,128)(2,1)}), bf16[4,2,128,128]{3,2,1,0:T(8,128)(2,1)S(1)}, u32[]{:S(2)}, u32[]{:S(2)}) async-start(bf16[4,2,128,128]{3,2,1,0:T(8,128)(2,1)} %bitcast.4), calls=%async_computation | async-start | bytes 524288 | tf_op jit(solution)/shard_map/gather_d/all_to_all | solution.py:233
  8.1 1.0 constant_dynamic-slice_fusion
  9.1 1.6 %collective-permute-start.7 = (bf16[512,128]{1,0:T(8,128)(2,1)S(1)}, bf16[512,128]{1,0:T(8,128)(2,1)S(1)}, u32[]{:S(2)}, u32[]{:S(2)}) collective-permute-start(bf16[512,128]{1,0:T(8,128)(2,1)S(1)} %get-tuple-element.26), channel_id=1, source_target_pairs={{0,64},{64,0},{1,65},{65,1},{2,66},{66,2},{3,67},{67,3},{4,68},{68... | collective-permute-start | bytes 393224 | tf_op jit(solution)/shard_map/gather_w/ppermute | solution.py:229
  10.7 1.2 to_channels.1
  11.9 2.9 %all-to-all-done.refs_0_ = bf16[4,2,128,128]{3,2,1,0:T(8,128)(2,1)S(1)} async-done(((bf16[4,2,128,128]{3,2,1,0:T(8,128)(2,1)}), bf16[4,2,128,128]{3,2,1,0:T(8,128)(2,1)S(1)}, u32[]{:S(2)}, u32[]{:S(2)}) %all-to-all-start) | async-done | bytes 262176 | tf_op jit(solution)/shard_map/gather_d/all_to_all | solution.py:233
  14.8 6.4 %all-to-all-start.2 = ((bf16[32,3,32,128]{3,2,1,0:T(8,128)(2,1)}), bf16[32,3,32,128]{3,2,1,0:T(8,128)(2,1)S(1)}, u32[]{:S(2)}, u32[]{:S(2)}) async-start(bf16[32,3,32,128]{3,2,1,0:T(8,128)(2,1)} %to_channels.1), calls=%async_computation.2 | async-start | bytes 1572864 | tf_op jit(solution)/shard_map/to_channels/all_to_all | solution.py:233
  21.2 3.1 %collective-permute-start.10 = (bf16[2,512,128]{2,1,0:T(8,128)(2,1)S(1)}, bf16[2,512,128]{2,1,0:T(8,128)(2,1)S(1)}, u32[]{:S(2)}, u32[]{:S(2)}) collective-permute-start(bf16[2,512,128]{2,1,0:T(8,128)(2,1)S(1)} %pad_maximum_fusion.refs_8_), channel_id=1, source_target_pairs={{0,48},{16,32},{32,16},{48,0},{1,49},{17,33},{33,17},{49,1},{2,50}... | collective-permute-start | bytes 786440 | tf_op jit(solution)/shard_map/gather_w/ppermute | solution.py:229
  24.3 0.9 collective-permute-start.9
  25.2 2.7 %collective-permute-start.4 = (bf16[4,2,128,128]{3,2,1,0:T(8,128)(2,1)S(1)}, bf16[4,2,128,128]{3,2,1,0:T(8,128)(2,1)}, u32[]{:S(2)}, u32[]{:S(2)}) collective-permute-start(bf16[4,2,128,128]{3,2,1,0:T(8,128)(2,1)S(1)} %all-to-all-done.refs_0_), channel_id=1, source_target_pairs={{0,66},{2,64},{64,2},{66,0},{1,67},{3,65},{65,3},{67,1},{4,70},{6,... | collective-permute-start | bytes 786440 | tf_op jit(solution)/shard_map/gather_d/ppermute | solution.py:229
  27.9 0.8 collective-permute-start.3
  28.7 0.5 collective-permute-start
  29.3 13.4 %collective-permute-done.10.refs_11_ = bf16[2,512,128]{2,1,0:T(8,128)(2,1)S(1)} collective-permute-done((bf16[2,512,128]{2,1,0:T(8,128)(2,1)S(1)}, bf16[2,512,128]{2,1,0:T(8,128)(2,1)S(1)}, u32[]{:S(2)}, u32[]{:S(2)}) %collective-permute-start.10) | collective-permute-done | bytes 262176 | tf_op jit(solution)/shard_map/gather_w/ppermute | solution.py:229
  42.7 0.2 collective-permute-start.8
  42.9 0.0 collective-permute-done.9.refs_10_
  42.9 0.5 collective-permute-start.6
  43.4 0.0 collective-permute-done.3.refs_4_
  43.4 0.1 collective-permute-start.5
  43.5 0.4 collective-permute-start.2
  43.9 0.1 pad_add_fusion.where_ref
  44.0 0.0 copy-start.17
  44.1 6.0 %collective-permute-done.8.refs_9_ = bf16[2,512,128]{2,1,0:T(8,128)(2,1)} collective-permute-done((bf16[2,512,128]{2,1,0:T(8,128)(2,1)S(1)}, bf16[2,512,128]{2,1,0:T(8,128)(2,1)}, u32[]{:S(2)}, u32[]{:S(2)}) %collective-permute-start.8) | collective-permute-done | bytes 262176 | tf_op jit(solution)/shard_map/gather_w/ppermute | solution.py:229
  50.0 0.0 collective-permute-done.1.refs_2_
  50.0 0.0 collective-permute-done.6.refs_7_
  50.1 3.9 %grady.1 = (bf16[16,8,32,128]{3,2,1,0:T(8,128)(2,1)}, bf16[2,8,4,128,128]{4,3,2,1,0:T(8,128)(2,1)}) custom-call(s32[3]{0:T(128)S(1)} %pad_add_fusion.where_ref, bf16[4,2,128,128]{3,2,1,0:T(8,128)(2,1)S(1)} %all-to-all-done.refs_0_, bf16[4,2,128,128]{3,2,1,0:T(8,128)(2,1)} %collective-permute-done.refs_1_, ...), custom_call_target="tpu_custom_call" | custom-call | tf_op jit(solution)/shard_map/grady/pallas_call | solution.py:210
  54.0 4.8 %all-to-all-start.1 = ((bf16[16,8,32,128]{3,2,1,0:T(8,128)(2,1)}), bf16[16,8,32,128]{3,2,1,0:T(8,128)(2,1)S(1)}, u32[]{:S(2)}, u32[]{:S(2)}) async-start(bf16[16,8,32,128]{3,2,1,0:T(8,128)(2,1)} %get-tuple-element.15), calls=%async_computation.1 | async-start | bytes 2097152 | tf_op jit(solution)/shard_map/grady/all_to_all | solution.py:233
  58.9 0.8 dynamic_slice.12
  59.6 0.1 broadcast_in_dim.2.skip_ref
  59.7 0.0 copy-start.18
  59.7 0.9 copy-done.18
  60.6 0.9 copy-done.20
  61.5 0.9 copy-done.22
  62.4 0.9 copy-done.24
  63.3 0.9 copy-done.26
  64.2 3.2 %conv.1 = (bf16[32,32,128]{2,1,0:T(8,128)(2,1)S(1)}, bf16[4,4,8,32,128]{4,3,2,1,0:T(8,128)(2,1)S(1)}, f32[4,256,256]{2,1,0:T(8,128)S(1)}, f32[4,256,256]{2,1,0:T(8,128)S(1)}) custom-call(bf16[32,3,32,128]{3,2,1,0:T(8,128)(2,1)S(1)} %all-to-all-done.2.in_ref, f32[32,128]{1,0:T(8,128)S(1)} %broadcast_in_dim.2.skip_ref, bf16[512,256]{1,0:T(8,128)(2,1)S(1)} %copy-done.15, ...), custom_call_target="tpu_custom_call" | custom-call | tf_op jit(solution)/shard_map/conv/pallas_call | solution.py:210
  67.4 1.0 copy-done.5
  68.4 1.0 copy-done.6
  69.4 1.0 copy-done.8
  70.4 0.7 copy-done.30
  71.1 3.4 %all-to-all-done.1.part_ref = bf16[16,8,32,128]{3,2,1,0:T(8,128)(2,1)S(1)} async-done(((bf16[16,8,32,128]{3,2,1,0:T(8,128)(2,1)}), bf16[16,8,32,128]{3,2,1,0:T(8,128)(2,1)S(1)}, u32[]{:S(2)}, u32[]{:S(2)}) %all-to-all-start.1) | async-done | bytes 1048608 | tf_op jit(solution)/shard_map/grady/all_to_all | solution.py:233
  74.4 3.8 %all-to-all-start.4 = ((bf16[16,8,32,128]{3,2,1,0:T(8,128)(2,1)}), bf16[16,8,32,128]{3,2,1,0:T(8,128)(2,1)S(1)}, u32[]{:S(2)}, u32[]{:S(2)}) async-start(bf16[16,8,32,128]{3,2,1,0:T(8,128)(2,1)} %bitcast.10), calls=%async_computation.4 | async-start | bytes 2097152 | tf_op jit(solution)/shard_map/gated/all_to_all | solution.py:233
  78.3 1.2 copy-done.7
  79.5 0.9 copy-done.10
  80.5 0.9 copy-done.12
  81.4 0.9 copy-done.14
  82.4 0.9 copy-done.16
  83.3 0.9 copy-done.19
  84.2 0.9 copy-done.21
  85.1 0.9 copy-done.23
  86.0 0.9 copy-done.25
  86.9 0.9 copy-done.27
  87.8 0.9 copy-done.31
  88.8 4.5 %back.1 = bf16[32,3,32,128]{3,2,1,0:T(8,128)(2,1)S(1)} custom-call(bf16[16,8,32,128]{3,2,1,0:T(8,128)(2,1)S(1)} %all-to-all-done.1.part_ref, bf16[32,3,32,128]{3,2,1,0:T(8,128)(2,1)S(1)} %all-to-all-done.2.in_ref, bf16[32,32,128]{2,1,0:T(8,128)(2,1)S(1)} %copy-done.31, f32[32,128]{1,0:T(8,128)S(1)} %broadcast_in_dim.2.skip_ref, ...), custom_call_target="tpu_custom_call" | custom-call | tf_op jit(solution)/shard_map/back/pallas_call | solution.py:210
  93.3 0.9 copy-done.1
  94.2 8.5 %all-to-all-start.3 = ((bf16[32,3,32,128]{3,2,1,0:T(8,128)(2,1)}), bf16[32,3,32,128]{3,2,1,0:T(8,128)(2,1)S(1)}, u32[]{:S(2)}, u32[]{:S(2)}) async-start(bf16[32,3,32,128]{3,2,1,0:T(8,128)(2,1)} %copy-done.1), calls=%async_computation.3 | async-start | bytes 1572864 | tf_op jit(solution)/shard_map/back/all_to_all | solution.py:233
  102.8 1.6 %copy-done.2 = bf16[2,8,4,128,128]{4,3,2,1,0:T(8,128)(2,1)S(1)} copy-done((bf16[2,8,4,128,128]{4,3,2,1,0:T(8,128)(2,1)S(1)}, bf16[2,8,4,128,128]{4,3,2,1,0:T(8,128)(2,1)}, u32[]{:S(2)}) %copy-start.2) | copy-done | bytes 2097176
  104.4 1.2 wo.2
  105.6 1.0 copy-done
  106.6 8.2 %all-to-all-done.3.in_ref = bf16[32,3,32,128]{3,2,1,0:T(8,128)(2,1)S(1)} async-done(((bf16[32,3,32,128]{3,2,1,0:T(8,128)(2,1)}), bf16[32,3,32,128]{3,2,1,0:T(8,128)(2,1)S(1)}, u32[]{:S(2)}, u32[]{:S(2)}) %all-to-all-start.3) | async-done | bytes 786464 | tf_op jit(solution)/shard_map/back/all_to_all | solution.py:233
  114.8 3.7 %all-to-all-start.5 = ((bf16[8,512,128]{2,1,0:T(8,128)(2,1)}), bf16[8,512,128]{2,1,0:T(8,128)(2,1)S(1)}, u32[]{:S(2)}, u32[]{:S(2)}) async-start(bf16[8,512,128]{2,1,0:T(8,128)(2,1)} %copy-done), calls=%async_computation.5 | async-start | bytes 2097152 | tf_op jit(solution)/shard_map/wo/all_to_all | solution.py:233
  118.5 1.1 final.1
  119.6 11.2 %all-to-all-done.5.in_ref = bf16[8,512,128]{2,1,0:T(8,128)(2,1)S(1)} async-done(((bf16[8,512,128]{2,1,0:T(8,128)(2,1)}), bf16[8,512,128]{2,1,0:T(8,128)(2,1)S(1)}, u32[]{:S(2)}, u32[]{:S(2)}) %all-to-all-start.5) | async-done | bytes 1048608 | tf_op jit(solution)/shard_map/wo/all_to_all | solution.py:233
  130.9 0.9 wo.3
  (48 shorter events, 0.1 us)
Async XLA Ops:
  0.6 10.1 %copy-start.4 = (bf16[128,1024]{1,0:T(8,128)(2,1)S(1)}, bf16[128,1024]{1,0:T(8,128)(2,1)}, u32[]{:S(2)}) copy-start(bf16[128,1024]{1,0:T(8,128)(2,1)} %value_ref.3) | copy-start | bytes 786436
  0.6 10.0 %copy-start.3 = (bf16[128,1024]{1,0:T(8,128)(2,1)S(1)}, bf16[128,1024]{1,0:T(8,128)(2,1)}, u32[]{:S(2)}) copy-start(bf16[128,1024]{1,0:T(8,128)(2,1)} %key_ref.3) | copy-start | bytes 786436
  0.7 10.0 %copy-start.28 = (bf16[128,1024]{1,0:T(8,128)(2,1)S(1)}, bf16[128,1024]{1,0:T(8,128)(2,1)}, u32[]{:S(2)}) copy-start(bf16[128,1024]{1,0:T(8,128)(2,1)} %filt_ref.1) | copy-start | bytes 786436
  0.7 10.0 %copy-start.29 = (bf16[128,1024]{1,0:T(8,128)(2,1)S(1)}, bf16[128,1024]{1,0:T(8,128)(2,1)}, u32[]{:S(2)}) copy-start(bf16[128,1024]{1,0:T(8,128)(2,1)} %query_ref.1) | copy-start | bytes 786436
  2.7 12.1 %all-to-all-start = ((bf16[4,2,128,128]{3,2,1,0:T(8,128)(2,1)}), bf16[4,2,128,128]{3,2,1,0:T(8,128)(2,1)S(1)}, u32[]{:S(2)}, u32[]{:S(2)}) async-start(bf16[4,2,128,128]{3,2,1,0:T(8,128)(2,1)} %bitcast.4), calls=%async_computation | async-start | bytes 524288 | tf_op jit(solution)/shard_map/gather_d/all_to_all | solution.py:233
  9.1 12.1 %collective-permute-start.7 = (bf16[512,128]{1,0:T(8,128)(2,1)S(1)}, bf16[512,128]{1,0:T(8,128)(2,1)S(1)}, u32[]{:S(2)}, u32[]{:S(2)}) collective-permute-start(bf16[512,128]{1,0:T(8,128)(2,1)S(1)} %get-tuple-element.26), channel_id=1, source_target_pairs={{0,64},{64,0},{1,65},{65,1},{2,66},{66,2},{3,67},{67,3},{4,68},{68... | collective-permute-start | bytes 393224 | tf_op jit(solution)/shard_map/gather_w/ppermute | solution.py:229
  14.8 39.2 %all-to-all-start.2 = ((bf16[32,3,32,128]{3,2,1,0:T(8,128)(2,1)}), bf16[32,3,32,128]{3,2,1,0:T(8,128)(2,1)S(1)}, u32[]{:S(2)}, u32[]{:S(2)}) async-start(bf16[32,3,32,128]{3,2,1,0:T(8,128)(2,1)} %to_channels.1), calls=%async_computation.2 | async-start | bytes 1572864 | tf_op jit(solution)/shard_map/to_channels/all_to_all | solution.py:233
  21.2 21.4 %collective-permute-start.10 = (bf16[2,512,128]{2,1,0:T(8,128)(2,1)S(1)}, bf16[2,512,128]{2,1,0:T(8,128)(2,1)S(1)}, u32[]{:S(2)}, u32[]{:S(2)}) collective-permute-start(bf16[2,512,128]{2,1,0:T(8,128)(2,1)S(1)} %pad_maximum_fusion.refs_8_), channel_id=1, source_target_pairs={{0,48},{16,32},{32,16},{48,0},{1,49},{17,33},{33,17},{49,1},{2,50}... | collective-permute-start | bytes 786440 | tf_op jit(solution)/shard_map/gather_w/ppermute | solution.py:229
  24.3 18.6 %collective-permute-start.9 = (bf16[2,512,128]{2,1,0:T(8,128)(2,1)S(1)}, bf16[2,512,128]{2,1,0:T(8,128)(2,1)S(1)}, u32[]{:S(2)}, u32[]{:S(2)}) collective-permute-start(bf16[2,512,128]{2,1,0:T(8,128)(2,1)S(1)} %pad_maximum_fusion.refs_8_), channel_id=1, source_target_pairs={{0,32},{16,48},{32,0},{48,16},{1,33},{17,49},{33,1},{49,17},{2,34}... | collective-permute-start | bytes 786440 | tf_op jit(solution)/shard_map/gather_w/ppermute | solution.py:229
  25.2 17.7 %collective-permute-start.4 = (bf16[4,2,128,128]{3,2,1,0:T(8,128)(2,1)S(1)}, bf16[4,2,128,128]{3,2,1,0:T(8,128)(2,1)}, u32[]{:S(2)}, u32[]{:S(2)}) collective-permute-start(bf16[4,2,128,128]{3,2,1,0:T(8,128)(2,1)S(1)} %all-to-all-done.refs_0_), channel_id=1, source_target_pairs={{0,66},{2,64},{64,2},{66,0},{1,67},{3,65},{65,3},{67,1},{4,70},{6,... | collective-permute-start | bytes 786440 | tf_op jit(solution)/shard_map/gather_d/ppermute | solution.py:229
  27.9 15.5 %collective-permute-start.3 = (bf16[4,2,128,128]{3,2,1,0:T(8,128)(2,1)S(1)}, bf16[4,2,128,128]{3,2,1,0:T(8,128)(2,1)}, u32[]{:S(2)}, u32[]{:S(2)}) collective-permute-start(bf16[4,2,128,128]{3,2,1,0:T(8,128)(2,1)S(1)} %all-to-all-done.refs_0_), channel_id=1, source_target_pairs={{0,2},{2,0},{64,66},{66,64},{1,3},{3,1},{65,67},{67,65},{4,6},{6,4... | collective-permute-start | bytes 786440 | tf_op jit(solution)/shard_map/gather_d/ppermute | solution.py:229
  28.7 14.8 %collective-permute-start = (bf16[4,2,128,128]{3,2,1,0:T(8,128)(2,1)S(1)}, bf16[4,2,128,128]{3,2,1,0:T(8,128)(2,1)}, u32[]{:S(2)}, u32[]{:S(2)}) collective-permute-start(bf16[4,2,128,128]{3,2,1,0:T(8,128)(2,1)S(1)} %all-to-all-done.refs_0_), channel_id=1, source_target_pairs={{0,64},{2,66},{64,0},{66,2},{1,65},{3,67},{65,1},{67,3},{4,68},{6,... | collective-permute-start | bytes 786440 | tf_op jit(solution)/shard_map/gather_d/ppermute | solution.py:229
  42.7 7.4 %collective-permute-start.8 = (bf16[2,512,128]{2,1,0:T(8,128)(2,1)S(1)}, bf16[2,512,128]{2,1,0:T(8,128)(2,1)}, u32[]{:S(2)}, u32[]{:S(2)}) collective-permute-start(bf16[2,512,128]{2,1,0:T(8,128)(2,1)S(1)} %pad_maximum_fusion.refs_8_), channel_id=1, source_target_pairs={{0,16},{16,0},{32,48},{48,32},{1,17},{17,1},{33,49},{49,33},{2,18}... | collective-permute-start | bytes 786440 | tf_op jit(solution)/shard_map/gather_w/ppermute | solution.py:229
  42.9 7.1 %collective-permute-start.1 = (bf16[4,2,128,128]{3,2,1,0:T(8,128)(2,1)S(1)}, bf16[4,2,128,128]{3,2,1,0:T(8,128)(2,1)}, u32[]{:S(2)}, u32[]{:S(2)}) collective-permute-start(bf16[4,2,128,128]{3,2,1,0:T(8,128)(2,1)S(1)} %all-to-all-done.refs_0_), channel_id=1, source_target_pairs={{0,1},{1,0},{2,3},{3,2},{4,5},{5,4},{6,7},{7,6},{8,9},{9,8},{10,11... | collective-permute-start | bytes 786440 | tf_op jit(solution)/shard_map/gather_d/ppermute | solution.py:229
  42.9 7.1 %collective-permute-start.6 = (bf16[4,2,128,128]{3,2,1,0:T(8,128)(2,1)}, bf16[4,2,128,128]{3,2,1,0:T(8,128)(2,1)}, u32[]{:S(2)}, u32[]{:S(2)}) collective-permute-start(bf16[4,2,128,128]{3,2,1,0:T(8,128)(2,1)} %collective-permute-done.4.refs_5_), channel_id=1, source_target_pairs={{0,1},{1,0},{2,3},{3,2},{4,5},{5,4},{6,7},{7,6},{8,9},{9,8},{10,11... | collective-permute-start | bytes 786440 | tf_op jit(solution)/shard_map/gather_d/ppermute | solution.py:229
  43.4 6.6 %collective-permute-start.5 = (bf16[4,2,128,128]{3,2,1,0:T(8,128)(2,1)}, bf16[4,2,128,128]{3,2,1,0:T(8,128)(2,1)}, u32[]{:S(2)}, u32[]{:S(2)}) collective-permute-start(bf16[4,2,128,128]{3,2,1,0:T(8,128)(2,1)} %collective-permute-done.3.refs_4_), channel_id=1, source_target_pairs={{0,1},{1,0},{2,3},{3,2},{4,5},{5,4},{6,7},{7,6},{8,9},{9,8},{10,11... | collective-permute-start | bytes 786440 | tf_op jit(solution)/shard_map/gather_d/ppermute | solution.py:229
  43.5 6.5 %collective-permute-start.2 = (bf16[4,2,128,128]{3,2,1,0:T(8,128)(2,1)}, bf16[4,2,128,128]{3,2,1,0:T(8,128)(2,1)}, u32[]{:S(2)}, u32[]{:S(2)}) collective-permute-start(bf16[4,2,128,128]{3,2,1,0:T(8,128)(2,1)} %collective-permute-done.refs_1_), channel_id=1, source_target_pairs={{0,1},{1,0},{2,3},{3,2},{4,5},{5,4},{6,7},{7,6},{8,9},{9,8},{10,11... | collective-permute-start | bytes 786440 | tf_op jit(solution)/shard_map/gather_d/ppermute | solution.py:229
  44.0 15.7 %copy-start.9 = (bf16[256,512]{1,0:T(8,128)(2,1)S(1)}, bf16[256,512]{1,0:T(8,128)(2,1)}, u32[]{:S(2)}) copy-start(bf16[256,512]{1,0:T(8,128)(2,1)} %constant.68.clone.refs_7_) | copy-start | bytes 786436
  44.0 15.7 %copy-start.11 = (bf16[256,512]{1,0:T(8,128)(2,1)S(1)}, bf16[256,512]{1,0:T(8,128)(2,1)}, u32[]{:S(2)}) copy-start(bf16[256,512]{1,0:T(8,128)(2,1)} %constant.67.clone.refs_6_) | copy-start | bytes 786436
  44.0 15.7 %copy-start.13 = (bf16[512,256]{1,0:T(8,128)(2,1)S(1)}, bf16[512,256]{1,0:T(8,128)(2,1)}, u32[]{:S(2)}) copy-start(bf16[512,256]{1,0:T(8,128)(2,1)} %constant.62.clone.refs_1_) | copy-start | bytes 786436
  44.0 15.7 %copy-start.15 = (bf16[512,256]{1,0:T(8,128)(2,1)S(1)}, bf16[512,256]{1,0:T(8,128)(2,1)}, u32[]{:S(2)}) copy-start(bf16[512,256]{1,0:T(8,128)(2,1)} %constant.61.clone.refs_0_) | copy-start | bytes 786436
  44.0 15.7 %copy-start.17 = (f32[256,128]{1,0:T(8,128)S(1)}, f32[256,128]{1,0:T(8,128)}, u32[]{:S(2)}) copy-start(f32[256,128]{1,0:T(8,128)} %constant.70.clone.refs_9_) | copy-start | bytes 393220
  54.0 20.4 %all-to-all-start.1 = ((bf16[16,8,32,128]{3,2,1,0:T(8,128)(2,1)}), bf16[16,8,32,128]{3,2,1,0:T(8,128)(2,1)S(1)}, u32[]{:S(2)}, u32[]{:S(2)}) async-start(bf16[16,8,32,128]{3,2,1,0:T(8,128)(2,1)} %get-tuple-element.15), calls=%async_computation.1 | async-start | bytes 2097152 | tf_op jit(solution)/shard_map/grady/all_to_all | solution.py:233
  59.7 0.9 copy-start.18
  60.6 0.9 copy-start.20
  61.5 0.9 copy-start.22
  62.4 0.9 copy-start.24
  63.3 0.9 copy-start.26
  67.4 1.0 copy-start.5
  68.4 1.0 copy-start.6
  69.4 1.0 copy-start.8
  70.4 0.7 copy-start.30
  74.4 19.8 %all-to-all-start.4 = ((bf16[16,8,32,128]{3,2,1,0:T(8,128)(2,1)}), bf16[16,8,32,128]{3,2,1,0:T(8,128)(2,1)S(1)}, u32[]{:S(2)}, u32[]{:S(2)}) async-start(bf16[16,8,32,128]{3,2,1,0:T(8,128)(2,1)} %bitcast.10), calls=%async_computation.4 | async-start | bytes 2097152 | tf_op jit(solution)/shard_map/gated/all_to_all | solution.py:233
  78.3 1.2 copy-start.7
  79.5 0.9 copy-start.10
  80.5 0.9 copy-start.12
  81.4 0.9 copy-start.14
  82.4 0.9 copy-start.16
  83.3 0.9 copy-start.19
  84.2 0.9 copy-start.21
  85.1 0.9 copy-start.23
  86.0 0.9 copy-start.25
  86.9 0.9 copy-start.27
  87.8 0.9 copy-start.31
  93.3 0.9 copy-start.1
  94.2 20.6 %all-to-all-start.3 = ((bf16[32,3,32,128]{3,2,1,0:T(8,128)(2,1)}), bf16[32,3,32,128]{3,2,1,0:T(8,128)(2,1)S(1)}, u32[]{:S(2)}, u32[]{:S(2)}) async-start(bf16[32,3,32,128]{3,2,1,0:T(8,128)(2,1)} %copy-done.1), calls=%async_computation.3 | async-start | bytes 1572864 | tf_op jit(solution)/shard_map/back/all_to_all | solution.py:233
  102.8 1.6 %copy-start.2 = (bf16[2,8,4,128,128]{4,3,2,1,0:T(8,128)(2,1)S(1)}, bf16[2,8,4,128,128]{4,3,2,1,0:T(8,128)(2,1)}, u32[]{:S(2)}) copy-start(bf16[2,8,4,128,128]{4,3,2,1,0:T(8,128)(2,1)} %get-tuple-element.24.d_ref) | copy-start | bytes 6291460
  105.6 1.0 copy-start
  114.8 16.1 %all-to-all-start.5 = ((bf16[8,512,128]{2,1,0:T(8,128)(2,1)}), bf16[8,512,128]{2,1,0:T(8,128)(2,1)S(1)}, u32[]{:S(2)}, u32[]{:S(2)}) async-start(bf16[8,512,128]{2,1,0:T(8,128)(2,1)} %copy-done), calls=%async_computation.5 | async-start | bytes 2097152 | tf_op jit(solution)/shard_map/wo/all_to_all | solution.py:233
where the time goes:
time: 133 us; the launch traced here: 132 us
  waiting for transfers between devices  45.1 us (34%)
  starting transfers between devices  43.6 us (33%)
  local copies, waits for them, and re-layouts  26 us (20%)
  Pallas kernels  16.1 us (12%)
    all_to_all x6, starting transfers between devices, exchange(): return lax.all_to_all(value, axes, 0, 0)  32.7 us
    all_to_all x6, waiting for transfers between devices, exchange(): return lax.all_to_all(value, axes, 0, 0)  25.7 us
    unnamed x65, local copies, waits for them, and re-layouts  23.4 us
    ppermute x11, waiting for transfers between devices, flip(): return lax.ppermute(value, axes, [(i, i ^ by) for i in range(total)])  19.4 us
    pallas_call x7, Pallas kernels, call(): pl.pallas_call(kernel, out_shape=outs, in_specs=[first] + [VMEM] * (len(i...  16.1 us
    ppermute x11, starting transfers between devices, flip(): return lax.ppermute(value, axes, [(i, i ^ by) for i in range(total)])  10.9 us
  transfers between devices with their start and end apart: 17, of which 6 were waited for; matrix products, arithmetic and copies ran while one was open for 1% of the time, Pallas kernels for 11%

commit v1 on v0

v1 whole, which is shorter than its diff:
```python
import functools

import jax
import jax.numpy as jnp
import numpy as np
from jax import lax
from jax.experimental import pallas as pl
from jax.experimental.pallas import tpu as pltpu
from jax.sharding import Mesh
from jax.sharding import PartitionSpec as P

BF16 = jnp.bfloat16
F32 = jnp.float32
HBM = pl.BlockSpec(memory_space=pltpu.HBM)
PARAMS = pltpu.CompilerParams(vmem_limit_bytes=63 * 1024 * 1024)

M, N = 32, 128
GROUP = 8


def split(values):
    high = values.astype(jnp.bfloat16)
    return high, (values - high.astype(values.dtype)).astype(jnp.bfloat16)


@functools.cache
def tables():
    k1, m, n = np.arange(M) + 0.25, np.arange(M), np.arange(N)
    first = 2 * np.pi * np.outer(k1, m) / M
    second = 2 * np.pi * np.outer(n, n) / N
    turn = 2 * np.pi * np.outer(k1, n) / (M * N)
    eye = np.eye(GROUP)
    one = np.kron(np.concatenate([np.cos(first), -np.sin(first)]), eye)
    cos, sin = np.cos(second), np.sin(second)
    two = np.block([[cos, -sin], [sin, cos]])
    back_two = np.block([[cos, sin], [-sin, cos]])
    back_one = one.T / (M * N)

    parts = []
    for table in (one, two, back_two, back_one[:, :256], back_one[:, 256:]):
        high = table.astype(jnp.bfloat16)
        parts += [high, (table - high.astype(np.float64)).astype(jnp.bfloat16)]
    return np.concatenate(parts), np.stack([np.cos(turn), np.sin(turn)]).astype(np.float32)


ROWS = {}
for _name, _count in (("one", 512), ("two", 256), ("back_two", 256), ("left", 256), ("right", 256)):
    for _part in "hl":
        ROWS[_name, _part] = (sum(n for _, n in ROWS.values()), _count)


def table(tabs, name):
    return [tabs[0][start : start + count] for start, count in (ROWS[name, p] for p in "hl")]


def turns(tabs):
    return [
        jnp.broadcast_to(tabs[1][i][:, None, :], (M, GROUP, N)).reshape(M * GROUP, N)
        for i in range(2)
    ]


def dot(lhs, rhs):
    return jnp.dot(lhs, rhs, preferred_element_type=F32)


def rows_of(block, group):
    part = block[:, group * GROUP : (group + 1) * GROUP, :]
    return part.reshape(M * GROUP, N).astype(BF16)


def forward(sides, tabs):
    (one_h, one_l), (two_h, two_l) = table(tabs, "one"), table(tabs, "two")
    cos, sin = turns(tabs)
    cat = jnp.concatenate(sides, axis=1)
    part = dot(one_h, cat) + dot(one_l, cat)
    half = part.shape[0] // 2
    out = []
    for index in range(len(sides)):
        lanes = slice(index * N, (index + 1) * N)
        re, im = part[:half, lanes], part[half:, lanes]
        turned = jnp.concatenate([re * cos + im * sin, im * cos - re * sin], axis=1)
        high, low = split(turned)
        out.append(dot(high, two_h) + dot(low, two_h) + dot(high, two_l))
    return out


def inverse(specs, tabs):
    two_h, two_l = table(tabs, "back_two")
    one_h, one_l = (jnp.concatenate(p, axis=1) for p in zip(table(tabs, "left"), table(tabs, "right")))
    cos, sin = turns(tabs)
    cols = []
    for spec in specs:
        high, low = split(spec)
        part = dot(high, two_h) + dot(low, two_h) + dot(high, two_l)
        re, im = part[:, :N], part[:, N:]
        cols.append(jnp.concatenate([re * cos - im * sin, im * cos + re * sin], axis=0))
    high, low = split(jnp.concatenate(cols, axis=1))
    full = dot(one_h, high) + dot(one_h, low) + dot(one_l, high)
    return [full[:, i * N : (i + 1) * N] for i in range(len(specs))]


def times(a, b, conj_a):
    are, aim, bre, bim = a[:, :N], a[:, N:], b[:, :N], b[:, N:]
    if conj_a:
        return jnp.concatenate([are * bre + aim * bim, are * bim - aim * bre], axis=1)
    return jnp.concatenate([are * bre - aim * bim, are * bim + aim * bre], axis=1)


def pair_of(first, second):
    shape = (M, GROUP, N)
    return jnp.concatenate([first.reshape(shape), second.reshape(shape)], axis=1)


def prep_kernel(where, ins, outs, scratch, ready, emit):
    key_ref, value_ref, filt_ref, query_ref, skip_ref, w_ref, d_ref = ins
    (skip_s,) = scratch
    xl, y, z = where[0], where[1], where[3]

    def put(which, block):
        outs[0][:, which] = block.T.reshape(M, 32, N).astype(BF16)
        emit(0, slice(None), which)

    ready(0, 1)
    signal = key_ref[...].astype(F32) * value_ref[...].astype(F32)
    put(0, signal.astype(BF16).astype(F32))
    ready(2)
    put(1, filt_ref[...].astype(F32))
    ready(3)
    put(2, query_ref[...].astype(F32))
    ready(6)
    for to_y in range(4):
        for to_z in range(4):
            for lo in range(2):
                first = (4 * lo + to_z) * 128
                block = d_ref[32 * to_y : 32 * to_y + 32, first : first + 128]
                for side in range(2):
                    outs[0][side * 16 + to_y * 4 + to_z, 3 + lo] = block
    emit(0, slice(None), slice(3, 5))
    ready(4)
    row = jnp.broadcast_to(skip_ref[pl.ds(xl * 4 + y, 1), :], (N, N))
    skip_s[...] = row.T.reshape(4, 32, N)
    outs[3][...] = skip_s[z]
    emit(3)
    ready(5)
    for i in range(2):
        outs[1 + i][...] = w_ref[xl ^ i]
        emit(1 + i)


def swap_quarters(blocks):
    quarter = lax.broadcasted_iota(jnp.int32, blocks[0].shape, blocks[0].ndim - 1) // 32
    axis = blocks[0].ndim - 1
    out = []
    for r in range(4):
        total = blocks[r]
        for y in range(4):
            if y != r:
                total = jnp.where(
                    quarter == y, pltpu.roll(blocks[y], (y - r) * 32 % N, axis), total
                )
        out.append(total)
    return out


def conv_kernel(_, ins, outs, scratch, ready, emit):
    in_ref, skip_ref, *tabs = ins
    conv_ref, gated_ref, sig_ref, fil_ref = outs
    ready(0)
    signal, filt, query = (in_ref[:, i].astype(F32) for i in range(3))
    ready(1, 2, 3)
    for pair in range(2):
        groups = (2 * pair, 2 * pair + 1)
        chans = slice(16 * pair, 16 * pair + 16)
        spectra = forward([rows_of(a, g) for a in (signal, filt) for g in groups], tabs)
        for i, g in enumerate(groups):
            sig_ref[g], fil_ref[g] = spectra[i], spectra[2 + i]
        emit(2, slice(2 * pair, 2 * pair + 2))
        emit(3, slice(2 * pair, 2 * pair + 2))
        conv = pair_of(*inverse([times(spectra[i], spectra[2 + i], False) for i in range(2)], tabs))
        conv = conv + skip_ref[chans, :][None] * signal[:, chans, :]
        conv = conv.astype(BF16)
        conv_ref[:, chans, :] = conv
        gated = (query[:, chans, :] * conv.astype(F32)).reshape(8, 4, 16, N)
        for y, block in enumerate(swap_quarters([gated[:, r] for r in range(4)])):
            for copy in range(4):
                gated_ref[y, copy, :, chans, :] = block.astype(BF16)
        every = slice(None)
        emit(1, every, every, every, chans)
        emit(0, every, chans)


def back_kernel(_, ins, outs, scratch, ready, emit):
    part_ref, in_ref, conv_ref, skip_ref, sig_ref, fil_ref, *tabs = ins
    (out_ref,), (gate_s,) = outs, scratch
    ready(0, 1, 2)
    for g in range(8):
        totals = []
        for y in range(4):
            total = part_ref[4 * y, g].astype(F32)
            for z in range(1, 4):
                total = total + part_ref[4 * y + z, g].astype(F32)
            totals.append(total)
        for r, grady in enumerate(swap_quarters(totals)):
            m = 4 * g + r
            out_ref[m, 0] = (grady * conv_ref[m].astype(F32)).astype(BF16)
            gate_s[m] = (grady * in_ref[m].astype(F32)).astype(BF16).astype(F32)
    emit(0, slice(None), 0)
    gate = gate_s[...]
    ready(*range(3, 8))
    for pair in range(2):
        groups = (2 * pair, 2 * pair + 1)
        chans = slice(16 * pair, 16 * pair + 16)
        spectra = forward([rows_of(gate, g) for g in groups], tabs)
        specs = [times(fil_ref[g], s, True) for g, s in zip(groups, spectra)]
        specs += [times(sig_ref[g], s, True) for g, s in zip(groups, spectra)]
        result = inverse(specs, tabs)
        back = pair_of(*result[:2]) + skip_ref[chans, :][None] * gate[:, chans, :]
        out_ref[:, 1, chans, :] = back.astype(BF16)
        emit(0, slice(None), 1, chans)
        out_ref[:, 2, chans, :] = pair_of(*result[2:]).astype(BF16)
        emit(0, slice(None), 2, chans)


def final_kernel(_, ins, outs, scratch, ready, emit):
    in_ref, key_ref, value_ref = ins

    def get(which):
        return in_ref[:, which].astype(F32).reshape(M * 32, N).T

    def put(which, block):
        outs[which][...] = block.astype(BF16)
        emit(which)

    ready(0)
    put(0, get(0))
    put(3, get(2))
    ready(1, 2)
    back = get(1)
    put(1, back * value_ref[...].astype(F32))
    put(2, back * key_ref[...].astype(F32))


def grady_kernel(where, ins, outs, scratch, ready, emit):
    d_refs, w_refs, (out_ref, d_ref), (w_s,) = ins[:4], ins[4:], outs, scratch
    xl, y, q = where[0], where[1], where[2]
    for p in range(4):
        ready(p)
        for lo in range(2):
            d_ref[2 * (q ^ (2 * (p & 1) + (p >> 1))) + lo] = d_refs[p][:, lo]
    emit(1)
    for s in range(4):
        ready(4 + s)
        for i in range(2):
            w_s[(xl ^ i) * 4 + (y ^ s)] = w_refs[s][i]
    lhs = jnp.concatenate([w_s[j] for j in range(8)], axis=1)
    for g in range(0, 8, 2):
        rhs = jnp.concatenate(
            [d_ref[j, 4 * g : 4 * g + 8].reshape(2 * N, 128) for j in range(8)], axis=1
        )
        part = lax.dot_general(lhs, rhs, (((1,), (1,)), ((), ())), preferred_element_type=F32)
        part = part.astype(BF16)
        for k in range(2):
            out_ref[:, g + k] = part[:, k * N : (k + 1) * N].reshape(16, 32, N)
        emit(0, slice(None), slice(g, g + 2))


def wo_kernel(where, ins, outs, scratch, ready, emit):
    (gated_ref, d_ref), (all_s,) = ins, scratch
    ready(0, 1)
    lhs = jnp.concatenate([gated_ref[:, b].reshape(512, N) for b in range(8)], axis=1)
    for xl in range(2):
        for to in range(0, 4, 2):
            rhs = jnp.concatenate(
                [d_ref[xl * 4 + to + k].reshape(1024, 128) for k in range(2)], axis=1
            )
            part = dot(lhs, rhs)
            for k in range(2):
                all_s[to + k, xl] = part[:, k * 128 : (k + 1) * 128].astype(BF16)
    for s in range(4):
        outs[s][...] = all_s[where[1] ^ s]
        emit(s)


def give_kernel(where, ins, outs, scratch, ready, emit):
    ready(0, 1, 2, 3)
    total = ins[0][where[0] ^ 1].astype(F32)
    for s in range(1, 4):
        total = total + ins[s][where[0] ^ 1].astype(F32)
    outs[0][...] = total.astype(BF16)
    emit(0)


def join_kernel(where, ins, outs, scratch, ready, emit):
    ready(0, 1, 2, 3, 4)
    total = ins[0][where[0]].astype(F32)
    for s in range(1, 4):
        total = total + ins[s][where[0]].astype(F32)
    outs[0][where[0]] = total
    outs[0][where[0] ^ 1] = ins[4][...].astype(F32)
    emit(0)


def call(kernel, ins, outs, scratch=(), parts={}, cost=2):
    n_in, n_out = len(ins), len(outs)

    def whole(*refs):
        xl, y, z, xh, co = (lax.axis_index(a) for a in ("xl", "y", "z", "xh", "co"))
        where = (xl, y, 2 * xh + co, z)
        hbm_in, refs = refs[:n_in], refs[n_in:]
        hbm_out, refs = refs[:n_out], refs[n_out:]
        in_refs, refs = refs[:n_in], refs[n_in:]
        out_refs, refs = refs[:n_out], refs[n_out:]
        (in_sem, out_sem), rest = refs[:2], refs[2:]
        loads = [
            pltpu.make_async_copy(
                hbm_in[i].at[parts[i]] if i in parts else hbm_in[i], in_refs[i], in_sem.at[i]
            )
            for i in range(n_in)
        ]
        for load in loads:
            load.start()
        waited, stores = set(), []

        def ready(*which):
            for i in which:
                if i not in waited:
                    waited.add(i)
                    loads[i].wait()

        def emit(j, *index):
            source, target = out_refs[j], hbm_out[j]
            if index:
                source, target = source.at[index], target.at[index]
            stores.append(pltpu.make_async_copy(source, target, out_sem.at[len(stores)]))
            stores[-1].start()

        kernel(where, in_refs, out_refs, rest, ready, emit)
        ready(*range(n_in))
        for store in stores:
            store.wait()

    shapes = [
        jax.eval_shape(lambda x, i=i: x[parts[i]], a) if i in parts else a
        for i, a in enumerate(ins)
    ]
    buffers = [pltpu.VMEM(a.shape, a.dtype) for a in (*shapes, *outs)]
    return pl.pallas_call(
        whole,
        out_shape=list(outs),
        in_specs=[HBM] * n_in,
        out_specs=[HBM] * n_out,
        scratch_shapes=buffers
        + [pltpu.SemaphoreType.DMA((n_in,)), pltpu.SemaphoreType.DMA((16,))]
        + list(scratch),
        compiler_params=PARAMS,
        cost_estimate=pl.CostEstimate(
            flops=0, bytes_accessed=cost * 3_000_000, transcendentals=0
        ),
    )(*ins)


def shape(*dims, dtype=BF16):
    return jax.ShapeDtypeStruct(dims, dtype)


CONTEXT = ("xl", "y", "z")


def flip(value, axes, sizes, by):
    total = int(np.prod(sizes))
    return lax.ppermute(value, axes, [(i, i ^ by) for i in range(total)])


def exchange(value, axes):
    return lax.all_to_all(value, axes, 0, 0)


def body(query, key_feat, value_feat, filt, skip, dout, w_out):
    tabs = tables()

    with jax.named_scope("prepare"):
        sent, keep, give, skip_c = call(
            prep_kernel,
            (key_feat, value_feat, filt, query, skip.reshape(8, 128), w_out.reshape(2, 512, 128), dout),
            [shape(M, 5, 32, N)] + [shape(512, 128)] * 2 + [shape(32, N, dtype=F32)],
            [pltpu.VMEM((4, 32, N), F32)],
            cost=3,
        )
    with jax.named_scope("to_channels"):
        held = exchange(sent, CONTEXT)
    with jax.named_scope("gather_w"):
        take = flip(give, "xl", (2,), 1)
    held, take = lax.optimization_barrier((held, take))
    with jax.named_scope("gather_d"):
        d = held[:, 3:]
        d = [d, flip(d, ("xl", "xh"), (2, 2), 3)]
    with jax.named_scope("gather_w"):
        w = jnp.stack([keep, take])
        w = [w] + [flip(w, "y", (4,), s) for s in (1, 2, 3)]
    with jax.named_scope("conv"):
        conv, gated, sig, fil = call(
            conv_kernel,
            (held, skip_c, *tabs),
            (
                shape(M, 32, N),
                shape(4, 4, 8, 32, N),
                shape(4, 256, 256, dtype=F32),
                shape(4, 256, 256, dtype=F32),
            ),
            (),
            {0: (slice(None), slice(0, 3))},
            cost=20,
        )
    gated, d, w = lax.optimization_barrier((gated, d, w))
    with jax.named_scope("gated"):
        gated = exchange(gated.reshape(16, 8, 32, N), ("y", "z"))
    with jax.named_scope("gather_d"):
        d_pieces = d + [flip(piece, "co", (2,), 1) for piece in d]
    with jax.named_scope("grady"):
        part, d_all = call(
            grady_kernel,
            (*d_pieces, *w),
            (shape(16, 8, 32, N), shape(8, 32, 32, 128)),
            [pltpu.VMEM((8, 512, 128), BF16)],
            cost=5,
        )
        part, gated = lax.optimization_barrier((part, gated))
        part = exchange(part, ("y", "z"))
    with jax.named_scope("wo"):
        wo = call(
            wo_kernel,
            (gated, d_all),
            [shape(2, 512, 128)] * 4,
            [pltpu.VMEM((4, 2, 512, 128), BF16)],
            cost=5,
        )
        part, _ = lax.optimization_barrier((part, wo))
        wo = [wo[0]] + [flip(wo[s], "y", (4,), s) for s in (1, 2, 3)]
    with jax.named_scope("back"):
        (sent,) = call(
            back_kernel,
            (part, held, conv, skip_c, sig, fil, *tabs),
            [shape(M, 3, 32, N)],
            [pltpu.VMEM((M, 32, N), F32)],
            {1: (slice(None), 2)},
            cost=7,
        )
    with jax.named_scope("wo"):
        sent, wo = lax.optimization_barrier((sent, wo))
        (give,) = call(give_kernel, wo, [shape(512, 128)])
        sent, give = lax.optimization_barrier((sent, give))
        take = flip(give, "xl", (2,), 1)
    with jax.named_scope("back"):
        got = exchange(sent, CONTEXT)
    with jax.named_scope("wo"):
        (wo_grad,) = call(
            join_kernel, (*wo, take), [shape(2, 512, 128, dtype=F32)]
        )
    with jax.named_scope("final"):
        grads = call(final_kernel, (got, key_feat, value_feat), [shape(128, 1024)] * 4)
    return (*grads, wo_grad.reshape(1024, 128))


def solution(mesh):
    fine = Mesh(mesh.devices.reshape(2, 4, 4, 2, 2), ("xl", "y", "z", "xh", "co"))
    tokens, channels = P(CONTEXT, ("xh", "co")), P(("xh", "co"))
    rows = P(("xh", "co"), CONTEXT)
    return jax.shard_map(
        body,
        mesh=fine,
        in_specs=(tokens, tokens, tokens, tokens, channels, tokens, rows),
        out_specs=(tokens, tokens, tokens, tokens, rows),
        check_vma=False,
    )
```

time: 133 us -> 127 us (0.955)
  local copies, waits for them, and re-layouts: 26 us -> 4.89 us
  Pallas kernels: 16.1 us -> 30.7 us
  waiting for transfers between devices: 45.1 us -> 48 us
  starting transfers between devices: 43.6 us -> 41.4 us
    unnamed x65 -> x24, local copies, waits for them, and re-layouts: 23.4 us -> 4.83 us
    pallas_call x7 -> x8, Pallas kernels: 16.1 us -> 30.7 us  [call(): pl.pallas_call(whole, out_shape=list(outs), in_specs=[HBM] * n_in, out_sp...]
    ppermute x11, waiting for transfers between devices: 19.4 us -> 31.6 us  [flip(): return lax.ppermute(value, axes, [(i, i ^ by) for i in range(total)])]
    all_to_all x6 -> x4, waiting for transfers between devices: 25.7 us -> 16.4 us  [exchange(): return lax.all_to_all(value, axes, 0, 0)]
    all_to_all x6 -> x4, starting transfers between devices: 32.7 us -> 26.1 us  [exchange(): return lax.all_to_all(value, axes, 0, 0)]
    ppermute x11, starting transfers between devices: 10.9 us -> 15.4 us  [flip(): return lax.ppermute(value, axes, [(i, i ^ by) for i in range(total)])]
    dynamic_slice x2 -> x0, local copies, waits for them, and re-layouts: 1.75 us -> none  [the longest x1 0.99 us: body(): keep = lax.dynamic_index_in_dim(halves, xl, 0, keepdims=False)]
  transfers between devices with their start and end apart: 17 -> 15, of which waited for: 6 -> 10; matrix products, arithmetic and copies ran while one was open for 1% -> 0% of each run, Pallas kernels for 11% -> 19%
where the time goes in v1:
time: 127 us; the launch traced here: 126 us
  waiting for transfers between devices  48 us (38%)
  starting transfers between devices  41.4 us (33%)
  Pallas kernels  30.7 us (24%)
  local copies, waits for them, and re-layouts  4.89 us (4%)
    ppermute x11, waiting for transfers between devices, flip(): return lax.ppermute(value, axes, [(i, i ^ by) for i in range(total)])  31.6 us
    pallas_call x8, Pallas kernels, call(): pl.pallas_call(whole, out_shape=list(outs), in_specs=[HBM] * n_in, out_sp...  30.7 us
    all_to_all x4, starting transfers between devices, exchange(): return lax.all_to_all(value, axes, 0, 0)  26.1 us
    all_to_all x4, waiting for transfers between devices, exchange(): return lax.all_to_all(value, axes, 0, 0)  16.4 us
    ppermute x11, starting transfers between devices, flip(): return lax.ppermute(value, axes, [(i, i ^ by) for i in range(total)])  15.4 us
    unnamed x24, local copies, waits for them, and re-layouts  4.83 us
  transfers between devices with their start and end apart: 15, of which 10 were waited for; matrix products, arithmetic and copies ran while one was open for 0% of the time, Pallas kernels for 19%

profile of v1, /device:TPU:0, one launch (start us, length us, event | category | flops | bytes accessed | tf_op | source)
XLA Modules:
  0.0 126.1 jit_solution(13188058885864255012)
XLA Ops:
  0.6 2.6 %prepare.1 = (bf16[32,5,32,128]{3,2,1,0:T(8,128)(2,1)}, bf16[512,128]{1,0:T(8,128)(2,1)}, bf16[512,128]{1,0:T(8,128)(2,1)}, f32[32,128]{1,0:T(8,128)}) custom-call(bf16[128,1024]{1,0:T(8,128)(2,1)} %refs_1_.3, bf16[128,1024]{1,0:T(8,128)(2,1)} %refs_2_.4, bf16[128,1024]{1,0:T(8,128)(2,1)} %refs_2_.3, bf16[128,1024]{1,0:T(8,128)(2,1)} %refs_3_.2, ...), custom_call_target="tpu_custom_call" | custom-call | bytes 9000000 | tf_op jit(solution)/shard_map/prepare/pallas_call | solution.py:348
  3.3 0.0 copy-start.11
  3.3 0.0 copy-start.9
  3.3 9.5 %all-to-all-start = ((bf16[32,5,32,128]{3,2,1,0:T(8,128)(2,1)}), bf16[32,5,32,128]{3,2,1,0:T(8,128)(2,1)S(1)}, u32[]{:S(2)}, u32[]{:S(2)}) async-start(bf16[32,5,32,128]{3,2,1,0:T(8,128)(2,1)} %get-tuple-element.42), calls=%async_computation | async-start | bytes 2621440 | tf_op jit(solution)/shard_map/to_channels/all_to_all | solution.py:376
  12.8 0.0 copy-done.11
  12.8 1.9 %collective-permute-start = (bf16[512,128]{1,0:T(8,128)(2,1)S(1)}, bf16[512,128]{1,0:T(8,128)(2,1)S(1)}, u32[]{:S(2)}, u32[]{:S(2)}) collective-permute-start(bf16[512,128]{1,0:T(8,128)(2,1)S(1)} %copy-done.11), channel_id=1, source_target_pairs={{0,64},{64,0},{1,65},{65,1},{2,66},{66,2},{3,67},{67,3},{4,68},{68... | collective-permute-start | bytes 393224 | tf_op jit(solution)/shard_map/gather_w/ppermute | solution.py:372
  14.7 17.0 %collective-permute-done = bf16[512,128]{1,0:T(8,128)(2,1)S(1)} collective-permute-done((bf16[512,128]{1,0:T(8,128)(2,1)S(1)}, bf16[512,128]{1,0:T(8,128)(2,1)S(1)}, u32[]{:S(2)}, u32[]{:S(2)}) %collective-permute-start) | collective-permute-done | bytes 131104 | tf_op jit(solution)/shard_map/gather_w/ppermute | solution.py:372
  31.7 0.9 all-to-all-done.refs_0_.refs_1_
  32.6 0.0 copy-start
  32.6 1.1 copy-done
  33.6 0.1 slice.3.refs_0_
  33.7 0.0 copy-start.2
  33.7 2.1 %collective-permute-start.1 = (bf16[32,2,32,128]{3,2,1,0:T(8,128)(2,1)S(1)}, bf16[32,2,32,128]{3,2,1,0:T(8,128)(2,1)}, u32[]{:S(2)}, u32[]{:S(2)}) collective-permute-start(bf16[32,2,32,128]{3,2,1,0:T(8,128)(2,1)S(1)} %slice.3.refs_0_), channel_id=1, source_target_pairs={{0,66},{2,64},{64,2},{66,0},{1,67},{3,65},{65,3},{67,1},{4,70},{6,... | collective-permute-start | bytes 1572872 | tf_op jit(solution)/shard_map/gather_d/ppermute | solution.py:372
  35.8 0.0 copy-done.9
  35.8 0.0 copy-start.3
  35.8 2.5 %collective-permute-start.4 = (bf16[2,512,128]{2,1,0:T(8,128)(2,1)S(1)}, bf16[2,512,128]{2,1,0:T(8,128)(2,1)}, u32[]{:S(2)}, u32[]{:S(2)}) collective-permute-start(bf16[2,512,128]{2,1,0:T(8,128)(2,1)S(1)} %pad_maximum_fusion.refs_4_), channel_id=1, source_target_pairs={{0,48},{16,32},{32,16},{48,0},{1,49},{17,33},{33,17},{49,1},{2,50}... | collective-permute-start | bytes 786440 | tf_op jit(solution)/shard_map/gather_w/ppermute | solution.py:372
  38.3 0.9 collective-permute-start.3
  39.3 0.7 collective-permute-start.2
  40.0 6.1 %conv.1 = (bf16[32,32,128]{2,1,0:T(8,128)(2,1)}, bf16[4,4,8,32,128]{4,3,2,1,0:T(8,128)(2,1)}, f32[4,256,256]{2,1,0:T(8,128)}, f32[4,256,256]{2,1,0:T(8,128)}) custom-call(bf16[32,5,32,128]{3,2,1,0:T(8,128)(2,1)} %copy-done, f32[32,128]{1,0:T(8,128)} %get-tuple-element.45.refs_1_.refs_3_, bf16[3072,256]{1,0:T(8,128)(2,1)} %constant.4.clone.refs_2_.refs_6_, ...), custom_call_target="tpu_custom_call" | custom-call | bytes 60000000 | tf_op jit(solution)/shard_map/conv/pallas_call | solution.py:348
  46.1 2.7 %collective-permute-done.4.refs_7_ = bf16[2,512,128]{2,1,0:T(8,128)(2,1)} collective-permute-done((bf16[2,512,128]{2,1,0:T(8,128)(2,1)S(1)}, bf16[2,512,128]{2,1,0:T(8,128)(2,1)}, u32[]{:S(2)}, u32[]{:S(2)}) %collective-permute-start.4) | collective-permute-done | bytes 262176 | tf_op jit(solution)/shard_map/gather_w/ppermute | solution.py:372
  48.8 0.0 collective-permute-done.3.refs_6_
  48.8 0.6 collective-permute-done.2.refs_5_
  49.4 0.0 collective-permute-done.1.refs_1_
  49.4 0.0 copy-done.3
  49.4 6.4 %all-to-all-start.1 = ((bf16[16,8,32,128]{3,2,1,0:T(8,128)(2,1)}), bf16[16,8,32,128]{3,2,1,0:T(8,128)(2,1)}, u32[]{:S(2)}, u32[]{:S(2)}) async-start(bf16[16,8,32,128]{3,2,1,0:T(8,128)(2,1)} %bitcast.6), calls=%async_computation.1 | async-start | bytes 2097152 | tf_op jit(solution)/shard_map/gated/all_to_all | solution.py:376
  55.8 0.0 copy-done.2
  55.8 0.1 collective-permute-start.5
  55.9 0.5 collective-permute-start.6
  56.4 1.4 %collective-permute-done.5.refs_2_ = bf16[32,2,32,128]{3,2,1,0:T(8,128)(2,1)S(1)} collective-permute-done((bf16[32,2,32,128]{3,2,1,0:T(8,128)(2,1)S(1)}, bf16[32,2,32,128]{3,2,1,0:T(8,128)(2,1)S(1)}, u32[]{:S(2)}, u32[]{:S(2)}) %collective-permute-start.5) | collective-permute-done | bytes 524320 | tf_op jit(solution)/shard_map/gather_d/ppermute | solution.py:372
  57.8 0.0 copy-start.7
  57.8 0.8 copy-done.7
  58.6 0.3 collective-permute-done.6.refs_3_
  58.9 4.2 %grady.1 = (bf16[16,8,32,128]{3,2,1,0:T(8,128)(2,1)}, bf16[8,32,32,128]{3,2,1,0:T(8,128)(2,1)}) custom-call(bf16[32,2,32,128]{3,2,1,0:T(8,128)(2,1)} %copy-done.2, bf16[32,2,32,128]{3,2,1,0:T(8,128)(2,1)} %collective-permute-done.1.refs_1_, bf16[32,2,32,128]{3,2,1,0:T(8,128)(2,1)} %copy-done.7, bf16[32,2,32,128]{3,2,1,0:T(8,128)(2,1)} %collective-permute-done.6.refs_3_, ...), custom_call_target="tpu_custom_call" | custom-call | bytes 15000000 | tf_op jit(solution)/shard_map/grady/pallas_call | solution.py:348
  63.1 8.5 %all-to-all-done.1.refs_0_ = bf16[16,8,32,128]{3,2,1,0:T(8,128)(2,1)} async-done(((bf16[16,8,32,128]{3,2,1,0:T(8,128)(2,1)}), bf16[16,8,32,128]{3,2,1,0:T(8,128)(2,1)}, u32[]{:S(2)}, u32[]{:S(2)}) %all-to-all-start.1) | async-done | bytes 1048608 | tf_op jit(solution)/shard_map/gated/all_to_all | solution.py:376
  71.6 4.3 %all-to-all-start.2 = ((bf16[16,8,32,128]{3,2,1,0:T(8,128)(2,1)}), bf16[16,8,32,128]{3,2,1,0:T(8,128)(2,1)}, u32[]{:S(2)}, u32[]{:S(2)}) async-start(bf16[16,8,32,128]{3,2,1,0:T(8,128)(2,1)} %get-tuple-element.57), calls=%async_computation.2 | async-start | bytes 2097152 | tf_op jit(solution)/shard_map/grady/all_to_all | solution.py:376
  75.9 4.3 %wo.3 = (bf16[2,512,128]{2,1,0:T(8,128)(2,1)}, bf16[2,512,128]{2,1,0:T(8,128)(2,1)}, bf16[2,512,128]{2,1,0:T(8,128)(2,1)}, bf16[2,512,128]{2,1,0:T(8,128)(2,1)}) custom-call(bf16[16,8,32,128]{3,2,1,0:T(8,128)(2,1)} %all-to-all-done.1.refs_0_, bf16[8,32,32,128]{3,2,1,0:T(8,128)(2,1)} %get-tuple-element.59.refs_1_), custom_call_target="tpu_custom_call" | custom-call | bytes 15000000 | tf_op jit(solution)/shard_map/wo/pallas_call | solution.py:348
  80.2 1.8 %collective-permute-start.7 = (bf16[2,512,128]{2,1,0:T(8,128)(2,1)}, bf16[2,512,128]{2,1,0:T(8,128)(2,1)S(1)}, u32[]{:S(2)}, u32[]{:S(2)}) collective-permute-start(bf16[2,512,128]{2,1,0:T(8,128)(2,1)} %get-tuple-element.61), channel_id=1, source_target_pairs={{0,16},{16,0},{32,48},{48,32},{1,17},{17,1},{33,49},{49,33},{2,18}... | collective-permute-start | bytes 786440 | tf_op jit(solution)/shard_map/wo/ppermute | solution.py:372
  82.1 2.8 %collective-permute-start.8 = (bf16[2,512,128]{2,1,0:T(8,128)(2,1)}, bf16[2,512,128]{2,1,0:T(8,128)(2,1)S(1)}, u32[]{:S(2)}, u32[]{:S(2)}) collective-permute-start(bf16[2,512,128]{2,1,0:T(8,128)(2,1)} %get-tuple-element.62), channel_id=1, source_target_pairs={{0,32},{16,48},{32,0},{48,16},{1,33},{17,49},{33,1},{49,17},{2,34}... | collective-permute-start | bytes 786440 | tf_op jit(solution)/shard_map/wo/ppermute | solution.py:372
  84.9 0.2 collective-permute-start.9
  85.0 7.1 %all-to-all-done.2.refs_0_ = bf16[16,8,32,128]{3,2,1,0:T(8,128)(2,1)} async-done(((bf16[16,8,32,128]{3,2,1,0:T(8,128)(2,1)}), bf16[16,8,32,128]{3,2,1,0:T(8,128)(2,1)}, u32[]{:S(2)}, u32[]{:S(2)}) %all-to-all-start.2) | async-done | bytes 1048608 | tf_op jit(solution)/shard_map/grady/all_to_all | solution.py:376
  92.1 6.7 %back.1 = bf16[32,3,32,128]{3,2,1,0:T(8,128)(2,1)} custom-call(bf16[16,8,32,128]{3,2,1,0:T(8,128)(2,1)} %all-to-all-done.2.refs_0_, bf16[32,5,32,128]{3,2,1,0:T(8,128)(2,1)} %copy-done, bf16[32,32,128]{2,1,0:T(8,128)(2,1)} %get-tuple-element.65.refs_2_, f32[32,128]{1,0:T(8,128)} %get-tuple-element.45.refs_1_.refs_3_, ...), custom_call_target="tpu_custom_call" | custom-call | bytes 21000000 | tf_op jit(solution)/shard_map/back/pallas_call | solution.py:348
  98.8 0.0 collective-permute-done.7.refs_1_
  98.8 0.0 copy-start.4
  98.8 1.5 %collective-permute-done.8.refs_2_ = bf16[2,512,128]{2,1,0:T(8,128)(2,1)S(1)} collective-permute-done((bf16[2,512,128]{2,1,0:T(8,128)(2,1)}, bf16[2,512,128]{2,1,0:T(8,128)(2,1)S(1)}, u32[]{:S(2)}, u32[]{:S(2)}) %collective-permute-start.8) | collective-permute-done | bytes 262176 | tf_op jit(solution)/shard_map/wo/ppermute | solution.py:372
  100.2 0.0 copy-start.5
  100.2 0.0 collective-permute-done.9.refs_3_
  100.2 0.0 copy-done.4
  100.2 0.7 copy-done.5
  100.9 0.0 copy-start.6
  100.9 0.7 copy-done.6
  101.6 2.1 %wo.4 = bf16[512,128]{1,0:T(8,128)(2,1)} custom-call(bf16[2,512,128]{2,1,0:T(8,128)(2,1)} %get-tuple-element.69.refs_0_, bf16[2,512,128]{2,1,0:T(8,128)(2,1)} %copy-done.4, bf16[2,512,128]{2,1,0:T(8,128)(2,1)} %copy-done.5, bf16[2,512,128]{2,1,0:T(8,128)(2,1)} %copy-done.6), custom_call_target="tpu_custom_call" | custom-call | bytes 6000000 | tf_op jit(solution)/shard_map/wo/pallas_call | solution.py:348
  103.7 0.0 copy-start.8
  103.7 5.9 %all-to-all-start.3 = ((bf16[32,3,32,128]{3,2,1,0:T(8,128)(2,1)}), bf16[32,3,32,128]{3,2,1,0:T(8,128)(2,1)S(1)}, u32[]{:S(2)}, u32[]{:S(2)}) async-start(bf16[32,3,32,128]{3,2,1,0:T(8,128)(2,1)} %back.1), calls=%async_computation.3 | async-start | bytes 1572864 | tf_op jit(solution)/shard_map/back/all_to_all | solution.py:376
  109.6 0.0 copy-done.8
  109.6 1.9 %collective-permute-start.10 = (bf16[512,128]{1,0:T(8,128)(2,1)S(1)}, bf16[512,128]{1,0:T(8,128)(2,1)S(1)}, u32[]{:S(2)}, u32[]{:S(2)}) collective-permute-start(bf16[512,128]{1,0:T(8,128)(2,1)S(1)} %copy-done.8), channel_id=1, source_target_pairs={{0,64},{64,0},{1,65},{65,1},{2,66},{66,2},{3,67},{67,3},{4,68},{68... | collective-permute-start | bytes 393224 | tf_op jit(solution)/shard_map/wo/ppermute | solution.py:372
  111.5 8.1 %collective-permute-done.10.refs_4_ = bf16[512,128]{1,0:T(8,128)(2,1)S(1)} collective-permute-done((bf16[512,128]{1,0:T(8,128)(2,1)S(1)}, bf16[512,128]{1,0:T(8,128)(2,1)S(1)}, u32[]{:S(2)}, u32[]{:S(2)}) %collective-permute-start.10) | collective-permute-done | bytes 131104 | tf_op jit(solution)/shard_map/wo/ppermute | solution.py:372
  119.6 0.0 copy-start.10
  119.6 0.7 copy-done.10
  120.3 2.3 %wo.5 = f32[2,512,128]{2,1,0:T(8,128)} custom-call(bf16[2,512,128]{2,1,0:T(8,128)(2,1)} %get-tuple-element.69.refs_0_, bf16[2,512,128]{2,1,0:T(8,128)(2,1)} %copy-done.4, bf16[2,512,128]{2,1,0:T(8,128)(2,1)} %copy-done.5, bf16[2,512,128]{2,1,0:T(8,128)(2,1)} %copy-done.6, bf16[512,128]{1,0:T(8,128)(2,1)} %copy-done.10), custom_call_target="tpu_custom_call" | custom-call | bytes 6000000 | tf_op jit(solution)/shard_map/wo/pallas_call | solution.py:348
  122.6 0.0 all-to-all-done.3.refs_0_
  122.6 0.0 copy-start.1
  122.6 0.9 copy-done.1
  123.5 2.5 %final.1 = (bf16[128,1024]{1,0:T(8,128)(2,1)}, bf16[128,1024]{1,0:T(8,128)(2,1)}, bf16[128,1024]{1,0:T(8,128)(2,1)}, bf16[128,1024]{1,0:T(8,128)(2,1)}) custom-call(bf16[32,3,32,128]{3,2,1,0:T(8,128)(2,1)} %copy-done.1, bf16[128,1024]{1,0:T(8,128)(2,1)} %refs_1_.3, bf16[128,1024]{1,0:T(8,128)(2,1)} %refs_2_.4), custom_call_target="tpu_custom_call" | custom-call | bytes 6000000 | tf_op jit(solution)/shard_map/final/pallas_call | solution.py:348
  (1 shorter events, 0.0 us)
Async XLA Ops:
  3.3 9.5 %copy-start.11 = (bf16[512,128]{1,0:T(8,128)(2,1)S(1)}, bf16[512,128]{1,0:T(8,128)(2,1)}, u32[]{:S(2)}) copy-start(bf16[512,128]{1,0:T(8,128)(2,1)} %get-tuple-element.43) | copy-start | bytes 393220
  3.3 32.5 %copy-start.9 = (bf16[512,128]{1,0:T(8,128)(2,1)S(1)}, bf16[512,128]{1,0:T(8,128)(2,1)}, u32[]{:S(2)}) copy-start(bf16[512,128]{1,0:T(8,128)(2,1)} %get-tuple-element.47) | copy-start | bytes 393220
  3.3 29.3 %all-to-all-start = ((bf16[32,5,32,128]{3,2,1,0:T(8,128)(2,1)}), bf16[32,5,32,128]{3,2,1,0:T(8,128)(2,1)S(1)}, u32[]{:S(2)}, u32[]{:S(2)}) async-start(bf16[32,5,32,128]{3,2,1,0:T(8,128)(2,1)} %get-tuple-element.42), calls=%async_computation | async-start | bytes 2621440 | tf_op jit(solution)/shard_map/to_channels/all_to_all | solution.py:376
  12.8 18.9 %collective-permute-start = (bf16[512,128]{1,0:T(8,128)(2,1)S(1)}, bf16[512,128]{1,0:T(8,128)(2,1)S(1)}, u32[]{:S(2)}, u32[]{:S(2)}) collective-permute-start(bf16[512,128]{1,0:T(8,128)(2,1)S(1)} %copy-done.11), channel_id=1, source_target_pairs={{0,64},{64,0},{1,65},{65,1},{2,66},{66,2},{3,67},{67,3},{4,68},{68... | collective-permute-start | bytes 393224 | tf_op jit(solution)/shard_map/gather_w/ppermute | solution.py:372
  32.6 1.1 copy-start
  33.7 22.1 %copy-start.2 = (bf16[32,2,32,128]{3,2,1,0:T(8,128)(2,1)}, bf16[32,2,32,128]{3,2,1,0:T(8,128)(2,1)S(1)}, u32[]{:S(2)}) copy-start(bf16[32,2,32,128]{3,2,1,0:T(8,128)(2,1)S(1)} %slice.3.refs_0_) | copy-start | bytes 1572868
  33.7 15.7 %collective-permute-start.1 = (bf16[32,2,32,128]{3,2,1,0:T(8,128)(2,1)S(1)}, bf16[32,2,32,128]{3,2,1,0:T(8,128)(2,1)}, u32[]{:S(2)}, u32[]{:S(2)}) collective-permute-start(bf16[32,2,32,128]{3,2,1,0:T(8,128)(2,1)S(1)} %slice.3.refs_0_), channel_id=1, source_target_pairs={{0,66},{2,64},{64,2},{66,0},{1,67},{3,65},{65,3},{67,1},{4,70},{6,... | collective-permute-start | bytes 1572872 | tf_op jit(solution)/shard_map/gather_d/ppermute | solution.py:372
  35.8 13.6 %copy-start.3 = (bf16[2,512,128]{2,1,0:T(8,128)(2,1)}, bf16[2,512,128]{2,1,0:T(8,128)(2,1)S(1)}, u32[]{:S(2)}) copy-start(bf16[2,512,128]{2,1,0:T(8,128)(2,1)S(1)} %pad_maximum_fusion.refs_4_) | copy-start | bytes 786436
  35.8 13.0 %collective-permute-start.4 = (bf16[2,512,128]{2,1,0:T(8,128)(2,1)S(1)}, bf16[2,512,128]{2,1,0:T(8,128)(2,1)}, u32[]{:S(2)}, u32[]{:S(2)}) collective-permute-start(bf16[2,512,128]{2,1,0:T(8,128)(2,1)S(1)} %pad_maximum_fusion.refs_4_), channel_id=1, source_target_pairs={{0,48},{16,32},{32,16},{48,0},{1,49},{17,33},{33,17},{49,1},{2,50}... | collective-permute-start | bytes 786440 | tf_op jit(solution)/shard_map/gather_w/ppermute | solution.py:372
  38.3 10.5 %collective-permute-start.3 = (bf16[2,512,128]{2,1,0:T(8,128)(2,1)S(1)}, bf16[2,512,128]{2,1,0:T(8,128)(2,1)}, u32[]{:S(2)}, u32[]{:S(2)}) collective-permute-start(bf16[2,512,128]{2,1,0:T(8,128)(2,1)S(1)} %pad_maximum_fusion.refs_4_), channel_id=1, source_target_pairs={{0,32},{16,48},{32,0},{48,16},{1,33},{17,49},{33,1},{49,17},{2,34}... | collective-permute-start | bytes 786440 | tf_op jit(solution)/shard_map/gather_w/ppermute | solution.py:372
  39.3 10.1 %collective-permute-start.2 = (bf16[2,512,128]{2,1,0:T(8,128)(2,1)S(1)}, bf16[2,512,128]{2,1,0:T(8,128)(2,1)}, u32[]{:S(2)}, u32[]{:S(2)}) collective-permute-start(bf16[2,512,128]{2,1,0:T(8,128)(2,1)S(1)} %pad_maximum_fusion.refs_4_), channel_id=1, source_target_pairs={{0,16},{16,0},{32,48},{48,32},{1,17},{17,1},{33,49},{49,33},{2,18}... | collective-permute-start | bytes 786440 | tf_op jit(solution)/shard_map/gather_w/ppermute | solution.py:372
  49.4 22.1 %all-to-all-start.1 = ((bf16[16,8,32,128]{3,2,1,0:T(8,128)(2,1)}), bf16[16,8,32,128]{3,2,1,0:T(8,128)(2,1)}, u32[]{:S(2)}, u32[]{:S(2)}) async-start(bf16[16,8,32,128]{3,2,1,0:T(8,128)(2,1)} %bitcast.6), calls=%async_computation.1 | async-start | bytes 2097152 | tf_op jit(solution)/shard_map/gated/all_to_all | solution.py:376
  55.8 2.0 %collective-permute-start.5 = (bf16[32,2,32,128]{3,2,1,0:T(8,128)(2,1)S(1)}, bf16[32,2,32,128]{3,2,1,0:T(8,128)(2,1)S(1)}, u32[]{:S(2)}, u32[]{:S(2)}) collective-permute-start(bf16[32,2,32,128]{3,2,1,0:T(8,128)(2,1)S(1)} %slice.3.refs_0_), channel_id=1, source_target_pairs={{0,1},{1,0},{2,3},{3,2},{4,5},{5,4},{6,7},{7,6},{8,9},{9,8},{10,11... | collective-permute-start | bytes 1572872 | tf_op jit(solution)/shard_map/gather_d/ppermute | solution.py:372
  55.9 3.0 %collective-permute-start.6 = (bf16[32,2,32,128]{3,2,1,0:T(8,128)(2,1)}, bf16[32,2,32,128]{3,2,1,0:T(8,128)(2,1)}, u32[]{:S(2)}, u32[]{:S(2)}) collective-permute-start(bf16[32,2,32,128]{3,2,1,0:T(8,128)(2,1)} %collective-permute-done.1.refs_1_), channel_id=1, source_target_pairs={{0,1},{1,0},{2,3},{3,2},{4,5},{5,4},{6,7},{7,6},{8,9},{9,8},{10,11... | collective-permute-start | bytes 1572872 | tf_op jit(solution)/shard_map/gather_d/ppermute | solution.py:372
  57.8 0.8 copy-start.7
  71.6 20.5 %all-to-all-start.2 = ((bf16[16,8,32,128]{3,2,1,0:T(8,128)(2,1)}), bf16[16,8,32,128]{3,2,1,0:T(8,128)(2,1)}, u32[]{:S(2)}, u32[]{:S(2)}) async-start(bf16[16,8,32,128]{3,2,1,0:T(8,128)(2,1)} %get-tuple-element.57), calls=%async_computation.2 | async-start | bytes 2097152 | tf_op jit(solution)/shard_map/grady/all_to_all | solution.py:376
  80.2 18.5 %collective-permute-start.7 = (bf16[2,512,128]{2,1,0:T(8,128)(2,1)}, bf16[2,512,128]{2,1,0:T(8,128)(2,1)S(1)}, u32[]{:S(2)}, u32[]{:S(2)}) collective-permute-start(bf16[2,512,128]{2,1,0:T(8,128)(2,1)} %get-tuple-element.61), channel_id=1, source_target_pairs={{0,16},{16,0},{32,48},{48,32},{1,17},{17,1},{33,49},{49,33},{2,18}... | collective-permute-start | bytes 786440 | tf_op jit(solution)/shard_map/wo/ppermute | solution.py:372
  82.1 18.2 %collective-permute-start.8 = (bf16[2,512,128]{2,1,0:T(8,128)(2,1)}, bf16[2,512,128]{2,1,0:T(8,128)(2,1)S(1)}, u32[]{:S(2)}, u32[]{:S(2)}) collective-permute-start(bf16[2,512,128]{2,1,0:T(8,128)(2,1)} %get-tuple-element.62), channel_id=1, source_target_pairs={{0,32},{16,48},{32,0},{48,16},{1,33},{17,49},{33,1},{49,17},{2,34}... | collective-permute-start | bytes 786440 | tf_op jit(solution)/shard_map/wo/ppermute | solution.py:372
  84.9 15.4 %collective-permute-start.9 = (bf16[2,512,128]{2,1,0:T(8,128)(2,1)}, bf16[2,512,128]{2,1,0:T(8,128)(2,1)S(1)}, u32[]{:S(2)}, u32[]{:S(2)}) collective-permute-start(bf16[2,512,128]{2,1,0:T(8,128)(2,1)} %get-tuple-element.63), channel_id=1, source_target_pairs={{0,48},{16,32},{32,16},{48,0},{1,49},{17,33},{33,17},{49,1},{2,50}... | collective-permute-start | bytes 786440 | tf_op jit(solution)/shard_map/wo/ppermute | solution.py:372
  98.8 1.5 %copy-start.4 = (bf16[2,512,128]{2,1,0:T(8,128)(2,1)}, bf16[2,512,128]{2,1,0:T(8,128)(2,1)S(1)}, u32[]{:S(2)}) copy-start(bf16[2,512,128]{2,1,0:T(8,128)(2,1)S(1)} %collective-permute-done.7.refs_1_) | copy-start | bytes 786436
  100.2 0.7 copy-start.5
  100.9 0.7 copy-start.6
  103.7 5.9 %copy-start.8 = (bf16[512,128]{1,0:T(8,128)(2,1)S(1)}, bf16[512,128]{1,0:T(8,128)(2,1)}, u32[]{:S(2)}) copy-start(bf16[512,128]{1,0:T(8,128)(2,1)} %wo.4) | copy-start | bytes 393220
  103.7 18.8 %all-to-all-start.3 = ((bf16[32,3,32,128]{3,2,1,0:T(8,128)(2,1)}), bf16[32,3,32,128]{3,2,1,0:T(8,128)(2,1)S(1)}, u32[]{:S(2)}, u32[]{:S(2)}) async-start(bf16[32,3,32,128]{3,2,1,0:T(8,128)(2,1)} %back.1), calls=%async_computation.3 | async-start | bytes 1572864 | tf_op jit(solution)/shard_map/back/all_to_all | solution.py:376
  109.6 10.0 %collective-permute-start.10 = (bf16[512,128]{1,0:T(8,128)(2,1)S(1)}, bf16[512,128]{1,0:T(8,128)(2,1)S(1)}, u32[]{:S(2)}, u32[]{:S(2)}) collective-permute-start(bf16[512,128]{1,0:T(8,128)(2,1)S(1)} %copy-done.8), channel_id=1, source_target_pairs={{0,64},{64,0},{1,65},{65,1},{2,66},{66,2},{3,67},{67,3},{4,68},{68... | collective-permute-start | bytes 393224 | tf_op jit(solution)/shard_map/wo/ppermute | solution.py:372
  119.6 0.7 copy-start.10
  122.6 0.9 copy-start.1

commit v2 on v1

--- a/solution.py
+++ b/solution.py
@@ -11,8 +11,7 @@
 
 BF16 = jnp.bfloat16
 F32 = jnp.float32
-HBM = pl.BlockSpec(memory_space=pltpu.HBM)
-PARAMS = pltpu.CompilerParams(vmem_limit_bytes=63 * 1024 * 1024)
+PARAMS = pltpu.CompilerParams(vmem_limit_bytes=16 * 1024 * 1024)
 
 M, N = 32, 128
 GROUP = 8
@@ -222,23 +221,31 @@
         emit(0, slice(None), 2, chans)
 
 
-def final_kernel(_, ins, outs, scratch, ready, emit):
-    in_ref, key_ref, value_ref = ins
+def final_kernel(where, ins, outs, scratch, ready, emit):
+    *got, key_ref, value_ref, wo_0, wo_1, wo_2, wo_3, take_ref = ins
+    wo_refs, wo_ref = (wo_0, wo_1, wo_2, wo_3), outs[4]
 
     def get(which):
-        return in_ref[:, which].astype(F32).reshape(M * 32, N).T
+        ready(which)
+        return got[which][...].astype(F32).reshape(M * 32, N).T
 
     def put(which, block):
         outs[which][...] = block.astype(BF16)
         emit(which)
 
-    ready(0)
     put(0, get(0))
-    put(3, get(2))
-    ready(1, 2)
-    back = get(1)
+    put(3, get(1))
+    back = get(2)
+    ready(3, 4)
     put(1, back * value_ref[...].astype(F32))
     put(2, back * key_ref[...].astype(F32))
+    ready(*range(5, 10))
+    total = wo_refs[0][...].astype(F32)
+    for s in range(1, 4):
+        total = total + wo_refs[s][...].astype(F32)
+    wo_ref[where[0]] = total
+    wo_ref[where[0] ^ 1] = take_ref[...].astype(F32)
+    emit(4)
 
 
 def grady_kernel(where, ins, outs, scratch, ready, emit):
@@ -269,14 +276,12 @@
     (gated_ref, d_ref), (all_s,) = ins, scratch
     ready(0, 1)
     lhs = jnp.concatenate([gated_ref[:, b].reshape(512, N) for b in range(8)], axis=1)
-    for xl in range(2):
-        for to in range(0, 4, 2):
-            rhs = jnp.concatenate(
-                [d_ref[xl * 4 + to + k].reshape(1024, 128) for k in range(2)], axis=1
-            )
-            part = dot(lhs, rhs)
-            for k in range(2):
-                all_s[to + k, xl] = part[:, k * 128 : (k + 1) * 128].astype(BF16)
+    for j in range(0, 8, 2):
+        rhs = jnp.concatenate([d_ref[j + k].reshape(1024, 128) for k in range(2)], axis=1)
+        part = dot(lhs, rhs)
+        for k in range(2):
+            column = j + k
+            all_s[column % 4, column // 4] = part[:, k * 128 : (k + 1) * 128].astype(BF16)
     for s in range(4):
         outs[s][...] = all_s[where[1] ^ s]
         emit(s)
@@ -284,52 +289,53 @@
 
 def give_kernel(where, ins, outs, scratch, ready, emit):
     ready(0, 1, 2, 3)
-    total = ins[0][where[0] ^ 1].astype(F32)
+    total = ins[0][...].astype(F32)
     for s in range(1, 4):
-        total = total + ins[s][where[0] ^ 1].astype(F32)
+        total = total + ins[s][...].astype(F32)
     outs[0][...] = total.astype(BF16)
     emit(0)
 
 
-def join_kernel(where, ins, outs, scratch, ready, emit):
-    ready(0, 1, 2, 3, 4)
-    total = ins[0][where[0]].astype(F32)
-    for s in range(1, 4):
-        total = total + ins[s][where[0]].astype(F32)
-    outs[0][where[0]] = total
-    outs[0][where[0] ^ 1] = ins[4][...].astype(F32)
-    emit(0)
-
-
-def call(kernel, ins, outs, scratch=(), parts={}, cost=2):
+def index(part, xl):
+    return {"xl": xl, "other": xl ^ 1}[part] if isinstance(part, str) else part
+
+
+def call(kernel, ins, outs, scratch=(), parts={}, homes="", cost=2):
     n_in, n_out = len(ins), len(outs)
+    in_homes, out_homes = homes[:n_in], homes[n_in:]
+    assert len(out_homes) == n_out
 
     def whole(*refs):
         xl, y, z, xh, co = (lax.axis_index(a) for a in ("xl", "y", "z", "xh", "co"))
         where = (xl, y, 2 * xh + co, z)
-        hbm_in, refs = refs[:n_in], refs[n_in:]
-        hbm_out, refs = refs[:n_out], refs[n_out:]
-        in_refs, refs = refs[:n_in], refs[n_in:]
-        out_refs, refs = refs[:n_out], refs[n_out:]
+        in_homes_refs, refs = list(refs[:n_in]), refs[n_in:]
+        out_homes_refs, refs = refs[:n_out], refs[n_out:]
+        in_copies, refs = refs[: in_homes.count("h")], refs[in_homes.count("h") :]
+        out_copies, refs = list(refs[: out_homes.count("h")]), refs[out_homes.count("h") :]
         (in_sem, out_sem), rest = refs[:2], refs[2:]
-        loads = [
-            pltpu.make_async_copy(
-                hbm_in[i].at[parts[i]] if i in parts else hbm_in[i], in_refs[i], in_sem.at[i]
-            )
-            for i in range(n_in)
+        in_refs, loads, stores = [], {}, []
+        for i, ref in enumerate(in_homes_refs):
+            if i in parts:
+                ref = ref.at[index(parts[i], xl)]
+            if in_homes[i] == "h":
+                copy = in_copies[len(loads)]
+                loads[i] = pltpu.make_async_copy(ref, copy, in_sem.at[len(loads)])
+                loads[i].start()
+                ref = copy
+            in_refs.append(ref)
+        out_refs = [
+            out_copies.pop(0) if out_homes[j] == "h" else out_homes_refs[j] for j in range(n_out)
         ]
-        for load in loads:
-            load.start()
-        waited, stores = set(), []
 
         def ready(*which):
             for i in which:
-                if i not in waited:
-                    waited.add(i)
-                    loads[i].wait()
+                if i in loads:
+                    loads.pop(i).wait()
 
         def emit(j, *index):
-            source, target = out_refs[j], hbm_out[j]
+            if out_homes[j] == "v":
+                return
+            source, target = out_refs[j], out_homes_refs[j]
             if index:
                 source, target = source.at[index], target.at[index]
             stores.append(pltpu.make_async_copy(source, target, out_sem.at[len(stores)]))
@@ -341,23 +347,27 @@
             store.wait()
 
     shapes = [
-        jax.eval_shape(lambda x, i=i: x[parts[i]], a) if i in parts else a
+        jax.eval_shape(lambda x, i=i: x[index(parts[i], 0)], a) if i in parts else a
         for i, a in enumerate(ins)
     ]
-    buffers = [pltpu.VMEM(a.shape, a.dtype) for a in (*shapes, *outs)]
+    buffers = [
+        pltpu.VMEM(a.shape, a.dtype) for a, home in zip((*shapes, *outs), homes) if home == "h"
+    ]
+    spaces = {"v": pltpu.VMEM, "h": pltpu.HBM}
+    specs = [pl.BlockSpec(memory_space=spaces[home]) for home in homes]
     return pl.pallas_call(
         whole,
-        out_shape=list(outs),
-        in_specs=[HBM] * n_in,
-        out_specs=[HBM] * n_out,
+        out_shape=[spaces[home](a.shape, a.dtype) for a, home in zip(outs, out_homes)],
+        in_specs=specs[:n_in],
+        out_specs=specs[n_in:],
         scratch_shapes=buffers
-        + [pltpu.SemaphoreType.DMA((n_in,)), pltpu.SemaphoreType.DMA((16,))]
+        + [pltpu.SemaphoreType.DMA((max(n_in, 1),)), pltpu.SemaphoreType.DMA((16,))]
         + list(scratch),
         compiler_params=PARAMS,
         cost_estimate=pl.CostEstimate(
             flops=0, bytes_accessed=cost * 3_000_000, transcendentals=0
         ),
-    )(*ins)
+    )(*[pltpu.with_memory_space_constraint(a, spaces[home]) for a, home in zip(ins, in_homes)])
 
 
 def shape(*dims, dtype=BF16):
@@ -385,6 +395,7 @@
             (key_feat, value_feat, filt, query, skip.reshape(8, 128), w_out.reshape(2, 512, 128), dout),
             [shape(M, 5, 32, N)] + [shape(512, 128)] * 2 + [shape(32, N, dtype=F32)],
             [pltpu.VMEM((4, 32, N), F32)],
+            homes="hhhhhhh" + "hvvv",
             cost=3,
         )
     with jax.named_scope("to_channels"):
@@ -410,9 +421,10 @@
             ),
             (),
             {0: (slice(None), slice(0, 3))},
+            homes="vvvv" + "hhhh",
             cost=20,
         )
-    gated, d, w = lax.optimization_barrier((gated, d, w))
+    gated, w = lax.optimization_barrier((gated, w))
     with jax.named_scope("gated"):
         gated = exchange(gated.reshape(16, 8, 32, N), ("y", "z"))
     with jax.named_scope("gather_d"):
@@ -423,6 +435,7 @@
             (*d_pieces, *w),
             (shape(16, 8, 32, N), shape(8, 32, 32, 128)),
             [pltpu.VMEM((8, 512, 128), BF16)],
+            homes="hvvv" + "h" * 4 + "hh",
             cost=5,
         )
         part, gated = lax.optimization_barrier((part, gated))
@@ -433,6 +446,7 @@
             (gated, d_all),
             [shape(2, 512, 128)] * 4,
             [pltpu.VMEM((4, 2, 512, 128), BF16)],
+            homes="vh" + "vvvv",
             cost=5,
         )
         part, _ = lax.optimization_barrier((part, wo))
@@ -444,21 +458,28 @@
             [shape(M, 3, 32, N)],
             [pltpu.VMEM((M, 32, N), F32)],
             {1: (slice(None), 2)},
+            homes="hhhhhhvv" + "h",
             cost=7,
         )
     with jax.named_scope("wo"):
         sent, wo = lax.optimization_barrier((sent, wo))
-        (give,) = call(give_kernel, wo, [shape(512, 128)])
+        (give,) = call(
+            give_kernel, wo, [shape(512, 128)], (), {i: "other" for i in range(4)}, "vvvvv"
+        )
         sent, give = lax.optimization_barrier((sent, give))
         take = flip(give, "xl", (2,), 1)
     with jax.named_scope("back"):
         got = exchange(sent, CONTEXT)
-    with jax.named_scope("wo"):
-        (wo_grad,) = call(
-            join_kernel, (*wo, take), [shape(2, 512, 128, dtype=F32)]
-        )
     with jax.named_scope("final"):
-        grads = call(final_kernel, (got, key_feat, value_feat), [shape(128, 1024)] * 4)
+        *grads, wo_grad = call(
+            final_kernel,
+            (got, got, got, key_feat, value_feat, *wo, take),
+            [shape(128, 1024)] * 4 + [shape(2, 512, 128, dtype=F32)],
+            (),
+            {0: (slice(None), 0), 1: (slice(None), 2), 2: (slice(None), 1)}
+            | {i: "xl" for i in range(5, 9)},
+            "vvv" + "h" * 7 + "h" * 5,
+        )
     return (*grads, wo_grad.reshape(1024, 128))
 
 

time: 127 us -> 120 us (0.945)
  Pallas kernels: 30.7 us -> 23.8 us
  local copies, waits for them, and re-layouts: 4.89 us -> 1.62 us
  waiting for transfers between devices: 48 us -> 51.2 us
    pallas_call x8 -> x7, Pallas kernels: 30.7 us -> 23.8 us  [call(): pl.pallas_call(whole, out_shape=[spaces[home](a.shape, a.dtype) for a, ho...]
    all_to_all x4, waiting for transfers between devices: 16.4 us -> 20.7 us  [exchange(): return lax.all_to_all(value, axes, 0, 0)]
    unnamed x24 -> x26, local copies, waits for them, and re-layouts: 4.83 us -> 0.76 us
  transfers between devices with their start and end apart: 15 -> 15, of which waited for: 10 -> 12; matrix products, arithmetic and copies ran while one was open for 0% -> 1% of each run, Pallas kernels for 19% -> 15%
where the time goes in v2:
time: 120 us; the launch traced here: 119 us
  waiting for transfers between devices  51.2 us (43%)
  starting transfers between devices  41.3 us (34%)
  Pallas kernels  23.8 us (20%)
  local copies, waits for them, and re-layouts  1.62 us (1%)
    ppermute x11, waiting for transfers between devices, flip(): return lax.ppermute(value, axes, [(i, i ^ by) for i in range(total)])  30.5 us
    all_to_all x4, starting transfers between devices, exchange(): return lax.all_to_all(value, axes, 0, 0)  26 us
    pallas_call x7, Pallas kernels, call(): pl.pallas_call(whole, out_shape=[spaces[home](a.shape, a.dtype) for a, ho...  23.8 us
    all_to_all x4, waiting for transfers between devices, exchange(): return lax.all_to_all(value, axes, 0, 0)  20.7 us
    ppermute x11, starting transfers between devices, flip(): return lax.ppermute(value, axes, [(i, i ^ by) for i in range(total)])  15.3 us
  transfers between devices with their start and end apart: 15, of which 12 were waited for; matrix products, arithmetic and copies ran while one was open for 1% of the time, Pallas kernels for 15%

profile of v2, /device:TPU:0, one launch (start us, length us, event | category | flops | bytes accessed | tf_op | source)
XLA Modules:
  0.0 119.0 jit_solution(10175398821366892353)
XLA Ops:
  0.6 2.6 %prepare.1 = (bf16[32,5,32,128]{3,2,1,0:T(8,128)(2,1)}, bf16[512,128]{1,0:T(8,128)(2,1)S(1)}, bf16[512,128]{1,0:T(8,128)(2,1)S(1)}, f32[32,128]{1,0:T(8,128)S(1)}) custom-call(bf16[128,1024]{1,0:T(8,128)(2,1)} %refs_3_.4, bf16[128,1024]{1,0:T(8,128)(2,1)} %refs_4_.1, bf16[128,1024]{1,0:T(8,128)(2,1)} %refs_2_.2, bf16[128,1024]{1,0:T(8,128)(2,1)} %refs_3_.3, ...), custom_call_target="tpu_custom_call" | custom-call | bytes 9000000 | tf_op jit(solution)/shard_map/prepare/pallas_call | solution.py:358
  3.2 0.0 copy-start.7
  3.2 0.0 copy-start.1
  3.2 0.0 copy-start.6
  3.3 9.5 %all-to-all-start = ((bf16[32,5,32,128]{3,2,1,0:T(8,128)(2,1)}), bf16[32,5,32,128]{3,2,1,0:T(8,128)(2,1)S(1)}, u32[]{:S(2)}, u32[]{:S(2)}) async-start(bf16[32,5,32,128]{3,2,1,0:T(8,128)(2,1)} %get-tuple-element.41), calls=%async_computation | async-start | bytes 2621440 | tf_op jit(solution)/shard_map/to_channels/all_to_all | solution.py:386
  12.8 1.9 %collective-permute-start = (bf16[512,128]{1,0:T(8,128)(2,1)S(1)}, bf16[512,128]{1,0:T(8,128)(2,1)S(1)}, u32[]{:S(2)}, u32[]{:S(2)}) collective-permute-start(bf16[512,128]{1,0:T(8,128)(2,1)S(1)} %get-tuple-element.42), channel_id=1, source_target_pairs={{0,64},{64,0},{1,65},{65,1},{2,66},{66,2},{3,67},{67,3},{4,68},{68... | collective-permute-start | bytes 393224 | tf_op jit(solution)/shard_map/gather_w/ppermute | solution.py:382
  14.6 17.0 %collective-permute-done = bf16[512,128]{1,0:T(8,128)(2,1)S(1)} collective-permute-done((bf16[512,128]{1,0:T(8,128)(2,1)S(1)}, bf16[512,128]{1,0:T(8,128)(2,1)S(1)}, u32[]{:S(2)}, u32[]{:S(2)}) %collective-permute-start) | collective-permute-done | bytes 131104 | tf_op jit(solution)/shard_map/gather_w/ppermute | solution.py:382
  31.7 0.9 all-to-all-done.refs_0_.refs_1_
  32.5 0.0 copy-start
  32.6 0.0 copy-start.8
  32.6 2.7 %collective-permute-start.6 = (bf16[2,512,128]{2,1,0:T(8,128)(2,1)S(1)}, bf16[2,512,128]{2,1,0:T(8,128)(2,1)S(1)}, u32[]{:S(2)}, u32[]{:S(2)}) collective-permute-start(bf16[2,512,128]{2,1,0:T(8,128)(2,1)S(1)} %pad_maximum_fusion.refs_4_), channel_id=1, source_target_pairs={{0,48},{16,32},{32,16},{48,0},{1,49},{17,33},{33,17},{49,1},{2,50}... | collective-permute-start | bytes 786440 | tf_op jit(solution)/shard_map/gather_w/ppermute | solution.py:382
  35.3 0.1 collective-permute-start.5
  35.3 1.4 %collective-permute-start.4 = (bf16[2,512,128]{2,1,0:T(8,128)(2,1)S(1)}, bf16[2,512,128]{2,1,0:T(8,128)(2,1)S(1)}, u32[]{:S(2)}, u32[]{:S(2)}) collective-permute-start(bf16[2,512,128]{2,1,0:T(8,128)(2,1)S(1)} %pad_maximum_fusion.refs_4_), channel_id=1, source_target_pairs={{0,16},{16,0},{32,48},{48,32},{1,17},{17,1},{33,49},{49,33},{2,18}... | collective-permute-start | bytes 786440 | tf_op jit(solution)/shard_map/gather_w/ppermute | solution.py:382
  36.8 0.9 slice.3.refs_0_
  37.6 2.0 %collective-permute-start.1 = (bf16[32,2,32,128]{3,2,1,0:T(8,128)(2,1)}, bf16[32,2,32,128]{3,2,1,0:T(8,128)(2,1)S(1)}, u32[]{:S(2)}, u32[]{:S(2)}) collective-permute-start(bf16[32,2,32,128]{3,2,1,0:T(8,128)(2,1)} %slice.3.refs_0_), channel_id=1, source_target_pairs={{0,66},{2,64},{64,2},{66,0},{1,67},{3,65},{65,3},{67,1},{4,70},{6,... | collective-permute-start | bytes 1572872 | tf_op jit(solution)/shard_map/gather_d/ppermute | solution.py:382
  39.6 0.0 copy-done.7
  39.6 0.0 copy-done.1
  39.6 0.0 copy-done.6
  39.6 4.6 %conv.1 = (bf16[32,32,128]{2,1,0:T(8,128)(2,1)}, bf16[4,4,8,32,128]{4,3,2,1,0:T(8,128)(2,1)}, f32[4,256,256]{2,1,0:T(8,128)}, f32[4,256,256]{2,1,0:T(8,128)}) custom-call(bf16[32,5,32,128]{3,2,1,0:T(8,128)(2,1)S(1)} %all-to-all-done.refs_0_.refs_1_, f32[32,128]{1,0:T(8,128)S(1)} %get-tuple-element.44.refs_1_.refs_3_, bf16[3072,256]{1,0:T(8,128)(2,1)S(1)} %copy-done.1, ...), custom_call_target="tpu_custom_call" | custom-call | bytes 60000000 | tf_op jit(solution)/shard_map/conv/pallas_call | solution.py:358
  44.3 0.0 copy-done
  44.3 0.0 copy-done.8
  44.3 0.7 collective-permute-done.6.refs_7_
  44.9 0.0 copy-start.9
  44.9 0.6 collective-permute-done.5.refs_6_
  45.5 0.0 copy-start.10
  45.5 0.6 collective-permute-done.4.refs_5_
  46.1 0.0 copy-done.9
  46.1 0.0 copy-start.11
  46.1 0.1 copy-done.10
  46.2 0.6 copy-done.11
  46.8 6.8 %all-to-all-start.1 = ((bf16[16,8,32,128]{3,2,1,0:T(8,128)(2,1)}), bf16[16,8,32,128]{3,2,1,0:T(8,128)(2,1)S(1)}, u32[]{:S(2)}, u32[]{:S(2)}) async-start(bf16[16,8,32,128]{3,2,1,0:T(8,128)(2,1)} %bitcast.7), calls=%async_computation.1 | async-start | bytes 2097152 | tf_op jit(solution)/shard_map/gated/all_to_all | solution.py:386
  53.6 0.1 collective-permute-start.2
  53.7 0.0 collective-permute-done.1.refs_1_
  53.7 0.5 collective-permute-start.3
  54.2 1.6 %collective-permute-done.2.refs_2_ = bf16[32,2,32,128]{3,2,1,0:T(8,128)(2,1)S(1)} collective-permute-done((bf16[32,2,32,128]{3,2,1,0:T(8,128)(2,1)}, bf16[32,2,32,128]{3,2,1,0:T(8,128)(2,1)S(1)}, u32[]{:S(2)}, u32[]{:S(2)}) %collective-permute-start.2) | collective-permute-done | bytes 524320 | tf_op jit(solution)/shard_map/gather_d/ppermute | solution.py:382
  55.8 0.5 collective-permute-done.3.refs_3_
  56.3 3.7 %grady.1 = (bf16[16,8,32,128]{3,2,1,0:T(8,128)(2,1)}, bf16[8,32,32,128]{3,2,1,0:T(8,128)(2,1)}) custom-call(bf16[32,2,32,128]{3,2,1,0:T(8,128)(2,1)} %slice.3.refs_0_, bf16[32,2,32,128]{3,2,1,0:T(8,128)(2,1)S(1)} %collective-permute-done.1.refs_1_, bf16[32,2,32,128]{3,2,1,0:T(8,128)(2,1)S(1)} %collective-permute-done.2.refs_2_, ...), custom_call_target="tpu_custom_call" | custom-call | bytes 15000000 | tf_op jit(solution)/shard_map/grady/pallas_call | solution.py:358
  60.1 10.3 %all-to-all-done.1.refs_0_ = bf16[16,8,32,128]{3,2,1,0:T(8,128)(2,1)S(1)} async-done(((bf16[16,8,32,128]{3,2,1,0:T(8,128)(2,1)}), bf16[16,8,32,128]{3,2,1,0:T(8,128)(2,1)S(1)}, u32[]{:S(2)}, u32[]{:S(2)}) %all-to-all-start.1) | async-done | bytes 1048608 | tf_op jit(solution)/shard_map/gated/all_to_all | solution.py:386
  70.3 4.4 %all-to-all-start.2 = ((bf16[16,8,32,128]{3,2,1,0:T(8,128)(2,1)}), bf16[16,8,32,128]{3,2,1,0:T(8,128)(2,1)}, u32[]{:S(2)}, u32[]{:S(2)}) async-start(bf16[16,8,32,128]{3,2,1,0:T(8,128)(2,1)} %get-tuple-element.54), calls=%async_computation.2 | async-start | bytes 2097152 | tf_op jit(solution)/shard_map/grady/all_to_all | solution.py:386
  74.7 3.9 %wo.2 = (bf16[2,512,128]{2,1,0:T(8,128)(2,1)S(1)}, bf16[2,512,128]{2,1,0:T(8,128)(2,1)}, bf16[2,512,128]{2,1,0:T(8,128)(2,1)}, bf16[2,512,128]{2,1,0:T(8,128)(2,1)}) custom-call(bf16[16,8,32,128]{3,2,1,0:T(8,128)(2,1)S(1)} %all-to-all-done.1.refs_0_, bf16[8,32,32,128]{3,2,1,0:T(8,128)(2,1)} %get-tuple-element.56.refs_1_), custom_call_target="tpu_custom_call" | custom-call | bytes 15000000 | tf_op jit(solution)/shard_map/wo/pallas_call | solution.py:358
  78.6 0.0 copy-start.2
  78.6 1.9 %collective-permute-start.7 = (bf16[2,512,128]{2,1,0:T(8,128)(2,1)}, bf16[2,512,128]{2,1,0:T(8,128)(2,1)S(1)}, u32[]{:S(2)}, u32[]{:S(2)}) collective-permute-start(bf16[2,512,128]{2,1,0:T(8,128)(2,1)} %get-tuple-element.58), channel_id=1, source_target_pairs={{0,16},{16,0},{32,48},{48,32},{1,17},{17,1},{33,49},{49,33},{2,18}... | collective-permute-start | bytes 786440 | tf_op jit(solution)/shard_map/wo/ppermute | solution.py:382
  80.6 2.8 %collective-permute-start.8 = (bf16[2,512,128]{2,1,0:T(8,128)(2,1)}, bf16[2,512,128]{2,1,0:T(8,128)(2,1)S(1)}, u32[]{:S(2)}, u32[]{:S(2)}) collective-permute-start(bf16[2,512,128]{2,1,0:T(8,128)(2,1)} %get-tuple-element.59), channel_id=1, source_target_pairs={{0,32},{16,48},{32,0},{48,16},{1,33},{17,49},{33,1},{49,17},{2,34}... | collective-permute-start | bytes 786440 | tf_op jit(solution)/shard_map/wo/ppermute | solution.py:382
  83.3 0.1 collective-permute-start.9
  83.4 7.5 %all-to-all-done.2.refs_0_ = bf16[16,8,32,128]{3,2,1,0:T(8,128)(2,1)} async-done(((bf16[16,8,32,128]{3,2,1,0:T(8,128)(2,1)}), bf16[16,8,32,128]{3,2,1,0:T(8,128)(2,1)}, u32[]{:S(2)}, u32[]{:S(2)}) %all-to-all-start.2) | async-done | bytes 1048608 | tf_op jit(solution)/shard_map/grady/all_to_all | solution.py:386
  90.9 6.1 %back.1 = bf16[32,3,32,128]{3,2,1,0:T(8,128)(2,1)} custom-call(bf16[16,8,32,128]{3,2,1,0:T(8,128)(2,1)} %all-to-all-done.2.refs_0_, bf16[32,5,32,128]{3,2,1,0:T(8,128)(2,1)} %copy-done, bf16[32,32,128]{2,1,0:T(8,128)(2,1)} %get-tuple-element.62.refs_2_, f32[32,128]{1,0:T(8,128)} %copy-done.7, f32[4,256,256]{2,1,0:T(8,128)} %get-tuple-element.63.refs_4_, ...), custom_call_target="tpu_custom_call" | custom-call | bytes 21000000 | tf_op jit(solution)/shard_map/back/pallas_call | solution.py:358
  97.0 0.0 collective-permute-done.7.refs_1_.refs_6_
  97.0 0.0 copy-start.3
  97.0 1.7 %collective-permute-done.8.refs_2_.refs_7_ = bf16[2,512,128]{2,1,0:T(8,128)(2,1)S(1)} collective-permute-done((bf16[2,512,128]{2,1,0:T(8,128)(2,1)}, bf16[2,512,128]{2,1,0:T(8,128)(2,1)S(1)}, u32[]{:S(2)}, u32[]{:S(2)}) %collective-permute-start.8) | collective-permute-done | bytes 262176 | tf_op jit(solution)/shard_map/wo/ppermute | solution.py:382
  98.8 0.0 copy-start.4
  98.8 0.0 collective-permute-done.9.refs_3_.refs_8_
  98.8 0.0 copy-done.2
  98.8 0.0 copy-start.5
  98.8 0.3 wo.3
  99.0 5.4 %all-to-all-start.3 = ((bf16[32,3,32,128]{3,2,1,0:T(8,128)(2,1)}), bf16[32,3,32,128]{3,2,1,0:T(8,128)(2,1)S(1)}, u32[]{:S(2)}, u32[]{:S(2)}) async-start(bf16[32,3,32,128]{3,2,1,0:T(8,128)(2,1)} %back.1), calls=%async_computation.3 | async-start | bytes 1572864 | tf_op jit(solution)/shard_map/back/all_to_all | solution.py:386
  104.5 1.9 %collective-permute-start.10 = (bf16[512,128]{1,0:T(8,128)(2,1)S(1)}, bf16[512,128]{1,0:T(8,128)(2,1)S(1)}, u32[]{:S(2)}, u32[]{:S(2)}) collective-permute-start(bf16[512,128]{1,0:T(8,128)(2,1)S(1)} %wo.3), channel_id=1, source_target_pairs={{0,64},{64,0},{1,65},{65,1},{2,66},{66,2},{3,67},{67,3},{4,68},{68... | collective-permute-start | bytes 393224 | tf_op jit(solution)/shard_map/wo/ppermute | solution.py:382
  106.3 7.8 %collective-permute-done.10.refs_9_ = bf16[512,128]{1,0:T(8,128)(2,1)S(1)} collective-permute-done((bf16[512,128]{1,0:T(8,128)(2,1)S(1)}, bf16[512,128]{1,0:T(8,128)(2,1)S(1)}, u32[]{:S(2)}, u32[]{:S(2)}) %collective-permute-start.10) | collective-permute-done | bytes 131104 | tf_op jit(solution)/shard_map/wo/ppermute | solution.py:382
  114.1 0.0 copy-start.12
  114.1 2.1 %all-to-all-done.3.refs_0_.refs_1_.refs_2_ = bf16[32,3,32,128]{3,2,1,0:T(8,128)(2,1)S(1)} async-done(((bf16[32,3,32,128]{3,2,1,0:T(8,128)(2,1)}), bf16[32,3,32,128]{3,2,1,0:T(8,128)(2,1)S(1)}, u32[]{:S(2)}, u32[]{:S(2)}) %all-to-all-start.3) | async-done | bytes 786464 | tf_op jit(solution)/shard_map/back/all_to_all | solution.py:386
  116.2 0.0 copy-done.3
  116.2 0.0 copy-done.4
  116.2 0.0 copy-done.5
  116.2 0.0 copy-done.12
  116.2 2.6 %final.1 = (bf16[128,1024]{1,0:T(8,128)(2,1)}, bf16[128,1024]{1,0:T(8,128)(2,1)}, bf16[128,1024]{1,0:T(8,128)(2,1)}, bf16[128,1024]{1,0:T(8,128)(2,1)}, f32[2,512,128]{2,1,0:T(8,128)}) custom-call(bf16[32,3,32,128]{3,2,1,0:T(8,128)(2,1)S(1)} %all-to-all-done.3.refs_0_.refs_1_.refs_2_, bf16[32,3,32,128]{3,2,1,0:T(8,128)(2,1)S(1)} %all-to-all-done.3.refs_0_.refs_1_.refs_2_, ...), custom_call_target="tpu_custom_call" | custom-call | bytes 6000000 | tf_op jit(solution)/shard_map/final/pallas_call | solution.py:358
  (1 shorter events, 0.0 us)
Async XLA Ops:
  3.2 36.4 %copy-start.7 = (f32[32,128]{1,0:T(8,128)}, f32[32,128]{1,0:T(8,128)S(1)}, u32[]{:S(2)}) copy-start(f32[32,128]{1,0:T(8,128)S(1)} %get-tuple-element.44.refs_1_.refs_3_) | copy-start | bytes 49156
  3.2 36.4 %copy-start.1 = (bf16[3072,256]{1,0:T(8,128)(2,1)S(1)}, bf16[3072,256]{1,0:T(8,128)(2,1)}, u32[]{:S(2)}) copy-start(bf16[3072,256]{1,0:T(8,128)(2,1)} %constant.4.clone.refs_2_.refs_6_) | copy-start | bytes 4718596
  3.2 36.4 %copy-start.6 = (f32[2,32,128]{2,1,0:T(8,128)S(1)}, f32[2,32,128]{2,1,0:T(8,128)}, u32[]{:S(2)}) copy-start(f32[2,32,128]{2,1,0:T(8,128)} %constant.5.clone.refs_3_.refs_7_) | copy-start | bytes 98308
  3.3 29.3 %all-to-all-start = ((bf16[32,5,32,128]{3,2,1,0:T(8,128)(2,1)}), bf16[32,5,32,128]{3,2,1,0:T(8,128)(2,1)S(1)}, u32[]{:S(2)}, u32[]{:S(2)}) async-start(bf16[32,5,32,128]{3,2,1,0:T(8,128)(2,1)} %get-tuple-element.41), calls=%async_computation | async-start | bytes 2621440 | tf_op jit(solution)/shard_map/to_channels/all_to_all | solution.py:386
  12.8 18.9 %collective-permute-start = (bf16[512,128]{1,0:T(8,128)(2,1)S(1)}, bf16[512,128]{1,0:T(8,128)(2,1)S(1)}, u32[]{:S(2)}, u32[]{:S(2)}) collective-permute-start(bf16[512,128]{1,0:T(8,128)(2,1)S(1)} %get-tuple-element.42), channel_id=1, source_target_pairs={{0,64},{64,0},{1,65},{65,1},{2,66},{66,2},{3,67},{67,3},{4,68},{68... | collective-permute-start | bytes 393224 | tf_op jit(solution)/shard_map/gather_w/ppermute | solution.py:382
  32.5 11.7 %copy-start = (bf16[32,5,32,128]{3,2,1,0:T(8,128)(2,1)}, bf16[32,5,32,128]{3,2,1,0:T(8,128)(2,1)S(1)}, u32[]{:S(2)}) copy-start(bf16[32,5,32,128]{3,2,1,0:T(8,128)(2,1)S(1)} %all-to-all-done.refs_0_.refs_1_) | copy-start | bytes 3932164
  32.6 11.7 %copy-start.8 = (bf16[2,512,128]{2,1,0:T(8,128)(2,1)}, bf16[2,512,128]{2,1,0:T(8,128)(2,1)S(1)}, u32[]{:S(2)}) copy-start(bf16[2,512,128]{2,1,0:T(8,128)(2,1)S(1)} %pad_maximum_fusion.refs_4_) | copy-start | bytes 786436
  32.6 12.4 %collective-permute-start.6 = (bf16[2,512,128]{2,1,0:T(8,128)(2,1)S(1)}, bf16[2,512,128]{2,1,0:T(8,128)(2,1)S(1)}, u32[]{:S(2)}, u32[]{:S(2)}) collective-permute-start(bf16[2,512,128]{2,1,0:T(8,128)(2,1)S(1)} %pad_maximum_fusion.refs_4_), channel_id=1, source_target_pairs={{0,48},{16,32},{32,16},{48,0},{1,49},{17,33},{33,17},{49,1},{2,50}... | collective-permute-start | bytes 786440 | tf_op jit(solution)/shard_map/gather_w/ppermute | solution.py:382
  35.3 10.2 %collective-permute-start.5 = (bf16[2,512,128]{2,1,0:T(8,128)(2,1)S(1)}, bf16[2,512,128]{2,1,0:T(8,128)(2,1)S(1)}, u32[]{:S(2)}, u32[]{:S(2)}) collective-permute-start(bf16[2,512,128]{2,1,0:T(8,128)(2,1)S(1)} %pad_maximum_fusion.refs_4_), channel_id=1, source_target_pairs={{0,32},{16,48},{32,0},{48,16},{1,33},{17,49},{33,1},{49,17},{2,34}... | collective-permute-start | bytes 786440 | tf_op jit(solution)/shard_map/gather_w/ppermute | solution.py:382
  35.3 10.8 %collective-permute-start.4 = (bf16[2,512,128]{2,1,0:T(8,128)(2,1)S(1)}, bf16[2,512,128]{2,1,0:T(8,128)(2,1)S(1)}, u32[]{:S(2)}, u32[]{:S(2)}) collective-permute-start(bf16[2,512,128]{2,1,0:T(8,128)(2,1)S(1)} %pad_maximum_fusion.refs_4_), channel_id=1, source_target_pairs={{0,16},{16,0},{32,48},{48,32},{1,17},{17,1},{33,49},{49,33},{2,18}... | collective-permute-start | bytes 786440 | tf_op jit(solution)/shard_map/gather_w/ppermute | solution.py:382
  37.6 16.1 %collective-permute-start.1 = (bf16[32,2,32,128]{3,2,1,0:T(8,128)(2,1)}, bf16[32,2,32,128]{3,2,1,0:T(8,128)(2,1)S(1)}, u32[]{:S(2)}, u32[]{:S(2)}) collective-permute-start(bf16[32,2,32,128]{3,2,1,0:T(8,128)(2,1)} %slice.3.refs_0_), channel_id=1, source_target_pairs={{0,66},{2,64},{64,2},{66,0},{1,67},{3,65},{65,3},{67,1},{4,70},{6,... | collective-permute-start | bytes 1572872 | tf_op jit(solution)/shard_map/gather_d/ppermute | solution.py:382
  44.9 1.2 copy-start.9
  45.5 0.7 copy-start.10
  46.1 0.7 copy-start.11
  46.8 23.5 %all-to-all-start.1 = ((bf16[16,8,32,128]{3,2,1,0:T(8,128)(2,1)}), bf16[16,8,32,128]{3,2,1,0:T(8,128)(2,1)S(1)}, u32[]{:S(2)}, u32[]{:S(2)}) async-start(bf16[16,8,32,128]{3,2,1,0:T(8,128)(2,1)} %bitcast.7), calls=%async_computation.1 | async-start | bytes 2097152 | tf_op jit(solution)/shard_map/gated/all_to_all | solution.py:386
  53.6 2.2 %collective-permute-start.2 = (bf16[32,2,32,128]{3,2,1,0:T(8,128)(2,1)}, bf16[32,2,32,128]{3,2,1,0:T(8,128)(2,1)S(1)}, u32[]{:S(2)}, u32[]{:S(2)}) collective-permute-start(bf16[32,2,32,128]{3,2,1,0:T(8,128)(2,1)} %slice.3.refs_0_), channel_id=1, source_target_pairs={{0,1},{1,0},{2,3},{3,2},{4,5},{5,4},{6,7},{7,6},{8,9},{9,8},{10,11... | collective-permute-start | bytes 1572872 | tf_op jit(solution)/shard_map/gather_d/ppermute | solution.py:382
  53.7 2.6 %collective-permute-start.3 = (bf16[32,2,32,128]{3,2,1,0:T(8,128)(2,1)S(1)}, bf16[32,2,32,128]{3,2,1,0:T(8,128)(2,1)S(1)}, u32[]{:S(2)}, u32[]{:S(2)}) collective-permute-start(bf16[32,2,32,128]{3,2,1,0:T(8,128)(2,1)S(1)} %collective-permute-done.1.refs_1_), channel_id=1, source_target_pairs={{0,1},{1,0},{2,3},{3,2},{4,5},{5,4},{6,7},{7,6},{8,9},{9,8},{10,11... | collective-permute-start | bytes 1572872 | tf_op jit(solution)/shard_map/gather_d/ppermute | solution.py:382
  70.3 20.6 %all-to-all-start.2 = ((bf16[16,8,32,128]{3,2,1,0:T(8,128)(2,1)}), bf16[16,8,32,128]{3,2,1,0:T(8,128)(2,1)}, u32[]{:S(2)}, u32[]{:S(2)}) async-start(bf16[16,8,32,128]{3,2,1,0:T(8,128)(2,1)} %get-tuple-element.54), calls=%async_computation.2 | async-start | bytes 2097152 | tf_op jit(solution)/shard_map/grady/all_to_all | solution.py:386
  78.6 20.1 %copy-start.2 = (bf16[2,512,128]{2,1,0:T(8,128)(2,1)}, bf16[2,512,128]{2,1,0:T(8,128)(2,1)S(1)}, u32[]{:S(2)}) copy-start(bf16[2,512,128]{2,1,0:T(8,128)(2,1)S(1)} %get-tuple-element.66.refs_0_.refs_5_) | copy-start | bytes 786436
  78.6 18.4 %collective-permute-start.7 = (bf16[2,512,128]{2,1,0:T(8,128)(2,1)}, bf16[2,512,128]{2,1,0:T(8,128)(2,1)S(1)}, u32[]{:S(2)}, u32[]{:S(2)}) collective-permute-start(bf16[2,512,128]{2,1,0:T(8,128)(2,1)} %get-tuple-element.58), channel_id=1, source_target_pairs={{0,16},{16,0},{32,48},{48,32},{1,17},{17,1},{33,49},{49,33},{2,18}... | collective-permute-start | bytes 786440 | tf_op jit(solution)/shard_map/wo/ppermute | solution.py:382
  80.6 18.2 %collective-permute-start.8 = (bf16[2,512,128]{2,1,0:T(8,128)(2,1)}, bf16[2,512,128]{2,1,0:T(8,128)(2,1)S(1)}, u32[]{:S(2)}, u32[]{:S(2)}) collective-permute-start(bf16[2,512,128]{2,1,0:T(8,128)(2,1)} %get-tuple-element.59), channel_id=1, source_target_pairs={{0,32},{16,48},{32,0},{48,16},{1,33},{17,49},{33,1},{49,17},{2,34}... | collective-permute-start | bytes 786440 | tf_op jit(solution)/shard_map/wo/ppermute | solution.py:382
  83.3 15.4 %collective-permute-start.9 = (bf16[2,512,128]{2,1,0:T(8,128)(2,1)}, bf16[2,512,128]{2,1,0:T(8,128)(2,1)S(1)}, u32[]{:S(2)}, u32[]{:S(2)}) collective-permute-start(bf16[2,512,128]{2,1,0:T(8,128)(2,1)} %get-tuple-element.60), channel_id=1, source_target_pairs={{0,48},{16,32},{32,16},{48,0},{1,49},{17,33},{33,17},{49,1},{2,50}... | collective-permute-start | bytes 786440 | tf_op jit(solution)/shard_map/wo/ppermute | solution.py:382
  97.0 19.2 %copy-start.3 = (bf16[2,512,128]{2,1,0:T(8,128)(2,1)}, bf16[2,512,128]{2,1,0:T(8,128)(2,1)S(1)}, u32[]{:S(2)}) copy-start(bf16[2,512,128]{2,1,0:T(8,128)(2,1)S(1)} %collective-permute-done.7.refs_1_.refs_6_) | copy-start | bytes 786436
  98.8 17.5 %copy-start.4 = (bf16[2,512,128]{2,1,0:T(8,128)(2,1)}, bf16[2,512,128]{2,1,0:T(8,128)(2,1)S(1)}, u32[]{:S(2)}) copy-start(bf16[2,512,128]{2,1,0:T(8,128)(2,1)S(1)} %collective-permute-done.8.refs_2_.refs_7_) | copy-start | bytes 786436
  98.8 17.5 %copy-start.5 = (bf16[2,512,128]{2,1,0:T(8,128)(2,1)}, bf16[2,512,128]{2,1,0:T(8,128)(2,1)S(1)}, u32[]{:S(2)}) copy-start(bf16[2,512,128]{2,1,0:T(8,128)(2,1)S(1)} %collective-permute-done.9.refs_3_.refs_8_) | copy-start | bytes 786436
  99.0 17.2 %all-to-all-start.3 = ((bf16[32,3,32,128]{3,2,1,0:T(8,128)(2,1)}), bf16[32,3,32,128]{3,2,1,0:T(8,128)(2,1)S(1)}, u32[]{:S(2)}, u32[]{:S(2)}) async-start(bf16[32,3,32,128]{3,2,1,0:T(8,128)(2,1)} %back.1), calls=%async_computation.3 | async-start | bytes 1572864 | tf_op jit(solution)/shard_map/back/all_to_all | solution.py:386
  104.5 9.6 %collective-permute-start.10 = (bf16[512,128]{1,0:T(8,128)(2,1)S(1)}, bf16[512,128]{1,0:T(8,128)(2,1)S(1)}, u32[]{:S(2)}, u32[]{:S(2)}) collective-permute-start(bf16[512,128]{1,0:T(8,128)(2,1)S(1)} %wo.3), channel_id=1, source_target_pairs={{0,64},{64,0},{1,65},{65,1},{2,66},{66,2},{3,67},{67,3},{4,68},{68... | collective-permute-start | bytes 393224 | tf_op jit(solution)/shard_map/wo/ppermute | solution.py:382
  114.1 2.1 %copy-start.12 = (bf16[512,128]{1,0:T(8,128)(2,1)}, bf16[512,128]{1,0:T(8,128)(2,1)S(1)}, u32[]{:S(2)}) copy-start(bf16[512,128]{1,0:T(8,128)(2,1)S(1)} %collective-permute-done.10.refs_9_) | copy-start | bytes 393220

commit v3 on v2

--- a/solution.py
+++ b/solution.py
@@ -117,16 +117,16 @@
     xl, y, z = where[0], where[1], where[3]
 
     def put(which, block):
-        outs[0][:, which] = block.T.reshape(M, 32, N).astype(BF16)
+        outs[0][:, which] = block.T.reshape(M, 32, N)
         emit(0, slice(None), which)
 
     ready(0, 1)
     signal = key_ref[...].astype(F32) * value_ref[...].astype(F32)
-    put(0, signal.astype(BF16).astype(F32))
+    put(0, signal.astype(BF16))
     ready(2)
-    put(1, filt_ref[...].astype(F32))
+    put(1, filt_ref[...])
     ready(3)
-    put(2, query_ref[...].astype(F32))
+    put(2, query_ref[...])
     ready(6)
     for to_y in range(4):
         for to_z in range(4):
@@ -207,18 +207,16 @@
     emit(0, slice(None), 0)
     gate = gate_s[...]
     ready(*range(3, 8))
-    for pair in range(2):
-        groups = (2 * pair, 2 * pair + 1)
-        chans = slice(16 * pair, 16 * pair + 16)
-        spectra = forward([rows_of(gate, g) for g in groups], tabs)
-        specs = [times(fil_ref[g], s, True) for g, s in zip(groups, spectra)]
-        specs += [times(sig_ref[g], s, True) for g, s in zip(groups, spectra)]
-        result = inverse(specs, tabs)
-        back = pair_of(*result[:2]) + skip_ref[chans, :][None] * gate[:, chans, :]
-        out_ref[:, 1, chans, :] = back.astype(BF16)
-        emit(0, slice(None), 1, chans)
-        out_ref[:, 2, chans, :] = pair_of(*result[2:]).astype(BF16)
-        emit(0, slice(None), 2, chans)
+    spectra = forward([rows_of(gate, g) for g in range(4)], tabs)
+    for which, other in ((1, fil_ref), (2, sig_ref)):
+        result = inverse([times(other[g], s, True) for g, s in enumerate(spectra)], tabs)
+        for pair in range(2):
+            chans = slice(16 * pair, 16 * pair + 16)
+            total = pair_of(*result[2 * pair : 2 * pair + 2])
+            if which == 1:
+                total = total + skip_ref[chans, :][None] * gate[:, chans, :]
+            out_ref[:, which, chans, :] = total.astype(BF16)
+        emit(0, slice(None), which)
 
 
 def final_kernel(where, ins, outs, scratch, ready, emit):
@@ -227,7 +225,7 @@
 
     def get(which):
         ready(which)
-        return got[which][...].astype(F32).reshape(M * 32, N).T
+        return got[which][...].reshape(M * 32, N).T
 
     def put(which, block):
         outs[which][...] = block.astype(BF16)
@@ -235,10 +233,6 @@
 
     put(0, get(0))
     put(3, get(1))
-    back = get(2)
-    ready(3, 4)
-    put(1, back * value_ref[...].astype(F32))
-    put(2, back * key_ref[...].astype(F32))
     ready(*range(5, 10))
     total = wo_refs[0][...].astype(F32)
     for s in range(1, 4):
@@ -246,6 +240,10 @@
     wo_ref[where[0]] = total
     wo_ref[where[0] ^ 1] = take_ref[...].astype(F32)
     emit(4)
+    back = get(2).astype(F32)
+    ready(3, 4)
+    put(1, back * value_ref[...].astype(F32))
+    put(2, back * key_ref[...].astype(F32))
 
 
 def grady_kernel(where, ins, outs, scratch, ready, emit):

time: 120 us -> 120 us (level)
  no operation moved by 1% of the time
where the time goes in v3:
time: 120 us; the launch traced here: 119 us
  waiting for transfers between devices  51.4 us (43%)
  starting transfers between devices  41.3 us (34%)
  Pallas kernels  23.8 us (20%)
  local copies, waits for them, and re-layouts  1.62 us (1%)
    ppermute x11, waiting for transfers between devices, flip(): return lax.ppermute(value, axes, [(i, i ^ by) for i in range(total)])  30.7 us
    all_to_all x4, starting transfers between devices, exchange(): return lax.all_to_all(value, axes, 0, 0)  26 us
    pallas_call x7, Pallas kernels, call(): pl.pallas_call(whole, out_shape=[spaces[home](a.shape, a.dtype) for a, ho...  23.8 us
    all_to_all x4, waiting for transfers between devices, exchange(): return lax.all_to_all(value, axes, 0, 0)  20.7 us
    ppermute x11, starting transfers between devices, flip(): return lax.ppermute(value, axes, [(i, i ^ by) for i in range(total)])  15.3 us
  transfers between devices with their start and end apart: 15, of which 12 were waited for; matrix products, arithmetic and copies ran while one was open for 1% of the time, Pallas kernels for 15%

profile of v3, /device:TPU:0, one launch (start us, length us, event | category | flops | bytes accessed | tf_op | source)
XLA Modules:
  0.0 119.1 jit_solution(10244410165343414657)
XLA Ops:
  0.6 2.5 %prepare.1 = (bf16[32,5,32,128]{3,2,1,0:T(8,128)(2,1)}, bf16[512,128]{1,0:T(8,128)(2,1)S(1)}, bf16[512,128]{1,0:T(8,128)(2,1)S(1)}, f32[32,128]{1,0:T(8,128)S(1)}) custom-call(bf16[128,1024]{1,0:T(8,128)(2,1)} %refs_3_.4, bf16[128,1024]{1,0:T(8,128)(2,1)} %refs_4_.1, bf16[128,1024]{1,0:T(8,128)(2,1)} %refs_2_.2, bf16[128,1024]{1,0:T(8,128)(2,1)} %refs_3_.3, ...), custom_call_target="tpu_custom_call" | custom-call | bytes 9000000 | tf_op jit(solution)/shard_map/prepare/pallas_call | solution.py:356
  3.2 0.0 copy-start.7
  3.2 0.0 copy-start.1
  3.2 0.0 copy-start.6
  3.2 9.5 %all-to-all-start = ((bf16[32,5,32,128]{3,2,1,0:T(8,128)(2,1)}), bf16[32,5,32,128]{3,2,1,0:T(8,128)(2,1)S(1)}, u32[]{:S(2)}, u32[]{:S(2)}) async-start(bf16[32,5,32,128]{3,2,1,0:T(8,128)(2,1)} %get-tuple-element.41), calls=%async_computation | async-start | bytes 2621440 | tf_op jit(solution)/shard_map/to_channels/all_to_all | solution.py:384
  12.7 1.9 %collective-permute-start = (bf16[512,128]{1,0:T(8,128)(2,1)S(1)}, bf16[512,128]{1,0:T(8,128)(2,1)S(1)}, u32[]{:S(2)}, u32[]{:S(2)}) collective-permute-start(bf16[512,128]{1,0:T(8,128)(2,1)S(1)} %get-tuple-element.42), channel_id=1, source_target_pairs={{0,64},{64,0},{1,65},{65,1},{2,66},{66,2},{3,67},{67,3},{4,68},{68... | collective-permute-start | bytes 393224 | tf_op jit(solution)/shard_map/gather_w/ppermute | solution.py:380
  14.6 17.0 %collective-permute-done = bf16[512,128]{1,0:T(8,128)(2,1)S(1)} collective-permute-done((bf16[512,128]{1,0:T(8,128)(2,1)S(1)}, bf16[512,128]{1,0:T(8,128)(2,1)S(1)}, u32[]{:S(2)}, u32[]{:S(2)}) %collective-permute-start) | collective-permute-done | bytes 131104 | tf_op jit(solution)/shard_map/gather_w/ppermute | solution.py:380
  31.6 0.9 all-to-all-done.refs_0_.refs_1_
  32.5 0.0 copy-start
  32.5 0.0 copy-start.8
  32.5 2.7 %collective-permute-start.6 = (bf16[2,512,128]{2,1,0:T(8,128)(2,1)S(1)}, bf16[2,512,128]{2,1,0:T(8,128)(2,1)S(1)}, u32[]{:S(2)}, u32[]{:S(2)}) collective-permute-start(bf16[2,512,128]{2,1,0:T(8,128)(2,1)S(1)} %pad_maximum_fusion.refs_4_), channel_id=1, source_target_pairs={{0,48},{16,32},{32,16},{48,0},{1,49},{17,33},{33,17},{49,1},{2,50}... | collective-permute-start | bytes 786440 | tf_op jit(solution)/shard_map/gather_w/ppermute | solution.py:380
  35.2 0.1 collective-permute-start.5
  35.3 1.4 %collective-permute-start.4 = (bf16[2,512,128]{2,1,0:T(8,128)(2,1)S(1)}, bf16[2,512,128]{2,1,0:T(8,128)(2,1)S(1)}, u32[]{:S(2)}, u32[]{:S(2)}) collective-permute-start(bf16[2,512,128]{2,1,0:T(8,128)(2,1)S(1)} %pad_maximum_fusion.refs_4_), channel_id=1, source_target_pairs={{0,16},{16,0},{32,48},{48,32},{1,17},{17,1},{33,49},{49,33},{2,18}... | collective-permute-start | bytes 786440 | tf_op jit(solution)/shard_map/gather_w/ppermute | solution.py:380
  36.7 0.9 slice.3.refs_0_
  37.6 2.0 %collective-permute-start.1 = (bf16[32,2,32,128]{3,2,1,0:T(8,128)(2,1)}, bf16[32,2,32,128]{3,2,1,0:T(8,128)(2,1)S(1)}, u32[]{:S(2)}, u32[]{:S(2)}) collective-permute-start(bf16[32,2,32,128]{3,2,1,0:T(8,128)(2,1)} %slice.3.refs_0_), channel_id=1, source_target_pairs={{0,66},{2,64},{64,2},{66,0},{1,67},{3,65},{65,3},{67,1},{4,70},{6,... | collective-permute-start | bytes 1572872 | tf_op jit(solution)/shard_map/gather_d/ppermute | solution.py:380
  39.6 0.0 copy-done.7
  39.6 0.0 copy-done.1
  39.6 0.0 copy-done.6
  39.6 4.6 %conv.1 = (bf16[32,32,128]{2,1,0:T(8,128)(2,1)}, bf16[4,4,8,32,128]{4,3,2,1,0:T(8,128)(2,1)}, f32[4,256,256]{2,1,0:T(8,128)}, f32[4,256,256]{2,1,0:T(8,128)}) custom-call(bf16[32,5,32,128]{3,2,1,0:T(8,128)(2,1)S(1)} %all-to-all-done.refs_0_.refs_1_, f32[32,128]{1,0:T(8,128)S(1)} %get-tuple-element.44.refs_1_.refs_3_, bf16[3072,256]{1,0:T(8,128)(2,1)S(1)} %copy-done.1, ...), custom_call_target="tpu_custom_call" | custom-call | bytes 60000000 | tf_op jit(solution)/shard_map/conv/pallas_call | solution.py:356
  44.2 0.0 copy-done
  44.2 0.0 copy-done.8
  44.2 0.6 collective-permute-done.6.refs_7_
  44.9 0.0 copy-start.9
  44.9 0.6 collective-permute-done.5.refs_6_
  45.5 0.0 copy-start.10
  45.5 0.6 collective-permute-done.4.refs_5_
  46.1 0.0 copy-done.9
  46.1 0.0 copy-start.11
  46.1 0.1 copy-done.10
  46.2 0.6 copy-done.11
  46.8 6.8 %all-to-all-start.1 = ((bf16[16,8,32,128]{3,2,1,0:T(8,128)(2,1)}), bf16[16,8,32,128]{3,2,1,0:T(8,128)(2,1)S(1)}, u32[]{:S(2)}, u32[]{:S(2)}) async-start(bf16[16,8,32,128]{3,2,1,0:T(8,128)(2,1)} %bitcast.7), calls=%async_computation.1 | async-start | bytes 2097152 | tf_op jit(solution)/shard_map/gated/all_to_all | solution.py:384
  53.5 0.1 collective-permute-start.2
  53.6 0.0 collective-permute-done.1.refs_1_
  53.6 0.5 collective-permute-start.3
  54.1 1.6 %collective-permute-done.2.refs_2_ = bf16[32,2,32,128]{3,2,1,0:T(8,128)(2,1)S(1)} collective-permute-done((bf16[32,2,32,128]{3,2,1,0:T(8,128)(2,1)}, bf16[32,2,32,128]{3,2,1,0:T(8,128)(2,1)S(1)}, u32[]{:S(2)}, u32[]{:S(2)}) %collective-permute-start.2) | collective-permute-done | bytes 524320 | tf_op jit(solution)/shard_map/gather_d/ppermute | solution.py:380
  55.7 0.5 collective-permute-done.3.refs_3_
  56.3 3.7 %grady.1 = (bf16[16,8,32,128]{3,2,1,0:T(8,128)(2,1)}, bf16[8,32,32,128]{3,2,1,0:T(8,128)(2,1)}) custom-call(bf16[32,2,32,128]{3,2,1,0:T(8,128)(2,1)} %slice.3.refs_0_, bf16[32,2,32,128]{3,2,1,0:T(8,128)(2,1)S(1)} %collective-permute-done.1.refs_1_, bf16[32,2,32,128]{3,2,1,0:T(8,128)(2,1)S(1)} %collective-permute-done.2.refs_2_, ...), custom_call_target="tpu_custom_call" | custom-call | bytes 15000000 | tf_op jit(solution)/shard_map/grady/pallas_call | solution.py:356
  60.0 10.3 %all-to-all-done.1.refs_0_ = bf16[16,8,32,128]{3,2,1,0:T(8,128)(2,1)S(1)} async-done(((bf16[16,8,32,128]{3,2,1,0:T(8,128)(2,1)}), bf16[16,8,32,128]{3,2,1,0:T(8,128)(2,1)S(1)}, u32[]{:S(2)}, u32[]{:S(2)}) %all-to-all-start.1) | async-done | bytes 1048608 | tf_op jit(solution)/shard_map/gated/all_to_all | solution.py:384
  70.3 4.4 %all-to-all-start.2 = ((bf16[16,8,32,128]{3,2,1,0:T(8,128)(2,1)}), bf16[16,8,32,128]{3,2,1,0:T(8,128)(2,1)}, u32[]{:S(2)}, u32[]{:S(2)}) async-start(bf16[16,8,32,128]{3,2,1,0:T(8,128)(2,1)} %get-tuple-element.54), calls=%async_computation.2 | async-start | bytes 2097152 | tf_op jit(solution)/shard_map/grady/all_to_all | solution.py:384
  74.6 3.9 %wo.2 = (bf16[2,512,128]{2,1,0:T(8,128)(2,1)S(1)}, bf16[2,512,128]{2,1,0:T(8,128)(2,1)}, bf16[2,512,128]{2,1,0:T(8,128)(2,1)}, bf16[2,512,128]{2,1,0:T(8,128)(2,1)}) custom-call(bf16[16,8,32,128]{3,2,1,0:T(8,128)(2,1)S(1)} %all-to-all-done.1.refs_0_, bf16[8,32,32,128]{3,2,1,0:T(8,128)(2,1)} %get-tuple-element.56.refs_1_), custom_call_target="tpu_custom_call" | custom-call | bytes 15000000 | tf_op jit(solution)/shard_map/wo/pallas_call | solution.py:356
  78.6 0.0 copy-start.2
  78.6 1.9 %collective-permute-start.7 = (bf16[2,512,128]{2,1,0:T(8,128)(2,1)}, bf16[2,512,128]{2,1,0:T(8,128)(2,1)S(1)}, u32[]{:S(2)}, u32[]{:S(2)}) collective-permute-start(bf16[2,512,128]{2,1,0:T(8,128)(2,1)} %get-tuple-element.58), channel_id=1, source_target_pairs={{0,16},{16,0},{32,48},{48,32},{1,17},{17,1},{33,49},{49,33},{2,18}... | collective-permute-start | bytes 786440 | tf_op jit(solution)/shard_map/wo/ppermute | solution.py:380
  80.5 2.8 %collective-permute-start.8 = (bf16[2,512,128]{2,1,0:T(8,128)(2,1)}, bf16[2,512,128]{2,1,0:T(8,128)(2,1)S(1)}, u32[]{:S(2)}, u32[]{:S(2)}) collective-permute-start(bf16[2,512,128]{2,1,0:T(8,128)(2,1)} %get-tuple-element.59), channel_id=1, source_target_pairs={{0,32},{16,48},{32,0},{48,16},{1,33},{17,49},{33,1},{49,17},{2,34}... | collective-permute-start | bytes 786440 | tf_op jit(solution)/shard_map/wo/ppermute | solution.py:380
  83.3 0.1 collective-permute-start.9
  83.4 7.5 %all-to-all-done.2.refs_0_ = bf16[16,8,32,128]{3,2,1,0:T(8,128)(2,1)} async-done(((bf16[16,8,32,128]{3,2,1,0:T(8,128)(2,1)}), bf16[16,8,32,128]{3,2,1,0:T(8,128)(2,1)}, u32[]{:S(2)}, u32[]{:S(2)}) %all-to-all-start.2) | async-done | bytes 1048608 | tf_op jit(solution)/shard_map/grady/all_to_all | solution.py:384
  90.9 5.9 %back.1 = bf16[32,3,32,128]{3,2,1,0:T(8,128)(2,1)} custom-call(bf16[16,8,32,128]{3,2,1,0:T(8,128)(2,1)} %all-to-all-done.2.refs_0_, bf16[32,5,32,128]{3,2,1,0:T(8,128)(2,1)} %copy-done, bf16[32,32,128]{2,1,0:T(8,128)(2,1)} %get-tuple-element.62.refs_2_, f32[32,128]{1,0:T(8,128)} %copy-done.7, f32[4,256,256]{2,1,0:T(8,128)} %get-tuple-element.63.refs_4_, ...), custom_call_target="tpu_custom_call" | custom-call | bytes 21000000 | tf_op jit(solution)/shard_map/back/pallas_call | solution.py:356
  96.8 0.0 collective-permute-done.7.refs_1_.refs_6_
  96.8 0.0 copy-start.3
  96.8 1.9 %collective-permute-done.8.refs_2_.refs_7_ = bf16[2,512,128]{2,1,0:T(8,128)(2,1)S(1)} collective-permute-done((bf16[2,512,128]{2,1,0:T(8,128)(2,1)}, bf16[2,512,128]{2,1,0:T(8,128)(2,1)S(1)}, u32[]{:S(2)}, u32[]{:S(2)}) %collective-permute-start.8) | collective-permute-done | bytes 262176 | tf_op jit(solution)/shard_map/wo/ppermute | solution.py:380
  98.7 0.0 copy-start.4
  98.7 0.0 collective-permute-done.9.refs_3_.refs_8_
  98.7 0.0 copy-done.2
  98.7 0.0 copy-start.5
  98.7 0.3 wo.3
  99.0 5.4 %all-to-all-start.3 = ((bf16[32,3,32,128]{3,2,1,0:T(8,128)(2,1)}), bf16[32,3,32,128]{3,2,1,0:T(8,128)(2,1)S(1)}, u32[]{:S(2)}, u32[]{:S(2)}) async-start(bf16[32,3,32,128]{3,2,1,0:T(8,128)(2,1)} %back.1), calls=%async_computation.3 | async-start | bytes 1572864 | tf_op jit(solution)/shard_map/back/all_to_all | solution.py:384
  104.4 1.9 %collective-permute-start.10 = (bf16[512,128]{1,0:T(8,128)(2,1)S(1)}, bf16[512,128]{1,0:T(8,128)(2,1)S(1)}, u32[]{:S(2)}, u32[]{:S(2)}) collective-permute-start(bf16[512,128]{1,0:T(8,128)(2,1)S(1)} %wo.3), channel_id=1, source_target_pairs={{0,64},{64,0},{1,65},{65,1},{2,66},{66,2},{3,67},{67,3},{4,68},{68... | collective-permute-start | bytes 393224 | tf_op jit(solution)/shard_map/wo/ppermute | solution.py:380
  106.3 7.8 %collective-permute-done.10.refs_9_ = bf16[512,128]{1,0:T(8,128)(2,1)S(1)} collective-permute-done((bf16[512,128]{1,0:T(8,128)(2,1)S(1)}, bf16[512,128]{1,0:T(8,128)(2,1)S(1)}, u32[]{:S(2)}, u32[]{:S(2)}) %collective-permute-start.10) | collective-permute-done | bytes 131104 | tf_op jit(solution)/shard_map/wo/ppermute | solution.py:380
  114.1 0.0 copy-start.12
  114.1 2.1 %all-to-all-done.3.refs_0_.refs_1_.refs_2_ = bf16[32,3,32,128]{3,2,1,0:T(8,128)(2,1)S(1)} async-done(((bf16[32,3,32,128]{3,2,1,0:T(8,128)(2,1)}), bf16[32,3,32,128]{3,2,1,0:T(8,128)(2,1)S(1)}, u32[]{:S(2)}, u32[]{:S(2)}) %all-to-all-start.3) | async-done | bytes 786464 | tf_op jit(solution)/shard_map/back/all_to_all | solution.py:384
  116.2 0.0 copy-done.3
  116.2 0.0 copy-done.4
  116.2 0.0 copy-done.5
  116.2 0.0 copy-done.12
  116.2 2.8 %final.1 = (bf16[128,1024]{1,0:T(8,128)(2,1)}, bf16[128,1024]{1,0:T(8,128)(2,1)}, bf16[128,1024]{1,0:T(8,128)(2,1)}, bf16[128,1024]{1,0:T(8,128)(2,1)}, f32[2,512,128]{2,1,0:T(8,128)}) custom-call(bf16[32,3,32,128]{3,2,1,0:T(8,128)(2,1)S(1)} %all-to-all-done.3.refs_0_.refs_1_.refs_2_, bf16[32,3,32,128]{3,2,1,0:T(8,128)(2,1)S(1)} %all-to-all-done.3.refs_0_.refs_1_.refs_2_, ...), custom_call_target="tpu_custom_call" | custom-call | bytes 6000000 | tf_op jit(solution)/shard_map/final/pallas_call | solution.py:356
  (1 shorter events, 0.0 us)
Async XLA Ops:
  3.2 36.4 %copy-start.7 = (f32[32,128]{1,0:T(8,128)}, f32[32,128]{1,0:T(8,128)S(1)}, u32[]{:S(2)}) copy-start(f32[32,128]{1,0:T(8,128)S(1)} %get-tuple-element.44.refs_1_.refs_3_) | copy-start | bytes 49156
  3.2 36.4 %copy-start.1 = (bf16[3072,256]{1,0:T(8,128)(2,1)S(1)}, bf16[3072,256]{1,0:T(8,128)(2,1)}, u32[]{:S(2)}) copy-start(bf16[3072,256]{1,0:T(8,128)(2,1)} %constant.4.clone.refs_2_.refs_6_) | copy-start | bytes 4718596
  3.2 36.4 %copy-start.6 = (f32[2,32,128]{2,1,0:T(8,128)S(1)}, f32[2,32,128]{2,1,0:T(8,128)}, u32[]{:S(2)}) copy-start(f32[2,32,128]{2,1,0:T(8,128)} %constant.5.clone.refs_3_.refs_7_) | copy-start | bytes 98308
  3.2 29.3 %all-to-all-start = ((bf16[32,5,32,128]{3,2,1,0:T(8,128)(2,1)}), bf16[32,5,32,128]{3,2,1,0:T(8,128)(2,1)S(1)}, u32[]{:S(2)}, u32[]{:S(2)}) async-start(bf16[32,5,32,128]{3,2,1,0:T(8,128)(2,1)} %get-tuple-element.41), calls=%async_computation | async-start | bytes 2621440 | tf_op jit(solution)/shard_map/to_channels/all_to_all | solution.py:384
  12.7 18.9 %collective-permute-start = (bf16[512,128]{1,0:T(8,128)(2,1)S(1)}, bf16[512,128]{1,0:T(8,128)(2,1)S(1)}, u32[]{:S(2)}, u32[]{:S(2)}) collective-permute-start(bf16[512,128]{1,0:T(8,128)(2,1)S(1)} %get-tuple-element.42), channel_id=1, source_target_pairs={{0,64},{64,0},{1,65},{65,1},{2,66},{66,2},{3,67},{67,3},{4,68},{68... | collective-permute-start | bytes 393224 | tf_op jit(solution)/shard_map/gather_w/ppermute | solution.py:380
  32.5 11.7 %copy-start = (bf16[32,5,32,128]{3,2,1,0:T(8,128)(2,1)}, bf16[32,5,32,128]{3,2,1,0:T(8,128)(2,1)S(1)}, u32[]{:S(2)}) copy-start(bf16[32,5,32,128]{3,2,1,0:T(8,128)(2,1)S(1)} %all-to-all-done.refs_0_.refs_1_) | copy-start | bytes 3932164
  32.5 11.7 %copy-start.8 = (bf16[2,512,128]{2,1,0:T(8,128)(2,1)}, bf16[2,512,128]{2,1,0:T(8,128)(2,1)S(1)}, u32[]{:S(2)}) copy-start(bf16[2,512,128]{2,1,0:T(8,128)(2,1)S(1)} %pad_maximum_fusion.refs_4_) | copy-start | bytes 786436
  32.5 12.4 %collective-permute-start.6 = (bf16[2,512,128]{2,1,0:T(8,128)(2,1)S(1)}, bf16[2,512,128]{2,1,0:T(8,128)(2,1)S(1)}, u32[]{:S(2)}, u32[]{:S(2)}) collective-permute-start(bf16[2,512,128]{2,1,0:T(8,128)(2,1)S(1)} %pad_maximum_fusion.refs_4_), channel_id=1, source_target_pairs={{0,48},{16,32},{32,16},{48,0},{1,49},{17,33},{33,17},{49,1},{2,50}... | collective-permute-start | bytes 786440 | tf_op jit(solution)/shard_map/gather_w/ppermute | solution.py:380
  35.2 10.2 %collective-permute-start.5 = (bf16[2,512,128]{2,1,0:T(8,128)(2,1)S(1)}, bf16[2,512,128]{2,1,0:T(8,128)(2,1)S(1)}, u32[]{:S(2)}, u32[]{:S(2)}) collective-permute-start(bf16[2,512,128]{2,1,0:T(8,128)(2,1)S(1)} %pad_maximum_fusion.refs_4_), channel_id=1, source_target_pairs={{0,32},{16,48},{32,0},{48,16},{1,33},{17,49},{33,1},{49,17},{2,34}... | collective-permute-start | bytes 786440 | tf_op jit(solution)/shard_map/gather_w/ppermute | solution.py:380
  35.3 10.8 %collective-permute-start.4 = (bf16[2,512,128]{2,1,0:T(8,128)(2,1)S(1)}, bf16[2,512,128]{2,1,0:T(8,128)(2,1)S(1)}, u32[]{:S(2)}, u32[]{:S(2)}) collective-permute-start(bf16[2,512,128]{2,1,0:T(8,128)(2,1)S(1)} %pad_maximum_fusion.refs_4_), channel_id=1, source_target_pairs={{0,16},{16,0},{32,48},{48,32},{1,17},{17,1},{33,49},{49,33},{2,18}... | collective-permute-start | bytes 786440 | tf_op jit(solution)/shard_map/gather_w/ppermute | solution.py:380
  37.6 16.1 %collective-permute-start.1 = (bf16[32,2,32,128]{3,2,1,0:T(8,128)(2,1)}, bf16[32,2,32,128]{3,2,1,0:T(8,128)(2,1)S(1)}, u32[]{:S(2)}, u32[]{:S(2)}) collective-permute-start(bf16[32,2,32,128]{3,2,1,0:T(8,128)(2,1)} %slice.3.refs_0_), channel_id=1, source_target_pairs={{0,66},{2,64},{64,2},{66,0},{1,67},{3,65},{65,3},{67,1},{4,70},{6,... | collective-permute-start | bytes 1572872 | tf_op jit(solution)/shard_map/gather_d/ppermute | solution.py:380
  44.9 1.2 copy-start.9
  45.5 0.7 copy-start.10
  46.1 0.7 copy-start.11
  46.8 23.5 %all-to-all-start.1 = ((bf16[16,8,32,128]{3,2,1,0:T(8,128)(2,1)}), bf16[16,8,32,128]{3,2,1,0:T(8,128)(2,1)S(1)}, u32[]{:S(2)}, u32[]{:S(2)}) async-start(bf16[16,8,32,128]{3,2,1,0:T(8,128)(2,1)} %bitcast.7), calls=%async_computation.1 | async-start | bytes 2097152 | tf_op jit(solution)/shard_map/gated/all_to_all | solution.py:384
  53.5 2.2 %collective-permute-start.2 = (bf16[32,2,32,128]{3,2,1,0:T(8,128)(2,1)}, bf16[32,2,32,128]{3,2,1,0:T(8,128)(2,1)S(1)}, u32[]{:S(2)}, u32[]{:S(2)}) collective-permute-start(bf16[32,2,32,128]{3,2,1,0:T(8,128)(2,1)} %slice.3.refs_0_), channel_id=1, source_target_pairs={{0,1},{1,0},{2,3},{3,2},{4,5},{5,4},{6,7},{7,6},{8,9},{9,8},{10,11... | collective-permute-start | bytes 1572872 | tf_op jit(solution)/shard_map/gather_d/ppermute | solution.py:380
  53.6 2.6 %collective-permute-start.3 = (bf16[32,2,32,128]{3,2,1,0:T(8,128)(2,1)S(1)}, bf16[32,2,32,128]{3,2,1,0:T(8,128)(2,1)S(1)}, u32[]{:S(2)}, u32[]{:S(2)}) collective-permute-start(bf16[32,2,32,128]{3,2,1,0:T(8,128)(2,1)S(1)} %collective-permute-done.1.refs_1_), channel_id=1, source_target_pairs={{0,1},{1,0},{2,3},{3,2},{4,5},{5,4},{6,7},{7,6},{8,9},{9,8},{10,11... | collective-permute-start | bytes 1572872 | tf_op jit(solution)/shard_map/gather_d/ppermute | solution.py:380
  70.3 20.6 %all-to-all-start.2 = ((bf16[16,8,32,128]{3,2,1,0:T(8,128)(2,1)}), bf16[16,8,32,128]{3,2,1,0:T(8,128)(2,1)}, u32[]{:S(2)}, u32[]{:S(2)}) async-start(bf16[16,8,32,128]{3,2,1,0:T(8,128)(2,1)} %get-tuple-element.54), calls=%async_computation.2 | async-start | bytes 2097152 | tf_op jit(solution)/shard_map/grady/all_to_all | solution.py:384
  78.6 20.1 %copy-start.2 = (bf16[2,512,128]{2,1,0:T(8,128)(2,1)}, bf16[2,512,128]{2,1,0:T(8,128)(2,1)S(1)}, u32[]{:S(2)}) copy-start(bf16[2,512,128]{2,1,0:T(8,128)(2,1)S(1)} %get-tuple-element.66.refs_0_.refs_5_) | copy-start | bytes 786436
  78.6 18.2 %collective-permute-start.7 = (bf16[2,512,128]{2,1,0:T(8,128)(2,1)}, bf16[2,512,128]{2,1,0:T(8,128)(2,1)S(1)}, u32[]{:S(2)}, u32[]{:S(2)}) collective-permute-start(bf16[2,512,128]{2,1,0:T(8,128)(2,1)} %get-tuple-element.58), channel_id=1, source_target_pairs={{0,16},{16,0},{32,48},{48,32},{1,17},{17,1},{33,49},{49,33},{2,18}... | collective-permute-start | bytes 786440 | tf_op jit(solution)/shard_map/wo/ppermute | solution.py:380
  80.5 18.2 %collective-permute-start.8 = (bf16[2,512,128]{2,1,0:T(8,128)(2,1)}, bf16[2,512,128]{2,1,0:T(8,128)(2,1)S(1)}, u32[]{:S(2)}, u32[]{:S(2)}) collective-permute-start(bf16[2,512,128]{2,1,0:T(8,128)(2,1)} %get-tuple-element.59), channel_id=1, source_target_pairs={{0,32},{16,48},{32,0},{48,16},{1,33},{17,49},{33,1},{49,17},{2,34}... | collective-permute-start | bytes 786440 | tf_op jit(solution)/shard_map/wo/ppermute | solution.py:380
  83.3 15.4 %collective-permute-start.9 = (bf16[2,512,128]{2,1,0:T(8,128)(2,1)}, bf16[2,512,128]{2,1,0:T(8,128)(2,1)S(1)}, u32[]{:S(2)}, u32[]{:S(2)}) collective-permute-start(bf16[2,512,128]{2,1,0:T(8,128)(2,1)} %get-tuple-element.60), channel_id=1, source_target_pairs={{0,48},{16,32},{32,16},{48,0},{1,49},{17,33},{33,17},{49,1},{2,50}... | collective-permute-start | bytes 786440 | tf_op jit(solution)/shard_map/wo/ppermute | solution.py:380
  96.8 19.4 %copy-start.3 = (bf16[2,512,128]{2,1,0:T(8,128)(2,1)}, bf16[2,512,128]{2,1,0:T(8,128)(2,1)S(1)}, u32[]{:S(2)}) copy-start(bf16[2,512,128]{2,1,0:T(8,128)(2,1)S(1)} %collective-permute-done.7.refs_1_.refs_6_) | copy-start | bytes 786436
  98.7 17.5 %copy-start.4 = (bf16[2,512,128]{2,1,0:T(8,128)(2,1)}, bf16[2,512,128]{2,1,0:T(8,128)(2,1)S(1)}, u32[]{:S(2)}) copy-start(bf16[2,512,128]{2,1,0:T(8,128)(2,1)S(1)} %collective-permute-done.8.refs_2_.refs_7_) | copy-start | bytes 786436
  98.7 17.5 %copy-start.5 = (bf16[2,512,128]{2,1,0:T(8,128)(2,1)}, bf16[2,512,128]{2,1,0:T(8,128)(2,1)S(1)}, u32[]{:S(2)}) copy-start(bf16[2,512,128]{2,1,0:T(8,128)(2,1)S(1)} %collective-permute-done.9.refs_3_.refs_8_) | copy-start | bytes 786436
  99.0 17.2 %all-to-all-start.3 = ((bf16[32,3,32,128]{3,2,1,0:T(8,128)(2,1)}), bf16[32,3,32,128]{3,2,1,0:T(8,128)(2,1)S(1)}, u32[]{:S(2)}, u32[]{:S(2)}) async-start(bf16[32,3,32,128]{3,2,1,0:T(8,128)(2,1)} %back.1), calls=%async_computation.3 | async-start | bytes 1572864 | tf_op jit(solution)/shard_map/back/all_to_all | solution.py:384
  104.4 9.6 %collective-permute-start.10 = (bf16[512,128]{1,0:T(8,128)(2,1)S(1)}, bf16[512,128]{1,0:T(8,128)(2,1)S(1)}, u32[]{:S(2)}, u32[]{:S(2)}) collective-permute-start(bf16[512,128]{1,0:T(8,128)(2,1)S(1)} %wo.3), channel_id=1, source_target_pairs={{0,64},{64,0},{1,65},{65,1},{2,66},{66,2},{3,67},{67,3},{4,68},{68... | collective-permute-start | bytes 393224 | tf_op jit(solution)/shard_map/wo/ppermute | solution.py:380
  114.1 2.1 %copy-start.12 = (bf16[512,128]{1,0:T(8,128)(2,1)}, bf16[512,128]{1,0:T(8,128)(2,1)S(1)}, u32[]{:S(2)}) copy-start(bf16[512,128]{1,0:T(8,128)(2,1)S(1)} %collective-permute-done.10.refs_9_) | copy-start | bytes 393220

commit v4 on v2

--- a/solution.py
+++ b/solution.py
@@ -403,9 +403,6 @@
     with jax.named_scope("gather_w"):
         take = flip(give, "xl", (2,), 1)
     held, take = lax.optimization_barrier((held, take))
-    with jax.named_scope("gather_d"):
-        d = held[:, 3:]
-        d = [d, flip(d, ("xl", "xh"), (2, 2), 3)]
     with jax.named_scope("gather_w"):
         w = jnp.stack([keep, take])
         w = [w] + [flip(w, "y", (4,), s) for s in (1, 2, 3)]
@@ -424,6 +421,10 @@
             homes="vvvv" + "hhhh",
             cost=20,
         )
+    with jax.named_scope("gather_d"):
+        after, _ = lax.optimization_barrier((held, conv))
+        d = after[:, 3:]
+        d = [d, flip(d, ("xl", "xh"), (2, 2), 3)]
     gated, w = lax.optimization_barrier((gated, w))
     with jax.named_scope("gated"):
         gated = exchange(gated.reshape(16, 8, 32, N), ("y", "z"))

time: 120 us -> 120 us (level)
  transfers between devices with their start and end apart: 15 -> 15, of which waited for: 12 -> 13; matrix products, arithmetic and copies ran while one was open for 1% -> 1% of each run, Pallas kernels for 15% -> 15%
where the time goes in v4:
time: 120 us; the launch traced here: 119 us
  waiting for transfers between devices  51.7 us (43%)
  starting transfers between devices  40.8 us (34%)
  Pallas kernels  23.8 us (20%)
  local copies, waits for them, and re-layouts  1.62 us (1%)
    ppermute x11, waiting for transfers between devices, flip(): return lax.ppermute(value, axes, [(i, i ^ by) for i in range(total)])  31.1 us
    all_to_all x4, starting transfers between devices, exchange(): return lax.all_to_all(value, axes, 0, 0)  26 us
    pallas_call x7, Pallas kernels, call(): pl.pallas_call(whole, out_shape=[spaces[home](a.shape, a.dtype) for a, ho...  23.8 us
    all_to_all x4, waiting for transfers between devices, exchange(): return lax.all_to_all(value, axes, 0, 0)  20.6 us
    ppermute x11, starting transfers between devices, flip(): return lax.ppermute(value, axes, [(i, i ^ by) for i in range(total)])  14.8 us
  transfers between devices with their start and end apart: 15, of which 13 were waited for; matrix products, arithmetic and copies ran while one was open for 1% of the time, Pallas kernels for 15%

profile of v4, /device:TPU:0, one launch (start us, length us, event | category | flops | bytes accessed | tf_op | source)
XLA Modules:
  0.0 119.0 jit_solution(288831195395366979)
XLA Ops:
  0.6 2.6 %prepare.1 = (bf16[32,5,32,128]{3,2,1,0:T(8,128)(2,1)}, bf16[512,128]{1,0:T(8,128)(2,1)S(1)}, bf16[512,128]{1,0:T(8,128)(2,1)S(1)}, f32[32,128]{1,0:T(8,128)S(1)}) custom-call(bf16[128,1024]{1,0:T(8,128)(2,1)} %refs_3_.4, bf16[128,1024]{1,0:T(8,128)(2,1)} %refs_4_.1, bf16[128,1024]{1,0:T(8,128)(2,1)} %refs_2_.2, bf16[128,1024]{1,0:T(8,128)(2,1)} %refs_3_.3, ...), custom_call_target="tpu_custom_call" | custom-call | bytes 9000000 | tf_op jit(solution)/shard_map/prepare/pallas_call | solution.py:358
  3.2 0.0 copy-start.7
  3.2 0.0 copy-start.1
  3.2 0.0 copy-start.6
  3.3 9.5 %all-to-all-start = ((bf16[32,5,32,128]{3,2,1,0:T(8,128)(2,1)}), bf16[32,5,32,128]{3,2,1,0:T(8,128)(2,1)S(1)}, u32[]{:S(2)}, u32[]{:S(2)}) async-start(bf16[32,5,32,128]{3,2,1,0:T(8,128)(2,1)} %get-tuple-element.42), calls=%async_computation | async-start | bytes 2621440 | tf_op jit(solution)/shard_map/to_channels/all_to_all | solution.py:386
  12.8 1.9 %collective-permute-start = (bf16[512,128]{1,0:T(8,128)(2,1)S(1)}, bf16[512,128]{1,0:T(8,128)(2,1)S(1)}, u32[]{:S(2)}, u32[]{:S(2)}) collective-permute-start(bf16[512,128]{1,0:T(8,128)(2,1)S(1)} %get-tuple-element.43), channel_id=1, source_target_pairs={{0,64},{64,0},{1,65},{65,1},{2,66},{66,2},{3,67},{67,3},{4,68},{68... | collective-permute-start | bytes 393224 | tf_op jit(solution)/shard_map/gather_w/ppermute | solution.py:382
  14.6 17.0 %collective-permute-done = bf16[512,128]{1,0:T(8,128)(2,1)S(1)} collective-permute-done((bf16[512,128]{1,0:T(8,128)(2,1)S(1)}, bf16[512,128]{1,0:T(8,128)(2,1)S(1)}, u32[]{:S(2)}, u32[]{:S(2)}) %collective-permute-start) | collective-permute-done | bytes 131104 | tf_op jit(solution)/shard_map/gather_w/ppermute | solution.py:382
  31.7 0.9 all-to-all-done.refs_0_.refs_1_
  32.5 0.0 copy-start
  32.6 0.0 copy-start.8
  32.6 2.7 %collective-permute-start.6 = (bf16[2,512,128]{2,1,0:T(8,128)(2,1)S(1)}, bf16[2,512,128]{2,1,0:T(8,128)(2,1)S(1)}, u32[]{:S(2)}, u32[]{:S(2)}) collective-permute-start(bf16[2,512,128]{2,1,0:T(8,128)(2,1)S(1)} %pad_maximum_fusion.refs_4_), channel_id=1, source_target_pairs={{0,48},{16,32},{32,16},{48,0},{1,49},{17,33},{33,17},{49,1},{2,50}... | collective-permute-start | bytes 786440 | tf_op jit(solution)/shard_map/gather_w/ppermute | solution.py:382
  35.3 0.1 collective-permute-start.5
  35.3 1.4 %collective-permute-start.4 = (bf16[2,512,128]{2,1,0:T(8,128)(2,1)S(1)}, bf16[2,512,128]{2,1,0:T(8,128)(2,1)S(1)}, u32[]{:S(2)}, u32[]{:S(2)}) collective-permute-start(bf16[2,512,128]{2,1,0:T(8,128)(2,1)S(1)} %pad_maximum_fusion.refs_4_), channel_id=1, source_target_pairs={{0,16},{16,0},{32,48},{48,32},{1,17},{17,1},{33,49},{49,33},{2,18}... | collective-permute-start | bytes 786440 | tf_op jit(solution)/shard_map/gather_w/ppermute | solution.py:382
  36.8 0.0 copy-done.7
  36.8 0.0 copy-done.1
  36.8 0.0 copy-done.6
  36.8 4.6 %conv.1 = (bf16[32,32,128]{2,1,0:T(8,128)(2,1)}, bf16[4,4,8,32,128]{4,3,2,1,0:T(8,128)(2,1)}, f32[4,256,256]{2,1,0:T(8,128)}, f32[4,256,256]{2,1,0:T(8,128)}) custom-call(bf16[32,5,32,128]{3,2,1,0:T(8,128)(2,1)S(1)} %all-to-all-done.refs_0_.refs_1_, f32[32,128]{1,0:T(8,128)S(1)} %get-tuple-element.45.refs_1_.refs_3_, bf16[3072,256]{1,0:T(8,128)(2,1)S(1)} %copy-done.1, ...), custom_call_target="tpu_custom_call" | custom-call | bytes 60000000 | tf_op jit(solution)/shard_map/conv/pallas_call | solution.py:358
  41.4 0.0 copy-done
  41.4 0.9 slice.3.refs_0_
  42.3 0.0 copy-done.8
  42.3 2.0 %collective-permute-start.1 = (bf16[32,2,32,128]{3,2,1,0:T(8,128)(2,1)}, bf16[32,2,32,128]{3,2,1,0:T(8,128)(2,1)S(1)}, u32[]{:S(2)}, u32[]{:S(2)}) collective-permute-start(bf16[32,2,32,128]{3,2,1,0:T(8,128)(2,1)} %slice.3.refs_0_), channel_id=1, source_target_pairs={{0,66},{2,64},{64,2},{66,0},{1,67},{3,65},{65,3},{67,1},{4,70},{6,... | collective-permute-start | bytes 1572872 | tf_op jit(solution)/shard_map/gather_d/ppermute | solution.py:382
  44.3 0.7 collective-permute-done.6.refs_7_
  44.9 0.0 copy-start.9
  44.9 0.6 collective-permute-done.5.refs_6_
  45.5 0.0 copy-start.10
  45.5 0.6 collective-permute-done.4.refs_5_
  46.1 0.0 copy-done.9
  46.1 0.0 copy-start.11
  46.1 0.1 copy-done.10
  46.2 0.6 copy-done.11
  46.8 6.8 %all-to-all-start.1 = ((bf16[16,8,32,128]{3,2,1,0:T(8,128)(2,1)}), bf16[16,8,32,128]{3,2,1,0:T(8,128)(2,1)S(1)}, u32[]{:S(2)}, u32[]{:S(2)}) async-start(bf16[16,8,32,128]{3,2,1,0:T(8,128)(2,1)} %bitcast.7), calls=%async_computation.1 | async-start | bytes 2097152 | tf_op jit(solution)/shard_map/gated/all_to_all | solution.py:386
  53.6 0.1 collective-permute-start.2
  53.7 0.8 collective-permute-done.1.refs_1_
  54.5 0.0 collective-permute-start.3
  54.5 1.3 %collective-permute-done.2.refs_2_ = bf16[32,2,32,128]{3,2,1,0:T(8,128)(2,1)S(1)} collective-permute-done((bf16[32,2,32,128]{3,2,1,0:T(8,128)(2,1)}, bf16[32,2,32,128]{3,2,1,0:T(8,128)(2,1)S(1)}, u32[]{:S(2)}, u32[]{:S(2)}) %collective-permute-start.2) | collective-permute-done | bytes 524320 | tf_op jit(solution)/shard_map/gather_d/ppermute | solution.py:382
  55.8 0.6 collective-permute-done.3.refs_3_
  56.4 3.7 %grady.1 = (bf16[16,8,32,128]{3,2,1,0:T(8,128)(2,1)}, bf16[8,32,32,128]{3,2,1,0:T(8,128)(2,1)}) custom-call(bf16[32,2,32,128]{3,2,1,0:T(8,128)(2,1)} %slice.3.refs_0_, bf16[32,2,32,128]{3,2,1,0:T(8,128)(2,1)S(1)} %collective-permute-done.1.refs_1_, bf16[32,2,32,128]{3,2,1,0:T(8,128)(2,1)S(1)} %collective-permute-done.2.refs_2_, ...), custom_call_target="tpu_custom_call" | custom-call | bytes 15000000 | tf_op jit(solution)/shard_map/grady/pallas_call | solution.py:358
  60.2 10.2 %all-to-all-done.1.refs_0_ = bf16[16,8,32,128]{3,2,1,0:T(8,128)(2,1)S(1)} async-done(((bf16[16,8,32,128]{3,2,1,0:T(8,128)(2,1)}), bf16[16,8,32,128]{3,2,1,0:T(8,128)(2,1)S(1)}, u32[]{:S(2)}, u32[]{:S(2)}) %all-to-all-start.1) | async-done | bytes 1048608 | tf_op jit(solution)/shard_map/gated/all_to_all | solution.py:386
  70.3 4.4 %all-to-all-start.2 = ((bf16[16,8,32,128]{3,2,1,0:T(8,128)(2,1)}), bf16[16,8,32,128]{3,2,1,0:T(8,128)(2,1)}, u32[]{:S(2)}, u32[]{:S(2)}) async-start(bf16[16,8,32,128]{3,2,1,0:T(8,128)(2,1)} %get-tuple-element.57), calls=%async_computation.2 | async-start | bytes 2097152 | tf_op jit(solution)/shard_map/grady/all_to_all | solution.py:386
  74.7 3.9 %wo.2 = (bf16[2,512,128]{2,1,0:T(8,128)(2,1)S(1)}, bf16[2,512,128]{2,1,0:T(8,128)(2,1)}, bf16[2,512,128]{2,1,0:T(8,128)(2,1)}, bf16[2,512,128]{2,1,0:T(8,128)(2,1)}) custom-call(bf16[16,8,32,128]{3,2,1,0:T(8,128)(2,1)S(1)} %all-to-all-done.1.refs_0_, bf16[8,32,32,128]{3,2,1,0:T(8,128)(2,1)} %get-tuple-element.59.refs_1_), custom_call_target="tpu_custom_call" | custom-call | bytes 15000000 | tf_op jit(solution)/shard_map/wo/pallas_call | solution.py:358
  78.6 0.0 copy-start.2
  78.6 1.9 %collective-permute-start.7 = (bf16[2,512,128]{2,1,0:T(8,128)(2,1)}, bf16[2,512,128]{2,1,0:T(8,128)(2,1)S(1)}, u32[]{:S(2)}, u32[]{:S(2)}) collective-permute-start(bf16[2,512,128]{2,1,0:T(8,128)(2,1)} %get-tuple-element.61), channel_id=1, source_target_pairs={{0,16},{16,0},{32,48},{48,32},{1,17},{17,1},{33,49},{49,33},{2,18}... | collective-permute-start | bytes 786440 | tf_op jit(solution)/shard_map/wo/ppermute | solution.py:382
  80.6 2.8 %collective-permute-start.8 = (bf16[2,512,128]{2,1,0:T(8,128)(2,1)}, bf16[2,512,128]{2,1,0:T(8,128)(2,1)S(1)}, u32[]{:S(2)}, u32[]{:S(2)}) collective-permute-start(bf16[2,512,128]{2,1,0:T(8,128)(2,1)} %get-tuple-element.62), channel_id=1, source_target_pairs={{0,32},{16,48},{32,0},{48,16},{1,33},{17,49},{33,1},{49,17},{2,34}... | collective-permute-start | bytes 786440 | tf_op jit(solution)/shard_map/wo/ppermute | solution.py:382
  83.3 0.1 collective-permute-start.9
  83.4 7.5 %all-to-all-done.2.refs_0_ = bf16[16,8,32,128]{3,2,1,0:T(8,128)(2,1)} async-done(((bf16[16,8,32,128]{3,2,1,0:T(8,128)(2,1)}), bf16[16,8,32,128]{3,2,1,0:T(8,128)(2,1)}, u32[]{:S(2)}, u32[]{:S(2)}) %all-to-all-start.2) | async-done | bytes 1048608 | tf_op jit(solution)/shard_map/grady/all_to_all | solution.py:386
  90.9 6.1 %back.1 = bf16[32,3,32,128]{3,2,1,0:T(8,128)(2,1)} custom-call(bf16[16,8,32,128]{3,2,1,0:T(8,128)(2,1)} %all-to-all-done.2.refs_0_, bf16[32,5,32,128]{3,2,1,0:T(8,128)(2,1)} %copy-done, bf16[32,32,128]{2,1,0:T(8,128)(2,1)} %get-tuple-element.46.refs_2_, f32[32,128]{1,0:T(8,128)} %copy-done.7, f32[4,256,256]{2,1,0:T(8,128)} %get-tuple-element.65.refs_4_, ...), custom_call_target="tpu_custom_call" | custom-call | bytes 21000000 | tf_op jit(solution)/shard_map/back/pallas_call | solution.py:358
  97.0 0.0 collective-permute-done.7.refs_1_.refs_6_
  97.0 0.0 copy-start.3
  97.0 1.7 %collective-permute-done.8.refs_2_.refs_7_ = bf16[2,512,128]{2,1,0:T(8,128)(2,1)S(1)} collective-permute-done((bf16[2,512,128]{2,1,0:T(8,128)(2,1)}, bf16[2,512,128]{2,1,0:T(8,128)(2,1)S(1)}, u32[]{:S(2)}, u32[]{:S(2)}) %collective-permute-start.8) | collective-permute-done | bytes 262176 | tf_op jit(solution)/shard_map/wo/ppermute | solution.py:382
  98.8 0.0 copy-start.4
  98.8 0.0 collective-permute-done.9.refs_3_.refs_8_
  98.8 0.0 copy-done.2
  98.8 0.0 copy-start.5
  98.8 0.3 wo.3
  99.0 5.4 %all-to-all-start.3 = ((bf16[32,3,32,128]{3,2,1,0:T(8,128)(2,1)}), bf16[32,3,32,128]{3,2,1,0:T(8,128)(2,1)S(1)}, u32[]{:S(2)}, u32[]{:S(2)}) async-start(bf16[32,3,32,128]{3,2,1,0:T(8,128)(2,1)} %back.1), calls=%async_computation.3 | async-start | bytes 1572864 | tf_op jit(solution)/shard_map/back/all_to_all | solution.py:386
  104.5 1.9 %collective-permute-start.10 = (bf16[512,128]{1,0:T(8,128)(2,1)S(1)}, bf16[512,128]{1,0:T(8,128)(2,1)S(1)}, u32[]{:S(2)}, u32[]{:S(2)}) collective-permute-start(bf16[512,128]{1,0:T(8,128)(2,1)S(1)} %wo.3), channel_id=1, source_target_pairs={{0,64},{64,0},{1,65},{65,1},{2,66},{66,2},{3,67},{67,3},{4,68},{68... | collective-permute-start | bytes 393224 | tf_op jit(solution)/shard_map/wo/ppermute | solution.py:382
  106.3 7.8 %collective-permute-done.10.refs_9_ = bf16[512,128]{1,0:T(8,128)(2,1)S(1)} collective-permute-done((bf16[512,128]{1,0:T(8,128)(2,1)S(1)}, bf16[512,128]{1,0:T(8,128)(2,1)S(1)}, u32[]{:S(2)}, u32[]{:S(2)}) %collective-permute-start.10) | collective-permute-done | bytes 131104 | tf_op jit(solution)/shard_map/wo/ppermute | solution.py:382
  114.1 0.0 copy-start.12
  114.1 2.1 %all-to-all-done.3.refs_0_.refs_1_.refs_2_ = bf16[32,3,32,128]{3,2,1,0:T(8,128)(2,1)S(1)} async-done(((bf16[32,3,32,128]{3,2,1,0:T(8,128)(2,1)}), bf16[32,3,32,128]{3,2,1,0:T(8,128)(2,1)S(1)}, u32[]{:S(2)}, u32[]{:S(2)}) %all-to-all-start.3) | async-done | bytes 786464 | tf_op jit(solution)/shard_map/back/all_to_all | solution.py:386
  116.2 0.0 copy-done.3
  116.2 0.0 copy-done.4
  116.2 0.0 copy-done.5
  116.2 0.0 copy-done.12
  116.2 2.6 %final.1 = (bf16[128,1024]{1,0:T(8,128)(2,1)}, bf16[128,1024]{1,0:T(8,128)(2,1)}, bf16[128,1024]{1,0:T(8,128)(2,1)}, bf16[128,1024]{1,0:T(8,128)(2,1)}, f32[2,512,128]{2,1,0:T(8,128)}) custom-call(bf16[32,3,32,128]{3,2,1,0:T(8,128)(2,1)S(1)} %all-to-all-done.3.refs_0_.refs_1_.refs_2_, bf16[32,3,32,128]{3,2,1,0:T(8,128)(2,1)S(1)} %all-to-all-done.3.refs_0_.refs_1_.refs_2_, ...), custom_call_target="tpu_custom_call" | custom-call | bytes 6000000 | tf_op jit(solution)/shard_map/final/pallas_call | solution.py:358
  (1 shorter events, 0.0 us)
Async XLA Ops:
  3.2 33.5 %copy-start.7 = (f32[32,128]{1,0:T(8,128)}, f32[32,128]{1,0:T(8,128)S(1)}, u32[]{:S(2)}) copy-start(f32[32,128]{1,0:T(8,128)S(1)} %get-tuple-element.45.refs_1_.refs_3_) | copy-start | bytes 49156
  3.2 33.5 %copy-start.1 = (bf16[3072,256]{1,0:T(8,128)(2,1)S(1)}, bf16[3072,256]{1,0:T(8,128)(2,1)}, u32[]{:S(2)}) copy-start(bf16[3072,256]{1,0:T(8,128)(2,1)} %constant.4.clone.refs_2_.refs_6_) | copy-start | bytes 4718596
  3.2 33.5 %copy-start.6 = (f32[2,32,128]{2,1,0:T(8,128)S(1)}, f32[2,32,128]{2,1,0:T(8,128)}, u32[]{:S(2)}) copy-start(f32[2,32,128]{2,1,0:T(8,128)} %constant.5.clone.refs_3_.refs_7_) | copy-start | bytes 98308
  3.3 29.3 %all-to-all-start = ((bf16[32,5,32,128]{3,2,1,0:T(8,128)(2,1)}), bf16[32,5,32,128]{3,2,1,0:T(8,128)(2,1)S(1)}, u32[]{:S(2)}, u32[]{:S(2)}) async-start(bf16[32,5,32,128]{3,2,1,0:T(8,128)(2,1)} %get-tuple-element.42), calls=%async_computation | async-start | bytes 2621440 | tf_op jit(solution)/shard_map/to_channels/all_to_all | solution.py:386
  12.8 18.9 %collective-permute-start = (bf16[512,128]{1,0:T(8,128)(2,1)S(1)}, bf16[512,128]{1,0:T(8,128)(2,1)S(1)}, u32[]{:S(2)}, u32[]{:S(2)}) collective-permute-start(bf16[512,128]{1,0:T(8,128)(2,1)S(1)} %get-tuple-element.43), channel_id=1, source_target_pairs={{0,64},{64,0},{1,65},{65,1},{2,66},{66,2},{3,67},{67,3},{4,68},{68... | collective-permute-start | bytes 393224 | tf_op jit(solution)/shard_map/gather_w/ppermute | solution.py:382
  32.5 8.9 %copy-start = (bf16[32,5,32,128]{3,2,1,0:T(8,128)(2,1)}, bf16[32,5,32,128]{3,2,1,0:T(8,128)(2,1)S(1)}, u32[]{:S(2)}) copy-start(bf16[32,5,32,128]{3,2,1,0:T(8,128)(2,1)S(1)} %all-to-all-done.refs_0_.refs_1_) | copy-start | bytes 3932164
  32.6 9.7 %copy-start.8 = (bf16[2,512,128]{2,1,0:T(8,128)(2,1)}, bf16[2,512,128]{2,1,0:T(8,128)(2,1)S(1)}, u32[]{:S(2)}) copy-start(bf16[2,512,128]{2,1,0:T(8,128)(2,1)S(1)} %pad_maximum_fusion.refs_4_) | copy-start | bytes 786436
  32.6 12.4 %collective-permute-start.6 = (bf16[2,512,128]{2,1,0:T(8,128)(2,1)S(1)}, bf16[2,512,128]{2,1,0:T(8,128)(2,1)S(1)}, u32[]{:S(2)}, u32[]{:S(2)}) collective-permute-start(bf16[2,512,128]{2,1,0:T(8,128)(2,1)S(1)} %pad_maximum_fusion.refs_4_), channel_id=1, source_target_pairs={{0,48},{16,32},{32,16},{48,0},{1,49},{17,33},{33,17},{49,1},{2,50}... | collective-permute-start | bytes 786440 | tf_op jit(solution)/shard_map/gather_w/ppermute | solution.py:382
  35.3 10.2 %collective-permute-start.5 = (bf16[2,512,128]{2,1,0:T(8,128)(2,1)S(1)}, bf16[2,512,128]{2,1,0:T(8,128)(2,1)S(1)}, u32[]{:S(2)}, u32[]{:S(2)}) collective-permute-start(bf16[2,512,128]{2,1,0:T(8,128)(2,1)S(1)} %pad_maximum_fusion.refs_4_), channel_id=1, source_target_pairs={{0,32},{16,48},{32,0},{48,16},{1,33},{17,49},{33,1},{49,17},{2,34}... | collective-permute-start | bytes 786440 | tf_op jit(solution)/shard_map/gather_w/ppermute | solution.py:382
  35.3 10.8 %collective-permute-start.4 = (bf16[2,512,128]{2,1,0:T(8,128)(2,1)S(1)}, bf16[2,512,128]{2,1,0:T(8,128)(2,1)S(1)}, u32[]{:S(2)}, u32[]{:S(2)}) collective-permute-start(bf16[2,512,128]{2,1,0:T(8,128)(2,1)S(1)} %pad_maximum_fusion.refs_4_), channel_id=1, source_target_pairs={{0,16},{16,0},{32,48},{48,32},{1,17},{17,1},{33,49},{49,33},{2,18}... | collective-permute-start | bytes 786440 | tf_op jit(solution)/shard_map/gather_w/ppermute | solution.py:382
  42.3 12.2 %collective-permute-start.1 = (bf16[32,2,32,128]{3,2,1,0:T(8,128)(2,1)}, bf16[32,2,32,128]{3,2,1,0:T(8,128)(2,1)S(1)}, u32[]{:S(2)}, u32[]{:S(2)}) collective-permute-start(bf16[32,2,32,128]{3,2,1,0:T(8,128)(2,1)} %slice.3.refs_0_), channel_id=1, source_target_pairs={{0,66},{2,64},{64,2},{66,0},{1,67},{3,65},{65,3},{67,1},{4,70},{6,... | collective-permute-start | bytes 1572872 | tf_op jit(solution)/shard_map/gather_d/ppermute | solution.py:382
  44.9 1.2 copy-start.9
  45.5 0.7 copy-start.10
  46.1 0.7 copy-start.11
  46.8 23.5 %all-to-all-start.1 = ((bf16[16,8,32,128]{3,2,1,0:T(8,128)(2,1)}), bf16[16,8,32,128]{3,2,1,0:T(8,128)(2,1)S(1)}, u32[]{:S(2)}, u32[]{:S(2)}) async-start(bf16[16,8,32,128]{3,2,1,0:T(8,128)(2,1)} %bitcast.7), calls=%async_computation.1 | async-start | bytes 2097152 | tf_op jit(solution)/shard_map/gated/all_to_all | solution.py:386
  53.6 2.2 %collective-permute-start.2 = (bf16[32,2,32,128]{3,2,1,0:T(8,128)(2,1)}, bf16[32,2,32,128]{3,2,1,0:T(8,128)(2,1)S(1)}, u32[]{:S(2)}, u32[]{:S(2)}) collective-permute-start(bf16[32,2,32,128]{3,2,1,0:T(8,128)(2,1)} %slice.3.refs_0_), channel_id=1, source_target_pairs={{0,1},{1,0},{2,3},{3,2},{4,5},{5,4},{6,7},{7,6},{8,9},{9,8},{10,11... | collective-permute-start | bytes 1572872 | tf_op jit(solution)/shard_map/gather_d/ppermute | solution.py:382
  54.5 1.9 %collective-permute-start.3 = (bf16[32,2,32,128]{3,2,1,0:T(8,128)(2,1)S(1)}, bf16[32,2,32,128]{3,2,1,0:T(8,128)(2,1)S(1)}, u32[]{:S(2)}, u32[]{:S(2)}) collective-permute-start(bf16[32,2,32,128]{3,2,1,0:T(8,128)(2,1)S(1)} %collective-permute-done.1.refs_1_), channel_id=1, source_target_pairs={{0,1},{1,0},{2,3},{3,2},{4,5},{5,4},{6,7},{7,6},{8,9},{9,8},{10,11... | collective-permute-start | bytes 1572872 | tf_op jit(solution)/shard_map/gather_d/ppermute | solution.py:382
  70.3 20.6 %all-to-all-start.2 = ((bf16[16,8,32,128]{3,2,1,0:T(8,128)(2,1)}), bf16[16,8,32,128]{3,2,1,0:T(8,128)(2,1)}, u32[]{:S(2)}, u32[]{:S(2)}) async-start(bf16[16,8,32,128]{3,2,1,0:T(8,128)(2,1)} %get-tuple-element.57), calls=%async_computation.2 | async-start | bytes 2097152 | tf_op jit(solution)/shard_map/grady/all_to_all | solution.py:386
  78.6 20.1 %copy-start.2 = (bf16[2,512,128]{2,1,0:T(8,128)(2,1)}, bf16[2,512,128]{2,1,0:T(8,128)(2,1)S(1)}, u32[]{:S(2)}) copy-start(bf16[2,512,128]{2,1,0:T(8,128)(2,1)S(1)} %get-tuple-element.68.refs_0_.refs_5_) | copy-start | bytes 786436
  78.6 18.4 %collective-permute-start.7 = (bf16[2,512,128]{2,1,0:T(8,128)(2,1)}, bf16[2,512,128]{2,1,0:T(8,128)(2,1)S(1)}, u32[]{:S(2)}, u32[]{:S(2)}) collective-permute-start(bf16[2,512,128]{2,1,0:T(8,128)(2,1)} %get-tuple-element.61), channel_id=1, source_target_pairs={{0,16},{16,0},{32,48},{48,32},{1,17},{17,1},{33,49},{49,33},{2,18}... | collective-permute-start | bytes 786440 | tf_op jit(solution)/shard_map/wo/ppermute | solution.py:382
  80.6 18.2 %collective-permute-start.8 = (bf16[2,512,128]{2,1,0:T(8,128)(2,1)}, bf16[2,512,128]{2,1,0:T(8,128)(2,1)S(1)}, u32[]{:S(2)}, u32[]{:S(2)}) collective-permute-start(bf16[2,512,128]{2,1,0:T(8,128)(2,1)} %get-tuple-element.62), channel_id=1, source_target_pairs={{0,32},{16,48},{32,0},{48,16},{1,33},{17,49},{33,1},{49,17},{2,34}... | collective-permute-start | bytes 786440 | tf_op jit(solution)/shard_map/wo/ppermute | solution.py:382
  83.3 15.4 %collective-permute-start.9 = (bf16[2,512,128]{2,1,0:T(8,128)(2,1)}, bf16[2,512,128]{2,1,0:T(8,128)(2,1)S(1)}, u32[]{:S(2)}, u32[]{:S(2)}) collective-permute-start(bf16[2,512,128]{2,1,0:T(8,128)(2,1)} %get-tuple-element.63), channel_id=1, source_target_pairs={{0,48},{16,32},{32,16},{48,0},{1,49},{17,33},{33,17},{49,1},{2,50}... | collective-permute-start | bytes 786440 | tf_op jit(solution)/shard_map/wo/ppermute | solution.py:382
  97.0 19.2 %copy-start.3 = (bf16[2,512,128]{2,1,0:T(8,128)(2,1)}, bf16[2,512,128]{2,1,0:T(8,128)(2,1)S(1)}, u32[]{:S(2)}) copy-start(bf16[2,512,128]{2,1,0:T(8,128)(2,1)S(1)} %collective-permute-done.7.refs_1_.refs_6_) | copy-start | bytes 786436
  98.8 17.5 %copy-start.4 = (bf16[2,512,128]{2,1,0:T(8,128)(2,1)}, bf16[2,512,128]{2,1,0:T(8,128)(2,1)S(1)}, u32[]{:S(2)}) copy-start(bf16[2,512,128]{2,1,0:T(8,128)(2,1)S(1)} %collective-permute-done.8.refs_2_.refs_7_) | copy-start | bytes 786436
  98.8 17.5 %copy-start.5 = (bf16[2,512,128]{2,1,0:T(8,128)(2,1)}, bf16[2,512,128]{2,1,0:T(8,128)(2,1)S(1)}, u32[]{:S(2)}) copy-start(bf16[2,512,128]{2,1,0:T(8,128)(2,1)S(1)} %collective-permute-done.9.refs_3_.refs_8_) | copy-start | bytes 786436
  99.0 17.2 %all-to-all-start.3 = ((bf16[32,3,32,128]{3,2,1,0:T(8,128)(2,1)}), bf16[32,3,32,128]{3,2,1,0:T(8,128)(2,1)S(1)}, u32[]{:S(2)}, u32[]{:S(2)}) async-start(bf16[32,3,32,128]{3,2,1,0:T(8,128)(2,1)} %back.1), calls=%async_computation.3 | async-start | bytes 1572864 | tf_op jit(solution)/shard_map/back/all_to_all | solution.py:386
  104.5 9.6 %collective-permute-start.10 = (bf16[512,128]{1,0:T(8,128)(2,1)S(1)}, bf16[512,128]{1,0:T(8,128)(2,1)S(1)}, u32[]{:S(2)}, u32[]{:S(2)}) collective-permute-start(bf16[512,128]{1,0:T(8,128)(2,1)S(1)} %wo.3), channel_id=1, source_target_pairs={{0,64},{64,0},{1,65},{65,1},{2,66},{66,2},{3,67},{67,3},{4,68},{68... | collective-permute-start | bytes 393224 | tf_op jit(solution)/shard_map/wo/ppermute | solution.py:382
  114.1 2.1 %copy-start.12 = (bf16[512,128]{1,0:T(8,128)(2,1)}, bf16[512,128]{1,0:T(8,128)(2,1)S(1)}, u32[]{:S(2)}) copy-start(bf16[512,128]{1,0:T(8,128)(2,1)S(1)} %collective-permute-done.10.refs_9_) | copy-start | bytes 393220
